TPU v7x, 32 devices: a whole 2x2x4 slice. The times are simulated.
32 devices in a mesh: dp: 4 (over y, x), ctx: 4 (over z), tp: 2 (over core).
Axes of the slice: x: 2, y: 2, z: 4, core: 2. Of those that a mesh axis runs over, the one named last changes fastest.
Arguments:
- block_input: bfloat16 [4, 1536, 2048], P('dp', 'ctx'), may hold values from -6 to 6
- cotangent: bfloat16 [4, 1536, 2048], P('dp', 'ctx'), may hold values from -6 to 6
- segment_ids: int32 [4, 1536], P('dp', 'ctx'), may hold values from 0 to 1535, as said below
- positions: int32 [4, 1536], P('dp', 'ctx'), may hold values from 0 to 1535, as said below
- norm_gain: bfloat16 [2048], replicated, may hold values from 0.099609375 to 1.8984375
- norm_bias: bfloat16 [2048], replicated, may hold values from -1.75 to 1.75
- w_qkv: bfloat16 [3, 2048, 2048], P(None, ('dp', 'ctx'), 'tp'), may hold values from -0.125 to 0.125
- qkv_bias: bfloat16 [3, 2048], P(None, 'tp'), may hold values from -3 to 3
- w_dense: bfloat16 [2048, 2048], P('tp', ('dp', 'ctx')), may hold values from -0.5 to 0.5
- w_fc1: bfloat16 [2048, 8192], P(('dp', 'ctx'), 'tp'), may hold values from -0.125 to 0.125
- fc1_bias: bfloat16 [8192], P('tp'), may hold values from -3 to 3
- w_fc2: bfloat16 [8192, 2048], P('tp', ('dp', 'ctx')), may hold values from -0.0625 to 0.0625
- out_bias: bfloat16 [2048], replicated, may hold values from -3 to 3
Outputs:
- output: bfloat16 [4, 1536, 2048], P('dp', 'ctx')
- grad_input: bfloat16 [4, 1536, 2048], P('dp', 'ctx')
- grad_norm_gain: float32 [2048], replicated
- grad_norm_bias: float32 [2048], replicated
- grad_w_qkv: float32 [3, 2048, 2048], P(None, ('dp', 'ctx'), 'tp')
- grad_qkv_bias: float32 [3, 2048], P(None, 'tp')
- grad_w_dense: float32 [2048, 2048], P('tp', ('dp', 'ctx'))
- grad_w_fc1: float32 [2048, 8192], P(('dp', 'ctx'), 'tp')
- grad_fc1_bias: float32 [8192], P('tp')
- grad_w_fc2: float32 [8192, 2048], P('tp', ('dp', 'ctx'))
- grad_out_bias: float32 [2048], replicated
Inputs may be any that keep to these rules, and one draw needn't show every extreme that they name: `segment_ids`: A document's id is the place of its first token in the sequence, so ids never fall along a sequence; the last token of every sequence is a document of its own. Every sequence holds one spanning document that starts within its first 384 tokens and ends within its last 385 tokens; before and after it, documents start at random places with mean spacing 400 and no least length. Within a document positions rise by one from token to token; a document's first position is at least 0, and except in the spanning document at most the place of its first token.
All inputs are finite; a program needn't handle non-finite values.
Results may differ from a plain program's by a relative error of at most 0.014.
Values may be sent and summed in bfloat16 or wider, within the bound.
A program may use at most 320 MiB of HBM per device.

v0:
```python
import math

import jax
import jax.numpy as jnp
from jax import lax
from jax.sharding import PartitionSpec as P

HD = 64
ROT = 32


epsilon = 1e-05


def rotation(places):
    half_rot = ROT // 2
    frequency = 10000.0 ** (-(jnp.arange(half_rot, dtype=jnp.float32) * 2.0 / ROT))
    angles = places.astype(jnp.float32)[:, None] * frequency[None, :]
    return (jnp.cos(angles)[:, None, :], jnp.sin(angles)[:, None, :])


def rotate(tensor, cosine_table, sine_table):
    half_rot = ROT // 2
    first_half = tensor[..., :half_rot]
    second_half = tensor[..., half_rot:ROT]
    return jnp.concatenate(
        [
            first_half * cosine_table - second_half * sine_table,
            second_half * cosine_table + first_half * sine_table,
            tensor[..., ROT:],
        ],
        -1,
    )


def span_size():
    return 512


def per_device(
    block_input,
    cotangent,
    segment_ids,
    positions,
    norm_gain,
    norm_bias,
    w_qkv,
    qkv_bias,
    w_dense,
    w_fc1,
    fc1_bias,
    w_fc2,
    out_bias,
):
    row_count = block_input.shape[1]
    heads_here = w_qkv.shape[2] // HD
    scaling = 1.0 / math.sqrt(HD)
    query_index = lax.axis_index("ctx") * row_count + jnp.arange(row_count, dtype=jnp.int32)
    query_seg = segment_ids[0]
    wide_qkv, wide_dense = (
        lax.all_gather(w_qkv, ("dp", "ctx"), axis=1, tiled=True),
        lax.all_gather(w_dense, ("dp", "ctx"), axis=1, tiled=True),
    )
    wide_fc1, wide_fc2 = (
        lax.all_gather(w_fc1, ("dp", "ctx"), axis=0, tiled=True),
        lax.all_gather(w_fc2, ("dp", "ctx"), axis=1, tiled=True),
    )
    inputs = block_input[0].astype(jnp.float32)
    mean_in = jnp.mean(inputs, -1, keepdims=True)
    centred = inputs - mean_in
    inv_std = lax.rsqrt(jnp.mean(centred * centred, -1, keepdims=True) + epsilon)
    x_hat = centred * inv_std
    gain_full = norm_gain.astype(jnp.float32)
    normed = (x_hat * gain_full + norm_bias.astype(jnp.float32)).astype(jnp.bfloat16)
    projected = (
        jnp.einsum("rd,cde->cre", normed, wide_qkv, preferred_element_type=jnp.float32)
        + qkv_bias.astype(jnp.float32)[:, None, :]
    )
    cosine_table, sine_table = rotation(positions[0])
    queries = rotate(
        projected[0].reshape(row_count, heads_here, HD), cosine_table, sine_table
    ).astype(jnp.bfloat16)
    keys = (
        rotate(projected[1].reshape(row_count, heads_here, HD), cosine_table, sine_table)
        .astype(jnp.bfloat16)
        .reshape(row_count, heads_here * HD)
    )
    values = projected[2].astype(jnp.bfloat16)

    def split_piece(pieces):
        key_piece, value_piece, seg_piece = pieces
        piece_rows = key_piece.shape[0]
        span_rows = span_size()
        blocks = piece_rows // span_rows
        key_index = jnp.arange(piece_rows, dtype=jnp.int32)
        return (
            (
                key_piece.reshape(blocks, span_rows, heads_here, HD),
                value_piece.reshape(blocks, span_rows, heads_here, HD),
                seg_piece.reshape(blocks, span_rows),
                key_index.reshape(blocks, span_rows),
            ),
            piece_rows,
            span_rows,
        )

    def block_scores(key_heads, seg_part, index_part):
        scores = (
            jnp.einsum("qhd,khd->hqk", queries, key_heads, preferred_element_type=jnp.float32)
            * scaling
        )
        allowed = (index_part[None, :] <= query_index[:, None]) & (
            seg_part[None, :] == query_seg[:, None]
        )
        return (jnp.where(allowed[None], scores, -1e30), allowed)

    start_state = (
        jnp.full((heads_here, row_count), -1e30, jnp.float32),
        jnp.zeros((heads_here, row_count), jnp.float32),
        jnp.zeros((heads_here, row_count, HD), jnp.float32),
    )
    carried = start_state
    batch_items, piece_rows, span_rows = split_piece(
        (
            lax.all_gather(keys, "ctx", axis=0, tiled=True),
            lax.all_gather(values, "ctx", axis=0, tiled=True),
            lax.all_gather(query_seg, "ctx", axis=0, tiled=True),
        )
    )

    def attend_step(carried_now, block_items):
        key_heads, value_heads, seg_part, index_part = block_items
        running_max, running_sum, weighted = carried_now
        scores, allowed = block_scores(key_heads, seg_part, index_part)
        new_max = jnp.maximum(running_max, jnp.max(scores, -1))
        expo = jnp.where(allowed[None], jnp.exp(scores - new_max[..., None]), 0.0)
        factor = jnp.exp(running_max - new_max)
        running_sum = running_sum * factor + jnp.sum(expo, -1)
        weighted = weighted * factor[..., None] + jnp.einsum(
            "hqk,khd->hqd",
            expo.astype(jnp.bfloat16),
            value_heads,
            preferred_element_type=jnp.float32,
        )
        return ((new_max, running_sum, weighted), None)

    carried, unused = lax.scan(attend_step, carried, batch_items)
    running_max, running_sum, weighted = carried
    heads_out = weighted / running_sum[..., None]
    log_total = running_max + jnp.log(running_sum)
    mixture = (
        jnp.transpose(heads_out, (1, 0, 2)).reshape(row_count, heads_here * HD).astype(jnp.bfloat16)
    )
    attn_out = jnp.dot(mixture, wide_dense, preferred_element_type=jnp.float32)
    hidden_pre = jnp.dot(normed, wide_fc1, preferred_element_type=jnp.float32) + fc1_bias.astype(
        jnp.float32
    )
    hidden = jax.nn.gelu(hidden_pre, approximate=True).astype(jnp.bfloat16)
    mlp_out = jnp.dot(hidden, wide_fc2, preferred_element_type=jnp.float32)
    branches = lax.psum((attn_out + mlp_out).astype(jnp.bfloat16), "tp").astype(jnp.float32)
    output = (inputs + branches + out_bias.astype(jnp.float32)).astype(jnp.bfloat16)
    back_qkv, back_dense = (
        lax.all_gather(w_qkv, ("dp", "ctx"), axis=1, tiled=True),
        lax.all_gather(w_dense, ("dp", "ctx"), axis=1, tiled=True),
    )
    back_fc1, back_fc2 = (
        lax.all_gather(w_fc1, ("dp", "ctx"), axis=0, tiled=True),
        lax.all_gather(w_fc2, ("dp", "ctx"), axis=1, tiled=True),
    )
    upstream = cotangent[0]
    upstream_wide = upstream.astype(jnp.float32)
    grad_dense = jnp.einsum("rk,rd->kd", mixture, upstream, preferred_element_type=jnp.float32)
    grad_fc2 = jnp.einsum("rf,rd->fd", hidden, upstream, preferred_element_type=jnp.float32)
    mix_grad = jnp.einsum(
        "rd,kd->rk", upstream, back_dense, preferred_element_type=jnp.float32
    ).astype(jnp.bfloat16)
    act_grad = jnp.einsum("rd,fd->rf", upstream, back_fc2, preferred_element_type=jnp.float32)
    unused_value, gelu_back = jax.vjp(
        lambda pre_act: jax.nn.gelu(pre_act, approximate=True), hidden_pre
    )
    hidden_grad = gelu_back(act_grad)[0].astype(jnp.bfloat16)
    grad_fc1 = jnp.einsum("rd,rf->df", normed, hidden_grad, preferred_element_type=jnp.float32)
    head_grad = mix_grad.reshape(row_count, heads_here, HD)
    row_delta = jnp.sum(jnp.transpose(head_grad.astype(jnp.float32), (1, 0, 2)) * heads_out, -1)
    query_grad = jnp.zeros((row_count, heads_here, HD), jnp.float32)
    batch_items, piece_rows, span_rows = split_piece(
        (
            lax.all_gather(keys, "ctx", axis=0, tiled=True),
            lax.all_gather(values, "ctx", axis=0, tiled=True),
            lax.all_gather(query_seg, "ctx", axis=0, tiled=True),
        )
    )

    def gradient_step(query_now, block_items):
        key_heads, value_heads, seg_part, index_part = block_items
        scores, allowed = block_scores(key_heads, seg_part, index_part)
        prob_block = jnp.where(allowed[None], jnp.exp(scores - log_total[..., None]), 0.0)
        prob_grad = jnp.einsum(
            "qhd,khd->hqk", head_grad, value_heads, preferred_element_type=jnp.float32
        )
        score_grad = (prob_block * (prob_grad - row_delta[..., None])).astype(jnp.bfloat16)
        query_now = (
            query_now
            + jnp.einsum("hqk,khd->qhd", score_grad, key_heads, preferred_element_type=jnp.float32)
            * scaling
        )
        key_part = (
            jnp.einsum("hqk,qhd->khd", score_grad, queries, preferred_element_type=jnp.float32)
            * scaling
        )
        value_part = jnp.einsum(
            "hqk,qhd->khd",
            prob_block.astype(jnp.bfloat16),
            head_grad,
            preferred_element_type=jnp.float32,
        )
        return (
            query_now,
            (
                key_part.reshape(span_rows, heads_here * HD),
                value_part.reshape(span_rows, heads_here * HD),
            ),
        )

    query_grad, (key_new, value_new) = lax.scan(gradient_step, query_grad, batch_items)
    key_grads = key_new.reshape(piece_rows, heads_here * HD)
    value_grads = value_new.reshape(piece_rows, heads_here * HD)
    query_grad, key_grads, value_grads = (query_grad, key_grads, value_grads)
    key_grad, value_grad = (
        lax.psum_scatter(
            key_grads.astype(jnp.bfloat16), "ctx", scatter_dimension=0, tiled=True
        ).astype(jnp.float32),
        lax.psum_scatter(
            value_grads.astype(jnp.bfloat16), "ctx", scatter_dimension=0, tiled=True
        ).astype(jnp.float32),
    )
    proj_grad = jnp.stack(
        [
            rotate(query_grad, cosine_table, -sine_table).reshape(row_count, heads_here * HD),
            rotate(key_grad.reshape(row_count, heads_here, HD), cosine_table, -sine_table).reshape(
                row_count, heads_here * HD
            ),
            value_grad,
        ]
    ).astype(jnp.bfloat16)
    grad_qkv = jnp.einsum("rd,cre->cde", normed, proj_grad, preferred_element_type=jnp.float32)
    qkv_bias_grad = jnp.sum(proj_grad.astype(jnp.float32), 1)
    normed_part = jnp.einsum("cre,cde->rd", proj_grad, back_qkv, preferred_element_type=jnp.float32)
    normed_part = normed_part + jnp.einsum(
        "rf,df->rd", hidden_grad, back_fc1, preferred_element_type=jnp.float32
    )
    normed_grad = lax.psum(normed_part.astype(jnp.bfloat16), "tp").astype(jnp.float32)
    scaled = normed_grad * gain_full
    grad_input = upstream_wide + inv_std * (
        scaled
        - jnp.mean(scaled, -1, keepdims=True)
        - x_hat * jnp.mean(scaled * x_hat, -1, keepdims=True)
    )
    small_sums = lax.psum(
        (
            jnp.sum(normed_grad * x_hat, 0),
            jnp.sum(normed_grad, 0),
            qkv_bias_grad,
            jnp.sum(hidden_grad.astype(jnp.float32), 0),
            jnp.sum(upstream_wide, 0),
        ),
        ("dp", "ctx"),
    )
    weight_sums = (
        lax.psum_scatter(grad_qkv, ("dp", "ctx"), scatter_dimension=1, tiled=True),
        lax.psum_scatter(grad_dense, ("dp", "ctx"), scatter_dimension=1, tiled=True),
        lax.psum_scatter(grad_fc1, ("dp", "ctx"), scatter_dimension=0, tiled=True),
        lax.psum_scatter(grad_fc2, ("dp", "ctx"), scatter_dimension=1, tiled=True),
    )
    return (
        output[None],
        grad_input.astype(jnp.bfloat16)[None],
        small_sums[0],
        small_sums[1],
        weight_sums[0],
        small_sums[2],
        weight_sums[1],
        weight_sums[2],
        small_sums[3],
        weight_sums[3],
        small_sums[4],
    )


def solution(mesh):
    placed = (
        P("dp", "ctx", None),
        P("dp", "ctx", None),
        P("dp", "ctx"),
        P("dp", "ctx"),
        P(),
        P(),
        P(None, ("dp", "ctx"), "tp"),
        P(None, "tp"),
        P("tp", ("dp", "ctx")),
        P(("dp", "ctx"), "tp"),
        P("tp"),
        P("tp", ("dp", "ctx")),
        P(),
    )
    return jax.shard_map(
        per_device,
        mesh=mesh,
        in_specs=placed,
        out_specs=(
            P("dp", "ctx", None),
            P("dp", "ctx", None),
            P(),
            P(),
            P(None, ("dp", "ctx"), "tp"),
            P(None, "tp"),
            P("tp", ("dp", "ctx")),
            P(("dp", "ctx"), "tp"),
            P("tp"),
            P("tp", ("dp", "ctx")),
            P(),
        ),
        check_vma=False,
    )
```

profile of v0, /device:TPU:0, one launch (start us, length us, event | category | flops | bytes accessed | tf_op | source)
XLA Modules:
  0.0 2928.1 jit_solution(6069119599765315126)
XLA Ops:
  14.6 150.8 %all-gather.9.cloned.1.call-done = bf16[3,2048,1024]{2,1,0:T(8,128)(2,1)} async-done(((bf16[3,128,1024]{2,1,0:T(8,128)(2,1)}), bf16[3,2048,1024]{2,1,0:T(8,128)(2,1)}) %all-gather.9.cloned.1.call-update) | async-done | bytes 12582928 | tf_op jit(solution)/shard_map/all_gather | solution.py:61
  198.6 57.0 %all-gather.13.cloned.1.call-done = bf16[1024,2048]{1,0:T(8,128)(2,1)} async-done(((bf16[1024,128]{1,0:T(8,128)(2,1)}), bf16[1024,2048]{1,0:T(8,128)(2,1)}) %all-gather.13.cloned.1.call-update) | async-done | bytes 4194320 | tf_op jit(solution)/shard_map/all_gather | solution.py:62
  262.6 56.7 %all-gather.11.cloned.1.call-done = bf16[1536,1024]{0,1:T(8,128)(2,1)} async-done(((bf16[384,1024]{0,1:T(8,128)(2,1)}), bf16[1536,1024]{0,1:T(8,128)(2,1)}) %all-gather.11.cloned.1.call-update) | async-done | bytes 3145744 | tf_op jit(solution)/shard_map/all_gather | solution.py:125
  334.7 48.7 %all-gather.19.cloned.1.call-done = bf16[1,1536,1024]{2,1,0:T(8,128)(2,1)} async-done(((bf16[1,384,1024]{2,1,0:T(8,128)(2,1)}), bf16[1,1536,1024]{2,1,0:T(8,128)(2,1)}) %all-gather.19.cloned.1.call-update) | async-done | bytes 3145744 | tf_op jit(solution)/shard_map/all_gather | solution.py:126
  400.4 69.0 %while.30 = (s32[]{:T(128)}, f32[16,384]{1,0:T(8,128)S(1)}, f32[16,384]{1,0:T(8,128)S(1)}, f32[16,384,64]{1,2,0:T(8,128)}, s32[3,512]{1,0:T(4,128)S(1)}, /*index...) while((s32[]{:T(128)}, f32[16,384]{1,0:T(8,128)S(1)}, ...), condition=%wide.region_5.6_spmd.clone, body=%wide.region_2.5_spmd.clone.sunk | while | flops 848001408 | bytes 95309504 | solution.py:147
  472.2 120.0 %while.31 = (s32[]{:T(128)}, f32[384,16,64]{0,2,1:T(8,128)S(1)}, bf16[3,512,1024]{2,1,0:T(8,128)(2,1)}, bf16[3,512,1024]{1,2,0:T(8,128)(2,1)}, bf16[3,512,16,64]...) while((s32[]{:T(128)}, f32[384,16,64]{0,2,1:T(8,128)S(1)}, ...), condition=%wide.region_9.10_spmd.clone, body=%wide.region_8.9_spmd.clone.sunk | while | flops 2053833088 | bytes 112881432 | solution.py:225
  480.3 13.8 fusion.157
  520.8 12.2 fusion.157
  560.2 12.2 fusion.157
  605.1 12.1 convolution_add_fusion
  617.2 209.5 %all-gather.17.cloned.1.call-done = bf16[4096,2048]{1,0:T(8,128)(2,1)} async-done(((bf16[4096,128]{1,0:T(8,128)(2,1)}), bf16[4096,2048]{1,0:T(8,128)(2,1)}) %all-gather.17.cloned.1.call-update) | async-done | bytes 16777232 | tf_op jit(solution)/shard_map/all_gather | solution.py:66
  826.7 15.2 convert_reduce_fusion
  841.9 13.5 fusion.99
  855.4 12.8 add_convert_fusion
  868.2 19.3 reduce-scatter.7.cloned.1.call-done
  895.5 54.5 %reduce-scatter.9.cloned.1.call-done = bf16[384,1024]{1,0:T(8,128)(2,1)} async-done(((bf16[1536,1024]{1,0:T(8,128)(2,1)}), bf16[384,1024]{1,0:T(8,128)(2,1)}) %reduce-scatter.9.cloned.1.call-update) | async-done | bytes 786448 | tf_op jit(solution)/shard_map/reduce_scatter | solution.py:233
  960.3 14.0 convolution_bitcast_fusion
  982.9 18.3 fusion.93
  1001.4 18.8 fusion.75
  1029.7 82.3 %all-reduce = (f32[2048]{0:T(1024)}, f32[2048]{0:T(1024)}, f32[3,1024]{1,0:T(4,128)}, f32[4096]{0:T(1024)}, f32[2048]{0:T(1024)}) all-reduce(f32[2048]{0:T(1024)S(1)} %get-tuple-element.309, f32[2048]{0:T(1024)S(1)} %get-tuple-element.312, ...), channel_id=1, replica_groups=mesh['dp'=4,'ctx'=4,'tp'=2] {'dp','ctx'}, use_global_device_ids=true, to_apply=%region_16.17 | all-reduce | flops 13312 | bytes 106496 | tf_op jit(solution)/shard_map/psum | solution.py:259
  1112.0 243.2 %reduce-scatter.11.cloned.1.call-done = f32[3,128,1024]{1,2,0:T(8,128)} async-done(((f32[3,2048,1024]{1,2,0:T(8,128)}), f32[3,128,1024]{1,2,0:T(8,128)}) %reduce-scatter.11.cloned.1.call-update) | async-done | bytes 1572880 | tf_op jit(solution)/shard_map/reduce_scatter | solution.py:270
  1358.2 181.3 %reduce-scatter.13.cloned.1.call-done = f32[1024,128]{1,0:T(8,128)} async-done(((f32[1024,2048]{1,0:T(8,128)}), f32[1024,128]{1,0:T(8,128)}) %reduce-scatter.13.cloned.1.call-update) | async-done | bytes 524304 | tf_op jit(solution)/shard_map/reduce_scatter | solution.py:271
  1539.5 690.1 %reduce-scatter.15.cloned.1.call-done = f32[128,4096]{1,0:T(8,128)} async-done(((f32[2048,4096]{1,0:T(8,128)}), f32[128,4096]{1,0:T(8,128)}) %reduce-scatter.15.cloned.1.call-update) | async-done | bytes 2097168 | tf_op jit(solution)/shard_map/reduce_scatter | solution.py:272
  2229.6 691.7 %reduce-scatter.17.cloned.1.call-done = f32[4096,128]{1,0:T(8,128)} async-done(((f32[4096,2048]{1,0:T(8,128)}), f32[4096,128]{1,0:T(8,128)}) %reduce-scatter.17.cloned.1.call-update) | async-done | bytes 2097168 | tf_op jit(solution)/shard_map/reduce_scatter | solution.py:273
  (237 shorter events, 284.8 us)
Async XLA Ops:
  7.2 158.3 %all-gather.9.cloned.1.call-start = ((), (), s32[]{:S(2)}) async-start(), calls=%async_computation.6 | async-start | bytes 13369344 | tf_op jit(solution)/shard_map/all_gather | solution.py:61
  7.9 247.6 %all-gather.13.cloned.1.call-start = ((), (), s32[]{:S(2)}) async-start(), calls=%async_computation.8 | async-start | bytes 4456448 | tf_op jit(solution)/shard_map/all_gather | solution.py:62
  8.7 310.6 %all-gather.11.cloned.1.call-start = ((), (), s32[]{:S(2)}) async-start(), calls=%async_computation.7 | async-start | bytes 3932160 | tf_op jit(solution)/shard_map/all_gather | solution.py:125
  10.1 155.3 %copy-start.24 = (f32[2048]{0:T(1024)}, f32[2048]{0:T(1024)S(1)}, u32[]{:S(2)}) copy-start(f32[2048]{0:T(1024)S(1)} %convert_element_type.119) | copy-start | bytes 24580
  10.8 154.7 %copy-start.22 = (f32[2048]{0:T(1024)}, f32[2048]{0:T(1024)S(1)}, u32[]{:S(2)}) copy-start(f32[2048]{0:T(1024)S(1)} %convert_element_type.118) | copy-start | bytes 24580
  13.2 152.2 %copy-start.28 = (f32[384]{0:T(512)}, f32[384]{0:T(512)S(1)}, u32[]{:S(2)}) copy-start(f32[384]{0:T(512)S(1)} %broadcast_multiply_fusion.2) | copy-start | bytes 4612
  13.8 151.7 %copy-start.30 = (f32[384]{0:T(512)}, f32[384]{0:T(512)S(1)}, u32[]{:S(2)}) copy-start(f32[384]{0:T(512)S(1)} %add_rsqrt_fusion) | copy-start | bytes 4612
  182.7 200.7 %all-gather.19.cloned.1.call-start = ((), (), s32[]{:S(2)}) async-start(), calls=%async_computation.17 | async-start | bytes 3932160 | tf_op jit(solution)/shard_map/all_gather | solution.py:126
  185.2 419.9 %all-gather.15.cloned.1.call-start = ((), (), s32[]{:S(2)}) async-start(), calls=%async_computation.9 | async-start | bytes 17825792 | tf_op jit(solution)/shard_map/all_gather | solution.py:65
  185.8 640.9 %all-gather.17.cloned.1.call-start = ((), (), s32[]{:S(2)}) async-start(), calls=%async_computation.10 | async-start | bytes 17825792 | tf_op jit(solution)/shard_map/all_gather | solution.py:66
  186.4 701.1 %reduce-scatter.7.cloned.1.call-start = ((), (), s32[]{:S(2)}) async-start(), calls=%async_computation.11 | async-start | bytes 3932160 | tf_op jit(solution)/shard_map/reduce_scatter | solution.py:230
  198.6 63.8 %copy-start.20 = (bf16[384,16,16]{0,2,1:T(8,128)(2,1)S(1)}, bf16[384,16,16]{0,2,1:T(8,128)(2,1)}, u32[]{:S(2)}) copy-start(bf16[384,16,16]{0,2,1:T(8,128)(2,1)} %get-tuple-element.384) | copy-start | bytes 589828
  198.6 63.8 %copy-start.21 = (bf16[384,16,16]{0,2,1:T(8,128)(2,1)S(1)}, bf16[384,16,16]{0,2,1:T(8,128)(2,1)}, u32[]{:S(2)}) copy-start(bf16[384,16,16]{0,2,1:T(8,128)(2,1)} %get-tuple-element.385) | copy-start | bytes 589828
  592.3 357.8 %reduce-scatter.9.cloned.1.call-start = ((), (), s32[]{:S(2)}) async-start(), calls=%async_computation.12 | async-start | bytes 3932160 | tf_op jit(solution)/shard_map/reduce_scatter | solution.py:233
  598.3 424.8 %all-reduce.4.cloned.1.call-start = ((), (), s32[]{:S(2)}) async-start(), calls=%async_computation.18 | async-start | bytes 6291456 | tf_op jit(solution)/shard_map/psum | solution.py:160
  605.1 221.6 %copy-start.8 = (bf16[1,384,2048]{2,1,0:T(8,128)(2,1)S(1)}, bf16[1,384,2048]{2,1,0:T(8,128)(2,1)}, u32[]{:S(2)}) copy-start(bf16[1,384,2048]{2,1,0:T(8,128)(2,1)} %param.18) | copy-start | bytes 4718596
  841.9 13.5 copy-start.17
  868.2 23.9 copy-start.7
  893.8 65.9 %copy-start.12 = (bf16[1,384,1024]{2,1,0:T(8,128)(2,1)}, bf16[1,384,1024]{2,1,0:T(8,128)(2,1)S(1)}, u32[]{:S(2)}) copy-start(bf16[1,384,1024]{2,1,0:T(8,128)(2,1)S(1)} %copy.60) | copy-start | bytes 2359300
  895.5 64.2 %copy-start.13 = (bf16[1,384,1024]{2,1,0:T(8,128)(2,1)}, bf16[1,384,1024]{2,1,0:T(8,128)(2,1)S(1)}, u32[]{:S(2)}) copy-start(bf16[1,384,1024]{2,1,0:T(8,128)(2,1)S(1)} %copy.59) | copy-start | bytes 2359300
  959.7 395.5 %reduce-scatter.11.cloned.1.call-start = ((), (), s32[]{:S(2)}) async-start(), calls=%async_computation.13 | async-start | bytes 26738688 | tf_op jit(solution)/shard_map/reduce_scatter | solution.py:270
  974.4 565.1 %reduce-scatter.13.cloned.1.call-start = ((), (), s32[]{:S(2)}) async-start(), calls=%async_computation.14 | async-start | bytes 8912896 | tf_op jit(solution)/shard_map/reduce_scatter | solution.py:271
  982.8 1246.8 %reduce-scatter.15.cloned.1.call-start = ((), (), s32[]{:S(2)}) async-start(), calls=%async_computation.15 | async-start | bytes 35651584 | tf_op jit(solution)/shard_map/reduce_scatter | solution.py:272
  1001.2 1920.2 %reduce-scatter.17.cloned.1.call-start = ((), (), s32[]{:S(2)}) async-start(), calls=%async_computation.16 | async-start | bytes 35651584 | tf_op jit(solution)/shard_map/reduce_scatter | solution.py:273
  (33 other events, 164.6 us)
Sparse Core Ops, SparseCore 0:
  10.8 154.5 all-gather.8
  168.2 87.3 all-gather.12
  257.7 61.5 all-gather.10
  321.3 62.0 all-gather.18
  386.0 190.2 all-gather.14
  578.8 247.8 all-gather.16
  829.0 58.4 reduce-scatter.6
  889.8 60.2 reduce-scatter.8
  959.8 23.2 all-reduce.3
  989.6 365.4 reduce-scatter.10
  1358.2 181.2 reduce-scatter.12
  1542.4 687.1 reduce-scatter.14
  2232.7 688.6 reduce-scatter.16
where the time goes:
time: 2940 us; the launch traced here: 2930 us
  waiting for transfers between devices  2410 us (82%)
  matrix products  290 us (10%)
  blocking collectives  94.3 us (3%)
  local copies, waits for them, and re-layouts  76 us (3%)
  other arithmetic  46.5 us (2%)
    reduce_scatter x1, waiting for transfers between devices, per_device(): lax.psum_scatter(grad_fc2, ('dp', 'ctx'), scatter_dimension=1, tiled=True)  692 us
    reduce_scatter x1, waiting for transfers between devices, per_device(): lax.psum_scatter(grad_fc1, ('dp', 'ctx'), scatter_dimension=0, tiled=True)  690 us
    reduce_scatter x1, waiting for transfers between devices, per_device(): lax.psum_scatter(grad_qkv, ('dp', 'ctx'), scatter_dimension=1, tiled=True)  243 us
    all_gather x1, waiting for transfers between devices, per_device(): lax.all_gather(w_fc2, ('dp', 'ctx'), axis=1, tiled=True)  209 us
    reduce_scatter x1, waiting for transfers between devices, per_device(): lax.psum_scatter(grad_dense, ('dp', 'ctx'), scatter_dimension=1, tiled=True)  181 us
    all_gather x1, waiting for transfers between devices, per_device(): lax.all_gather(w_qkv, ('dp', 'ctx'), axis=1, tiled=True)  151 us
    psum x1, blocking collectives, per_device(): lax.psum((jnp.sum(normed_grad * x_hat, 0), jnp.sum(normed_grad, 0), qkv_b...  82.3 us
  transfers between devices with their start and end apart: 13, of which 11 were waited for; matrix products, arithmetic and copies ran while one was open for 13% of the time, Pallas kernels for 0%

commit v1 on v0

v1 whole, which is shorter than its diff:
```python
import functools
import math

import jax
import jax.numpy as jnp
from jax import lax
from jax.experimental import pallas as pl
from jax.experimental.pallas import tpu as pltpu
from jax.sharding import PartitionSpec as P

HD = 64
ROT = 32
EPS = 1e-05
MIB = 1 << 20
F32 = jnp.float32
BF16 = jnp.bfloat16


def dot_nn(a, b):
    return lax.dot_general(a, b, (((1,), (0,)), ((), ())), preferred_element_type=F32)


def dot_nt(a, b):
    return lax.dot_general(a, b, (((1,), (1,)), ((), ())), preferred_element_type=F32)


def dot_tn(a, b):
    return lax.dot_general(a, b, (((0,), (0,)), ((), ())), preferred_element_type=F32)


def rotary_tables(places):
    half = ROT // 2
    frequency = 10000.0 ** (-(jnp.arange(half, dtype=F32) * 2.0 / ROT))
    angles = places.astype(F32)[:, None] * frequency[None, :]
    cos, sin = jnp.cos(angles), jnp.sin(angles)
    rows = places.shape[0]
    zero = jnp.zeros((rows, half), F32)
    rest0 = jnp.zeros((rows, HD - ROT), F32)
    rest1 = jnp.ones((rows, HD - ROT), F32)
    keep = jnp.concatenate([cos, cos, rest1] * 2, 1)
    from_right = jnp.concatenate([-sin, zero, rest0] * 2, 1)
    from_left = jnp.concatenate([zero, sin, rest0] * 2, 1)
    return keep, from_right, from_left


def turn(v, keep, from_right, from_left):
    half = ROT // 2
    return v * keep + pltpu.roll(v, 128 - half, 1) * from_right + pltpu.roll(v, half, 1) * from_left


def attention_body(
    block_rows, pq, pk, pv, mg, keep, fr, fl, seg_row, seg_col, mix, gq, gk, gv, q, k, v, dq, dk, dv
):
    rows = pq.shape[0]
    scale = 1.0 / math.sqrt(HD)
    q[...] = (turn(pq[...], keep[...], fr[...], fl[...]).astype(BF16) * scale).astype(BF16)
    k[...] = turn(pk[...], keep[...], fr[...], fl[...]).astype(BF16)
    v[...] = pv[...].astype(BF16)
    dk[...] = jnp.zeros_like(dk)
    dv[...] = jnp.zeros_like(dv)
    first = lax.broadcasted_iota(jnp.int32, (block_rows, 128), 1) < HD
    for i in range(rows // block_rows):
        here = pl.ds(i * block_rows, block_rows)
        seen = pl.ds(0, (i + 1) * block_rows)
        keys, values = k[seen, :], v[seen, :]
        shape = (block_rows, (i + 1) * block_rows)
        row_index = lax.broadcasted_iota(jnp.int32, shape, 0) + i * block_rows
        col_index = lax.broadcasted_iota(jnp.int32, shape, 1)
        allowed = (col_index <= row_index) & (seg_col[here, :] == seg_row[:, seen])
        parts = []
        for sub in range(2):
            mine = first if sub == 0 else ~first
            qi = jnp.where(mine, q[here, :], 0)
            mi = jnp.where(mine, mg[here, :], 0)
            scores = jnp.where(allowed, dot_nt(qi, keys), -1e30)
            top = jnp.max(scores, 1, keepdims=True)
            expo = jnp.exp(scores - top)
            probs = expo * (1.0 / jnp.sum(expo, 1, keepdims=True))
            low = probs.astype(BF16)
            out = dot_nn(low, values)
            prob_grad = dot_nt(mi, values)
            delta = jnp.sum(probs * prob_grad, 1, keepdims=True)
            score_grad = (probs * (prob_grad - delta)).astype(BF16)
            dqi = dot_nn(score_grad, keys) * scale
            dk[seen, :] += dot_tn(score_grad, qi)
            dv[seen, :] += dot_tn(low, mi)
            parts.append((out, dqi))
        mix[here, :] = jnp.where(first, parts[0][0], parts[1][0]).astype(BF16)
        dq[here, :] = jnp.where(first, parts[0][1], parts[1][1])
    gq[...] = turn(dq[...], keep[...], -fr[...], -fl[...]).astype(BF16)
    gk[...] = turn(dk[...], keep[...], -fr[...], -fl[...]).astype(BF16)
    gv[...] = dv[...].astype(BF16)


def attention(pq, pk, pv, mg, places, segments):
    rows, cols = pq.shape
    keep, fr, fl = rotary_tables(places)
    pair = pl.BlockSpec((rows, 128), lambda h: (0, h))
    whole = pl.BlockSpec((rows, 128), lambda h: (0, 0))
    return pl.pallas_call(
        functools.partial(attention_body, 256),
        grid=(cols // 128,),
        in_specs=[pair] * 4
        + [whole] * 3
        + [
            pl.BlockSpec((1, rows), lambda h: (0, 0)),
            pl.BlockSpec((rows, 1), lambda h: (0, 0)),
        ],
        out_specs=[pair] * 4,
        out_shape=[jax.ShapeDtypeStruct((rows, cols), BF16)] * 4,
        scratch_shapes=[pltpu.VMEM((rows, 128), BF16)] * 3 + [pltpu.VMEM((rows, 128), F32)] * 3,
        compiler_params=pltpu.CompilerParams(vmem_limit_bytes=48 * MIB),
    )(pq, pk, pv, mg, keep, fr, fl, segments[None, :], segments[:, None])


def attention_plain(pq, pk, pv, mg, places, segments):
    rows, cols = pq.shape
    heads = cols // HD
    half = ROT // 2
    scale = 1.0 / math.sqrt(HD)
    frequency = 10000.0 ** (-(jnp.arange(half, dtype=F32) * 2.0 / ROT))
    angles = places.astype(F32)[:, None] * frequency[None, :]
    cos, sin = jnp.cos(angles)[:, None, :], jnp.sin(angles)[:, None, :]

    def rotate(t, s):
        t = t.reshape(rows, heads, HD)
        a, b = t[..., :half], t[..., half:ROT]
        return jnp.concatenate([a * cos - b * s, b * cos + a * s, t[..., ROT:]], -1)

    q = rotate(pq, sin).astype(BF16)
    k = rotate(pk, sin).astype(BF16)
    v = pv.astype(BF16).reshape(rows, heads, HD)
    m = mg.reshape(rows, heads, HD)
    span = 256
    index = jnp.arange(rows, dtype=jnp.int32)

    def step(carry, items):
        dk, dv = carry
        qi, mi, row_index, row_seg = items
        scores = jnp.einsum("qhd,khd->hqk", qi, k, preferred_element_type=F32) * scale
        allowed = (index[None, :] <= row_index[:, None]) & (segments[None, :] == row_seg[:, None])
        scores = jnp.where(allowed[None], scores, -1e30)
        expo = jnp.exp(scores - jnp.max(scores, -1, keepdims=True))
        probs = expo / jnp.sum(expo, -1, keepdims=True)
        low = probs.astype(BF16)
        out = jnp.einsum("hqk,khd->qhd", low, v, preferred_element_type=F32).astype(BF16)
        prob_grad = jnp.einsum("qhd,khd->hqk", mi, v, preferred_element_type=F32)
        delta = jnp.sum(probs * prob_grad, -1, keepdims=True)
        score_grad = (probs * (prob_grad - delta)).astype(BF16)
        dq = jnp.einsum("hqk,khd->qhd", score_grad, k, preferred_element_type=F32) * scale
        dk = dk + jnp.einsum("hqk,qhd->khd", score_grad, qi, preferred_element_type=F32) * scale
        dv = dv + jnp.einsum("hqk,qhd->khd", low, mi, preferred_element_type=F32)
        return (dk, dv), (out, dq)

    zero = jnp.zeros((rows, heads, HD), F32)
    cut = lambda t: t.reshape((rows // span, span) + t.shape[1:])
    (dk, dv), (out, dq) = lax.scan(step, (zero, zero), (cut(q), cut(m), cut(index), cut(segments)))
    flat = lambda t: t.reshape(rows, cols)
    return (
        flat(out),
        flat(rotate(dq.reshape(rows, cols), -sin)).astype(BF16),
        flat(rotate(dk.reshape(rows, cols), -sin)).astype(BF16),
        flat(dv).astype(BF16),
    )


def gather_plain(x, g, wsrc, places, segments):
    pieces = lax.all_to_all(wsrc, "ctx", split_axis=1, concat_axis=1, tiled=True)
    weights = lax.all_gather(pieces, "dp", axis=1, tiled=True)
    along = lambda t: lax.all_gather(t, "ctx", axis=0, tiled=True)
    return along(x), along(g), weights, along(places), along(segments)


def scatter_plain(out_part, normed_part, weight_part):
    summed = lambda t: lax.psum(
        lax.psum_scatter(t, "ctx", scatter_dimension=0, tiled=True), "tp"
    ).astype(F32)
    pieces = lax.psum_scatter(weight_part, "dp", scatter_dimension=1, tiled=True)
    pieces = lax.all_to_all(pieces, "ctx", split_axis=1, concat_axis=1, tiled=True)
    return summed(out_part), summed(normed_part), pieces.astype(F32)


def layer_norm(x):
    xf = x.astype(F32)
    mean = jnp.mean(xf, -1, keepdims=True)
    centred = xf - mean
    inv_std = lax.rsqrt(jnp.mean(centred * centred, -1, keepdims=True) + EPS)
    return centred * inv_std, inv_std


def per_device(
    block_input,
    cotangent,
    segment_ids,
    positions,
    norm_gain,
    norm_bias,
    w_qkv,
    qkv_bias,
    w_dense,
    w_fc1,
    fc1_bias,
    w_fc2,
    out_bias,
):
    ways = lax.axis_size("ctx")
    me = lax.axis_index("ctx")
    x, g = block_input[0], cotangent[0]
    rows, width = x.shape
    depth = w_fc1.shape[0]
    cols = w_fc1.shape[1] // ways
    head_cols = w_qkv.shape[2] // ways

    fc1 = w_fc1.reshape(depth, ways, cols).transpose(1, 0, 2)
    fc2 = w_fc2.reshape(ways, cols, depth).transpose(0, 2, 1)
    qkv = w_qkv.reshape(3, depth, ways, head_cols).transpose(2, 1, 0, 3)
    dense = w_dense.reshape(ways, head_cols, depth).transpose(0, 2, 1)
    att = jnp.concatenate([qkv.reshape(ways, depth, 3 * head_cols), dense], -1)
    wsrc = jnp.stack([fc1, fc2, att])

    x_all, g_all, weights, places, segments = gather_plain(
        x, g, wsrc, positions[0], segment_ids[0]
    )
    weights = weights.reshape(3, width, cols)
    w1, w2, wa = weights[0], weights[1], weights[2]
    wp, wd = wa[:, : 3 * head_cols], wa[:, 3 * head_cols :]

    gain, shift = norm_gain.astype(F32), norm_bias.astype(F32)
    x_hat, unused = layer_norm(x_all)
    normed = (x_hat * gain + shift).astype(BF16)

    qkv_shift = lax.dynamic_slice_in_dim(qkv_bias, me * head_cols, head_cols, 1)
    fc1_shift = lax.dynamic_slice_in_dim(fc1_bias, me * cols, cols, 0)
    projected = dot_nn(normed, wp) + qkv_shift.astype(F32).reshape(1, 3 * head_cols)
    mix_grad = dot_nn(g_all, wd).astype(BF16)
    attend = attention if head_cols % 128 == 0 else attention_plain
    mixture, gq, gk, gv = attend(
        projected[:, :head_cols],
        projected[:, head_cols : 2 * head_cols],
        projected[:, 2 * head_cols :],
        mix_grad,
        places,
        segments,
    )
    proj_grad = jnp.concatenate([gq, gk, gv], 1)

    hidden_pre = dot_nn(normed, w1) + fc1_shift.astype(F32)
    hidden, gelu_back = jax.vjp(lambda t: jax.nn.gelu(t, approximate=True), hidden_pre)
    hidden = hidden.astype(BF16)
    hidden_grad = gelu_back(dot_nn(g_all, w2))[0].astype(BF16)

    out_part = (dot_nt(mixture, wd) + dot_nt(hidden, w2)).astype(BF16)
    normed_part = dot_nt(proj_grad, wp) + dot_nt(hidden_grad, w1)
    weight_part = jnp.stack(
        [
            dot_tn(normed, hidden_grad).astype(BF16),
            dot_tn(g_all, hidden).astype(BF16),
            jnp.concatenate([dot_tn(normed, proj_grad), dot_tn(g_all, mixture)], 1).astype(BF16),
        ]
    )
    gain_part = jnp.sum(normed_part * x_hat, 0)
    shift_part = jnp.sum(normed_part, 0)
    qkv_bias_part = jnp.sum(proj_grad.astype(F32), 0).reshape(3, head_cols)
    fc1_bias_part = jnp.sum(hidden_grad.astype(F32), 0)

    branches, normed_grad, weight_grads = scatter_plain(
        out_part, normed_part.astype(BF16), weight_part.reshape(3, -1, depth, cols)
    )

    gf = g.astype(F32)
    output = (x.astype(F32) + branches + out_bias.astype(F32)).astype(BF16)
    own_hat, inv_std = layer_norm(x)
    scaled = normed_grad * gain
    grad_input = gf + inv_std * (
        scaled
        - jnp.mean(scaled, -1, keepdims=True)
        - own_hat * jnp.mean(scaled * own_hat, -1, keepdims=True)
    )
    place = lambda t, whole, axis: lax.dynamic_update_slice_in_dim(
        jnp.zeros(whole, F32), t, me * t.shape[axis], axis
    )
    small = lax.psum(
        (
            place(qkv_bias_part, (3, head_cols * ways), 1),
            place(fc1_bias_part, (cols * ways,), 0),
            jnp.sum(gf, 0),
        ),
        ("dp", "ctx"),
    )
    norm_small = lax.psum((gain_part, shift_part), ("dp", "ctx", "tp"))

    grad_fc1 = weight_grads[0].transpose(1, 0, 2).reshape(depth, ways * cols)
    grad_fc2 = weight_grads[1].transpose(0, 2, 1).reshape(ways * cols, depth)
    grad_att = weight_grads[2].reshape(ways, depth, 4, head_cols)
    grad_qkv = grad_att[:, :, :3].transpose(2, 1, 0, 3).reshape(3, depth, ways * head_cols)
    grad_dense = grad_att[:, :, 3].transpose(0, 2, 1).reshape(ways * head_cols, depth)
    return (
        output[None],
        grad_input.astype(BF16)[None],
        norm_small[0],
        norm_small[1],
        grad_qkv,
        small[0],
        grad_dense,
        grad_fc1,
        small[1],
        grad_fc2,
        small[2],
    )


def solution(mesh):
    placed = (
        P("dp", "ctx", None),
        P("dp", "ctx", None),
        P("dp", "ctx"),
        P("dp", "ctx"),
        P(),
        P(),
        P(None, ("dp", "ctx"), "tp"),
        P(None, "tp"),
        P("tp", ("dp", "ctx")),
        P(("dp", "ctx"), "tp"),
        P("tp"),
        P("tp", ("dp", "ctx")),
        P(),
    )
    return jax.shard_map(
        per_device,
        mesh=mesh,
        in_specs=placed,
        out_specs=(
            P("dp", "ctx", None),
            P("dp", "ctx", None),
            P(),
            P(),
            P(None, ("dp", "ctx"), "tp"),
            P(None, "tp"),
            P("tp", ("dp", "ctx")),
            P(("dp", "ctx"), "tp"),
            P("tp"),
            P("tp", ("dp", "ctx")),
            P(),
        ),
        check_vma=False,
    )
```

time: 2940 us -> 1230 us (0.42)
  waiting for transfers between devices: 2410 us -> 667 us
  blocking collectives: 94.3 us -> 298 us
  matrix products: 290 us -> 108 us
  Pallas kernels: 0 us -> 36.1 us
    reduce_scatter x6 -> x2, waiting for transfers between devices: 1880 us -> 283 us  [scatter_plain(): lax.psum_scatter(t, 'ctx', scatter_dimension=0, tiled=True)]
    all_gather x6 -> x3, waiting for transfers between devices: 523 us -> 191 us  [the longest x2 99.8 us: gather_plain(): along = lambda t: lax.all_gather(t, 'ctx', axis=0, tiled=True)]
    unnamed x13 -> x8, waiting for transfers between devices: 2.58 us -> 193 us
    dot_general x33 -> x12, matrix products: 290 us -> 108 us  [the longest x4 42.7 us: dot_nt(): lax.dot_general(a, b, (((1,), (1,)), ((), ())), preferred_element_type=F32)]
    all_to_all x0 -> x1, blocking collectives: none -> 156 us  [gather_plain(): lax.all_to_all(wsrc, 'ctx', split_axis=1, concat_axis=1, tiled=True)]
    pallas_call x0 -> x1, Pallas kernels: none -> 36.1 us  [attention(): pl.pallas_call(functools.partial(attention_body, 256), grid=(cols // 128,...]
    psum x1 -> x2, blocking collectives: 82.3 us -> 118 us  [the longest x1 77.2 us: per_device(): lax.psum((place(qkv_bias_part, (3, head_cols * ways), 1), place(fc1_bias_...]
  transfers between devices with their start and end apart: 13 -> 8, of which waited for: 11 -> 5; matrix products, arithmetic and copies ran while one was open for 13% -> 8% of each run, Pallas kernels for 0% -> 0%
where the time goes in v1:
time: 1230 us; the launch traced here: 1220 us
  waiting for transfers between devices  667 us (54%)
  blocking collectives  298 us (24%)
  matrix products  108 us (9%)
  local copies, waits for them, and re-layouts  58.6 us (5%)
  Pallas kernels  36.1 us (3%)
  other arithmetic  34.2 us (3%)
  between operations  15.6 us (1%)
    reduce_scatter x2, waiting for transfers between devices, scatter_plain(): lax.psum_scatter(t, 'ctx', scatter_dimension=0, tiled=True)  283 us
    unnamed x8, waiting for transfers between devices  193 us
    all_to_all x1, blocking collectives, gather_plain(): lax.all_to_all(wsrc, 'ctx', split_axis=1, concat_axis=1, tiled=True)  156 us
    all_gather x2, waiting for transfers between devices, gather_plain(): along = lambda t: lax.all_gather(t, 'ctx', axis=0, tiled=True)  99.8 us
    all_gather x1, waiting for transfers between devices, gather_plain(): weights = lax.all_gather(pieces, 'dp', axis=1, tiled=True)  91.5 us
    psum x1, blocking collectives, per_device(): lax.psum((place(qkv_bias_part, (3, head_cols * ways), 1), place(fc1_bias_...  77.2 us
    dot_general x4, matrix products, dot_nt(): lax.dot_general(a, b, (((1,), (1,)), ((), ())), preferred_element_type=F32)  42.7 us
    psum x1, blocking collectives, per_device(): norm_small = lax.psum((gain_part, shift_part), ('dp', 'ctx', 'tp'))  40.9 us
  transfers between devices with their start and end apart: 8, of which 5 were waited for; matrix products, arithmetic and copies ran while one was open for 8% of the time, Pallas kernels for 0%

profile of v1, /device:TPU:0, one launch (start us, length us, event | category | flops | bytes accessed | tf_op | source)
XLA Modules:
  0.0 1223.4 jit_solution(1204297856551680707)
XLA Ops:
  12.1 155.9 %all_to_all.10 = bf16[3,4,128,1024]{2,3,0,1:T(8,128)(2,1)S(1)} all-to-all(bf16[3,4,128,1024]{2,3,0,1:T(8,128)(2,1)S(1)} %copy.102), channel_id=1, replica_groups=mesh['dp'=4,'ctx'=4,'tp'=2] {'ctx'}, dimensions={1} | all-to-all | bytes 6291456 | tf_op jit(solution)/shard_map/all_to_all | solution.py:168
  172.4 11.9 all-gather.2
  195.7 12.4 %all-gather.3.seg_row = s32[1,1536]{1,0:T(1,128)S(1)} all-gather(s32[1,384]{1,0:T(1,128)S(1)} %copy-done.21), channel_id=5, replica_groups=mesh['dp'=4,'ctx'=4,'tp'=2] {'ctx'}, dimensions={1}, use_global_device_ids=true | all-gather | bytes 7680 | tf_op jit(solution)/shard_map/all_gather | solution.py:170
  222.6 91.5 %all-gather.8.cloned.1.call-done = bf16[3,16,128,1024]{3,2,1,0:T(8,128)(2,1)} async-done(((bf16[3,4,128,1024]{3,2,1,0:T(8,128)(2,1)}), bf16[3,16,128,1024]{3,2,1,0:T(8,128)(2,1)}) %all-gather.8.cloned.1.call-update) | async-done | bytes 12582928 | tf_op jit(solution)/shard_map/all_gather | solution.py:169
  314.0 8.3 fusion.68
  323.9 5.1 convolution_add_fusion.1
  331.2 99.8 %all-gather.12.cloned.1.call-done = bf16[1,1536,2048]{2,1,0:T(8,128)(2,1)} async-done(((bf16[1,384,2048]{2,1,0:T(8,128)(2,1)}), bf16[1,1536,2048]{2,1,0:T(8,128)(2,1)}) %all-gather.12.cloned.1.call-update) | async-done | bytes 6291472 | tf_op jit(solution)/shard_map/all_gather | solution.py:170
  435.8 36.1 %shard_map.212 = (bf16[1536,256]{1,0:T(8,128)(2,1)S(1)}, bf16[1536,256]{1,0:T(8,128)(2,1)S(1)}, bf16[1536,256]{1,0:T(8,128)(2,1)S(1)}, bf16[1536,256]{1,0:T(8,128)(2,1)S(1)}) custom-call(f32[1536,256]{1,0:T(8,128)} %get-tuple-element.58.pq, f32[1536,256]{1,0:T(8,128)} %get-tuple-element.57.pk, f32[1536,256]{1,0:T(8,128)} %get-tuple-element.56.pv, ...), custom_call_target="tpu_custom_call" | custom-call | tf_op jit(solution)/shard_map/pallas_call | solution.py:100
  472.1 10.5 convolution_convert_fusion.1
  485.1 10.1 fusion.71
  495.3 14.8 %convert_reduce_fusion.1 = (f32[1024]{0:T(1024)S(1)}, bf16[1536,1024]{1,0:T(8,128)(2,1)S(1)}) fusion(f32[1536,1024]{1,0:T(8,128)S(1)} %fusion.71, f32[1024]{0:T(1024)S(1)} %dynamic-slice_convert_fusion, bf16[2048,1024]{1,0:T(8,128)(2,1)S(1)} %bitcast.190, bf16[1,1536,2048]{2,1,0:T(8,128)(2,1)} %all-gather.12.cloned.1.call-done), kind=kOutput, calls=%fused_computation.36 | convolution fusion | flops 6478625792 | bytes 19931136 | tf_op jit(solution)/shard_map/dot_general | solution.py:20
  510.1 8.6 convolution_convert_fusion
  518.7 9.7 convert_bitcast_fusion.1
  528.4 6.4 copy.116
  534.7 9.4 maximum_maximum_fusion
  545.8 10.4 fusion.46
  556.2 15.2 %fusion.67 = (f32[2048]{0:T(1024)S(1)}, f32[2048]{0:T(1024)S(1)}, bf16[1536,2048]{1,0:T(8,128)(2,1)}) fusion(f32[1536]{0:T(1024)S(1)} %add_rsqrt_fusion, f32[1536]{0:T(1024)S(1)} %broadcast_multiply_fusion, bf16[1,1536,2048]{2,1,0:T(8,128)(2,1)} %all-gather.10.cloned.1.call-done, f32[1536,2048]{1,0:T(8,128)} %fusion.46, bf16[1536,1024]{1,0:T(8,128)(2,1)} %copy-done.24, ...), kind=kOutput, calls=%fused_computation.96 | convolution fusion | flops 6467612672 | bytes 32534528 | tf_op jit(solution)/shard_map/dot_general | solution.py:24
  571.4 11.1 fusion.66
  582.6 5.9 add_convert_fusion
  590.4 191.7 %all-reduce.7.cloned.1.call-done = bf16[3,16,128,1024]{3,2,1,0:T(8,128)(2,1)} async-done(((bf16[3,16,128,1024]{3,2,1,0:T(8,128)(2,1)}), bf16[3,16,128,1024]{3,2,1,0:T(8,128)(2,1)}) %all-reduce.7.cloned.1.call-update) | async-done | bytes 12582928
  791.5 160.0 %reduce-scatter.8.cloned.1.call-done = bf16[384,2048]{1,0:T(8,128)(2,1)} async-done(((bf16[1536,2048]{1,0:T(8,128)(2,1)}), bf16[384,2048]{1,0:T(8,128)(2,1)}) %reduce-scatter.8.cloned.1.call-update) | async-done | bytes 1572880 | tf_op jit(solution)/shard_map/reduce_scatter | solution.py:176
  951.5 122.9 %reduce-scatter.6.cloned.1.call-done = bf16[384,2048]{1,0:T(8,128)(2,1)} async-done(((bf16[1536,2048]{1,0:T(8,128)(2,1)}), bf16[384,2048]{1,0:T(8,128)(2,1)}) %reduce-scatter.6.cloned.1.call-update) | async-done | bytes 1572880 | tf_op jit(solution)/shard_map/reduce_scatter | solution.py:176
  1076.9 40.9 %all-reduce.1 = (f32[2048]{0:T(1024)}, f32[2048]{0:T(1024)}) all-reduce(f32[2048]{0:T(1024)S(1)} %get-tuple-element.42, f32[2048]{0:T(1024)S(1)} %get-tuple-element.41), channel_id=1, replica_groups=mesh['dp'=4,'ctx'=4,'tp'=2] {'dp','ctx','tp'}, use_global_device_ids=true, to_apply=%region_11.0 | all-reduce | flops 4096 | bytes 32768 | tf_op jit(solution)/shard_map/psum | solution.py:290
  1117.8 77.2 %all-reduce.2 = (f32[3,1024]{1,0:T(4,128)}, f32[4096]{0:T(1024)}, f32[2048]{0:T(1024)}) all-reduce(f32[3,1024]{1,0:T(4,128)S(1)} %constant_dynamic-update-slice_fusion.3, f32[4096]{0:T(1024)S(1)} %dynamic_update_slice.7, f32[2048]{0:T(1024)S(1)} %convert_reduce_fusion.3), channel_id=1, replica_groups=mesh['dp'=4,'ctx'=4,'tp'=2] {'dp','ctx'}, use_global_device_ids=true, to_apply=%region_16.0 | all-reduce | flops 9216 | bytes 73728 | tf_op jit(solution)/shard_map/psum | solution.py:282
  (142 shorter events, 82.2 us)
Async XLA Ops:
  7.2 204.5 %all-gather.10.cloned.1.call-start = ((), (), s32[]{:S(2)}) async-start(), calls=%async_computation.7 | async-start | bytes 7864320 | tf_op jit(solution)/shard_map/all_gather | solution.py:170
  7.9 306.1 %all-gather.8.cloned.1.call-start = ((), (), s32[]{:S(2)}) async-start(), calls=%async_computation.4 | async-start | bytes 15728640 | tf_op jit(solution)/shard_map/all_gather | solution.py:169
  170.8 260.2 %all-gather.12.cloned.1.call-start = ((), (), s32[]{:S(2)}) async-start(), calls=%async_computation.8 | async-start | bytes 7864320 | tf_op jit(solution)/shard_map/all_gather | solution.py:170
  171.6 610.5 %all-reduce.7.cloned.1.call-start = ((), (), s32[]{:S(2)}) async-start(), calls=%async_computation.9 | async-start | bytes 25165824
  171.6 46.4 %copy-start.15 = (f32[2048]{0:T(1024)}, f32[2048]{0:T(1024)S(1)}, u32[]{:S(2)}) copy-start(f32[2048]{0:T(1024)S(1)} %convert_element_type.87) | copy-start | bytes 24580
  314.0 9.8 copy-start.5
  472.1 10.6 slice-start
  472.1 10.6 copy-start.7
  472.1 10.6 slice-start.1
  485.0 10.2 copy-start.10
  485.1 25.0 %slice-start.4 = ((s8[6291456]{0:T(1024)(128)(4,1)}), s8[4194304]{0:T(1024)(128)(4,1)S(1)}, s32[]{:S(2)}) async-start(s8[6291456]{0:T(1024)(128)(4,1)} %bitcast.185), calls=%async_computation.15 | async-start | bytes 8388608
  485.1 33.6 %slice-start.2 = ((s8[6291456]{0:T(1024)(128)(4,1)}), s8[4194304]{0:T(1024)(128)(4,1)S(1)}, s32[]{:S(2)}) async-start(s8[6291456]{0:T(1024)(128)(4,1)} %bitcast.175), calls=%async_computation.13 | async-start | bytes 8388608
  495.2 23.5 %copy-start.23 = (f32[1536,1024]{1,0:T(8,128)}, f32[1536,1024]{1,0:T(8,128)S(1)}, u32[]{:S(2)}) copy-start(f32[1536,1024]{1,0:T(8,128)S(1)} %fusion.71) | copy-start | bytes 18874372
  495.2 14.9 %slice-start.5 = ((s8[6291456]{0:T(1024)(128)(4,1)}), s8[2097152]{0:T(1024)(128)(4,1)S(1)}, s32[]{:S(2)}) async-start(s8[6291456]{0:T(1024)(128)(4,1)} %bitcast.185), calls=%async_computation.16 | async-start | bytes 4194304
  495.3 23.5 %slice-start.3 = ((s8[6291456]{0:T(1024)(128)(4,1)}), s8[2097152]{0:T(1024)(128)(4,1)S(1)}, s32[]{:S(2)}) async-start(s8[6291456]{0:T(1024)(128)(4,1)} %bitcast.175), calls=%async_computation.14 | async-start | bytes 4194304
  544.2 407.4 %reduce-scatter.8.cloned.1.call-start = ((), (), s32[]{:S(2)}) async-start(), calls=%async_computation.6 | async-start | bytes 7864320 | tf_op jit(solution)/shard_map/reduce_scatter | solution.py:176
  545.8 10.4 copy-start.11
  571.4 503.1 %reduce-scatter.6.cloned.1.call-start = ((), (), s32[]{:S(2)}) async-start(), calls=%async_computation.5 | async-start | bytes 7864320 | tf_op jit(solution)/shard_map/reduce_scatter | solution.py:176
  786.3 288.2 %copy-start.19 = (bf16[2048]{0:T(1024)(128)(2,1)S(1)}, bf16[2048]{0:T(1024)(128)(2,1)}, u32[]{:S(2)}) copy-start(bf16[2048]{0:T(1024)(128)(2,1)} %param.25) | copy-start | bytes 12292
  786.3 288.2 %copy-start.2 = (bf16[1,384,2048]{2,1,0:T(8,128)(2,1)S(1)}, bf16[1,384,2048]{2,1,0:T(8,128)(2,1)}, u32[]{:S(2)}) copy-start(bf16[1,384,2048]{2,1,0:T(8,128)(2,1)} %param.14) | copy-start | bytes 4718596
  786.3 288.5 %copy-start.1 = (bf16[1,384,2048]{2,1,0:T(8,128)(2,1)S(1)}, bf16[1,384,2048]{2,1,0:T(8,128)(2,1)}, u32[]{:S(2)}) copy-start(bf16[1,384,2048]{2,1,0:T(8,128)(2,1)} %param.13) | copy-start | bytes 4718596
  786.3 414.5 %all-to-all-start.1 = ((bf16[3,4,128,1024]{3,2,0,1:T(8,128)(2,1)}), bf16[3,4,128,1024]{3,2,0,1:T(8,128)(2,1)}, u32[]{:S(2)}, u32[]{:S(2)}) async-start(bf16[3,4,128,1024]{3,2,0,1:T(8,128)(2,1)} %copy.110), calls=%async_computation.3 | async-start | bytes 6291456 | tf_op jit(solution)/shard_map/all_to_all | solution.py:179
  791.3 403.8 %all-reduce.9.cloned.1.call-start = ((), (), s32[]{:S(2)}) async-start(), calls=%async_computation.10 | async-start | bytes 6291456 | tf_op jit(solution)/shard_map/psum | solution.py:175
  1074.5 120.5 %copy-start.16 = (f32[2048]{0:T(1024)S(1)}, f32[2048]{0:T(1024)}, u32[]{:S(2)}) copy-start(f32[2048]{0:T(1024)} %copy-done.15) | copy-start | bytes 24580
  (15 other events, 59.4 us)
Sparse Core Ops, SparseCore 0:
  9.6 180.7 all-gather.9
  192.3 121.7 all-gather.7
  315.6 115.3 all-gather.11
  544.3 237.7 all-reduce.6
  784.2 167.2 reduce-scatter.7
  953.7 120.7 reduce-scatter.5
  1076.8 23.7 all-reduce.8

commit v2 on v1

--- a/solution.py
+++ b/solution.py
@@ -14,6 +14,7 @@
 MIB = 1 << 20
 F32 = jnp.float32
 BF16 = jnp.bfloat16
+MESH = pl.DeviceIdType.MESH
 
 
 def dot_nn(a, b):
@@ -180,6 +181,487 @@
     return summed(out_part), summed(normed_part), pieces.astype(F32)
 
 
+def place_of():
+    dp, me, core = lax.axis_index("dp"), lax.axis_index("ctx"), lax.axis_index("tp")
+    return dp, me, core, dp + 1 - 2 * (dp % 2), dp + 2 - 4 * (dp // 2)
+
+
+def greet(ways):
+    dp, me, core, dpx, dpy = place_of()
+    barrier = pltpu.get_barrier_semaphore()
+    for device in [(dp, me, 1 - core), (dpx, me, core), (dpy, me, core)] + [
+        (dp, (me + k) % ways, core) for k in range(1, ways)
+    ]:
+        pl.semaphore_signal(barrier, inc=1, device_id=device, device_id_type=MESH)
+    pl.semaphore_wait(barrier, ways + 2)
+
+
+def remote(src, dst, send, recv, device):
+    return pltpu.make_async_remote_copy(
+        src_ref=src, dst_ref=dst, send_sem=send, recv_sem=recv, device_id=device, device_id_type=MESH
+    )
+
+
+PIECES = 2
+
+
+def gather_body(
+    ways, x, g, w, ids, xo, go, wo, ido, zs, zr, ts, tr, ws, wr, ls, lr, ds, dr, ids_s, ids_r, own
+):
+    dp, me, core, dpx, dpy = place_of()
+    rows = x.shape[0]
+    piece = rows // 2 // PIECES
+    groups = w.shape[0]
+    srcs, outs = (x, g), (xo, go)
+
+    def part(which, s):
+        return pl.ds(pl.multiple_of(which * (rows // 2) + s * piece, 16), piece)
+
+    def along(a, owner, s, side, mine=False):
+        at = part(core, s)
+        src = srcs[a].at[at, :] if mine else outs[a].at[owner, at, :]
+        return remote(
+            src,
+            outs[a].at[owner, at, :],
+            zs.at[side, a, owner, s],
+            zr.at[a, owner, s],
+            (dp, me - 1 + 2 * side, core),
+        )
+
+    def across(a, owner, s, which):
+        at = part(which, s)
+        ref = outs[a].at[owner, at, :]
+        return remote(ref, ref, ts.at[a, owner, s], tr.at[a, owner, s], (dp, me, 1 - core))
+
+    def share(grp, k):
+        return remote(
+            w.at[grp, (me + k) % ways],
+            wo.at[grp, dp, me],
+            ws.at[grp, k],
+            wr.at[grp, k],
+            (dp, (me + k) % ways, core),
+        )
+
+    def source(k):
+        return (me - k + ways) % ways
+
+    def spread(grp, k, axis):
+        src = w.at[grp, me] if k == 0 else wo.at[grp, dp, source(k)]
+        return remote(
+            src,
+            wo.at[grp, dp, source(k)],
+            ls.at[axis, grp, k],
+            lr.at[axis, grp, k],
+            ((dpx, dpy)[axis], me, core),
+        )
+
+    def corner(grp, k):
+        axis = (grp + k) % 2
+        ref = wo.at[grp, (dpx, dpy)[axis], source(k)]
+        return remote(ref, ref, ds.at[grp, k], dr.at[grp, k], ((dpy, dpx)[axis], me, core))
+
+    def labels(k):
+        return remote(
+            ids, ido.at[me], ids_s.at[k], ids_r.at[k], (dp, (me + k) % ways, core)
+        )
+
+    greet(ways)
+    local = [
+        pltpu.make_async_copy(x, xo.at[me], own.at[0]),
+        pltpu.make_async_copy(g, go.at[me], own.at[1]),
+        pltpu.make_async_copy(ids, ido.at[me], own.at[2]),
+    ] + [pltpu.make_async_copy(w.at[i], wo.at[i, dp, me], own.at[3 + i]) for i in range(0)]
+
+    def send_own(a):
+        for s in range(PIECES):
+            pl.when(me > 0)(lambda: along(a, me, s, 0, True).start())
+            pl.when(me < ways - 1)(lambda: along(a, me, s, 1, True).start())
+
+    def send_shares(grp):
+        for k in range(1, ways):
+            share(grp, k).start()
+        for axis in range(2):
+            spread(grp, 0, axis).start()
+
+    def pass_on(a, k):
+        for s in range(PIECES):
+
+            @pl.when(me + k < ways)
+            def _():
+                along(a, me + k, s, 0).wait_recv()
+                pl.when(me > 0)(lambda: along(a, me + k, s, 0).start())
+                across(a, me + k, s, core).start()
+
+            @pl.when(me - k >= 0)
+            def _():
+                along(a, me - k, s, 1).wait_recv()
+                pl.when(me < ways - 1)(lambda: along(a, me - k, s, 1).start())
+                across(a, me - k, s, core).start()
+
+    def spread_on(grp, k):
+        share(grp, k).wait_recv()
+        for axis in range(2):
+            spread(grp, k, axis).start()
+
+    def corner_on(grp, k):
+        axis = (grp + k) % 2
+        spread(grp, k, axis).wait_recv()
+        corner(grp, k).start()
+
+    for k in range(1, ways):
+        labels(k).start()
+    send_own(0)
+    send_shares(0)
+    for copy in local:
+        copy.start()
+    mine = [pltpu.make_async_copy(w.at[i, me], wo.at[i, dp, me], own.at[3 + i]) for i in range(groups)]
+    for copy in mine:
+        copy.start()
+    send_shares(1)
+    send_own(1)
+    send_shares(2)
+    for k in range(1, ways):
+        pass_on(0, k)
+        for grp in range(groups):
+            spread_on(grp, k)
+            corner_on(grp, k - 1)
+        pass_on(1, k)
+    for grp in range(groups):
+        corner_on(grp, ways - 1)
+
+    for k in range(1, ways):
+        labels(k).wait()
+    for copy in local + mine:
+        copy.wait()
+    for a in range(2):
+        for owner in range(ways):
+            for s in range(PIECES):
+
+                @pl.when(owner != me)
+                def _():
+                    across(a, owner, s, core).wait_send()
+                    across(a, owner, s, 1 - core).wait_recv()
+
+                @pl.when((me > 0) & (owner >= me))
+                def _():
+                    along(a, owner, s, 0).wait_send()
+
+                @pl.when((me < ways - 1) & (owner <= me))
+                def _():
+                    along(a, owner, s, 1).wait_send()
+
+    for grp in range(groups):
+        for k in range(ways):
+            axis = (grp + k) % 2
+            if k:
+                share(grp, k).wait_send()
+            for ax in range(2):
+                spread(grp, k, ax).wait_send()
+            spread(grp, k, 1 - axis).wait_recv()
+            corner(grp, k).wait()
+
+
+def gather(x, g, wsrc, places, segments):
+    ways = lax.axis_size("ctx")
+    chips = lax.axis_size("dp")
+    rows, width = x.shape
+    groups, unused, depth, cols = wsrc.shape
+    ids = jnp.zeros((8, rows), jnp.int32).at[0].set(places).at[1].set(segments)
+    dma = pltpu.SemaphoreType.DMA
+    anywhere = pl.BlockSpec(memory_space=pl.ANY)
+    xo, go, wo, ido = pl.pallas_call(
+        functools.partial(gather_body, ways),
+        in_specs=[anywhere] * 4,
+        out_specs=[anywhere] * 4,
+        out_shape=[
+            jax.ShapeDtypeStruct((ways, rows, width), BF16),
+            jax.ShapeDtypeStruct((ways, rows, width), BF16),
+            jax.ShapeDtypeStruct((groups, chips, ways, depth, cols), BF16),
+            jax.ShapeDtypeStruct((ways, 8, rows), jnp.int32),
+        ],
+        scratch_shapes=[
+            dma((2, 2, ways, PIECES)),
+            dma((2, ways, PIECES)),
+            dma((2, ways, PIECES)),
+            dma((2, ways, PIECES)),
+            dma((groups, ways)),
+            dma((groups, ways)),
+            dma((2, groups, ways)),
+            dma((2, groups, ways)),
+            dma((groups, ways)),
+            dma((groups, ways)),
+            dma((ways,)),
+            dma((ways,)),
+            dma((3 + groups,)),
+        ],
+        compiler_params=pltpu.CompilerParams(
+            collective_id=0, has_side_effects=True, vmem_limit_bytes=32 * MIB
+        ),
+    )(x, g, wsrc, ids)
+    ids_all = ido[:, :2].transpose(1, 0, 2).reshape(2, ways * rows)
+    flat = lambda t: t.reshape(ways * rows, width)
+    return flat(xo), flat(go), wo, ids_all[0], ids_all[1]
+
+
+def scatter_body(
+    ways, p0, p1, gw, out, gwo,
+    acc, tin, lin, rin, gown, first_in, second_in,
+    tps, tpr, zs, zr, fs, fr, ss, sr, ws, wr, os, orr, loc, gloc,
+):
+    dp, me, core, dpx, dpy = place_of()
+    rows, width = out.shape[1:]
+    half = rows // 2
+    piece = half // PIECES
+    groups = gw.shape[0]
+    span = gw.shape[2]
+    lanes = gw.shape[3] // 2
+    depth = span // ways
+    parts = (p0, p1)
+    nxt = (dpx, dpy)
+    far = dpx + dpy - dp
+
+    def part(which, s):
+        return pl.ds(pl.multiple_of(which * half + s * piece, 16), piece)
+
+    def swap(a, d, s):
+        return remote(
+            parts[a].at[d, part(1 - core, s), :],
+            tin.at[a, d, s],
+            tps.at[a, d, s],
+            tpr.at[a, d, s],
+            (dp, me, 1 - core),
+        )
+
+    def load(a, d, s):
+        return pltpu.make_async_copy(parts[a].at[d, part(core, s), :], acc.at[a, d, s], loc.at[a, d, s])
+
+    def stream(a, d, s, side):
+        return remote(
+            acc.at[a, d, s],
+            (rin, lin)[side].at[a, d, s],
+            zs.at[side, a, d, s],
+            zr.at[side, a, d, s],
+            (dp, me - 1 + 2 * side, core),
+        )
+
+    def finish(a, s):
+        ref = out.at[a, part(core, s), :]
+        return remote(ref, ref, os.at[a, s], orr.at[a, s], (dp, me, 1 - core))
+
+    def quarter(path, which):
+        return ((nxt[path], far), (nxt[1 - path], dp))[which]
+
+    def lanes_of(path):
+        return pl.ds(path * lanes, lanes)
+
+    def first(grp, path, i):
+        q = quarter(path, 0)[1 - i]
+        return remote(
+            gw.at[grp, q, :, lanes_of(path)],
+            first_in.at[grp, path, i],
+            fs.at[grp, path, i],
+            fr.at[grp, path, i],
+            (nxt[path], me, core),
+        )
+
+    def gload(grp, path, i):
+        q = quarter(path, 1)[i]
+        return pltpu.make_async_copy(
+            gw.at[grp, q, :, lanes_of(path)], gown.at[grp, path, i], gloc.at[grp, path, i]
+        )
+
+    def second(grp, path):
+        return remote(
+            gown.at[grp, path, 0],
+            second_in.at[grp, path],
+            ss.at[grp, path],
+            sr.at[grp, path],
+            (nxt[1 - path], me, core),
+        )
+
+    def share(grp, path, k):
+        d = (me + k) % ways
+        return remote(
+            gown.at[grp, path, 1, pl.ds(pl.multiple_of(d * depth, 16), depth), :],
+            gwo.at[grp, me, :, lanes_of(path)],
+            ws.at[grp, path, k],
+            wr.at[grp, path, k],
+            (dp, d, core),
+        )
+
+    def keep(grp, path):
+        return pltpu.make_async_copy(
+            gown.at[grp, path, 1, pl.ds(pl.multiple_of(me * depth, 16), depth), :],
+            gwo.at[grp, me, :, lanes_of(path)],
+            ws.at[grp, path, 0],
+        )
+
+    def add(dst, src, height):
+        step = 32
+
+        def body(i, carry):
+            at = pl.ds(pl.multiple_of(i * step, step), step)
+            dst[at, :] = dst[at, :] + src[at, :]
+            return carry
+
+        lax.fori_loop(0, height // step, body, 0)
+
+    greet(ways)
+    order = [0, 3, 1, 2] if ways == 4 else list(range(ways))
+    for a in range(2):
+        for d in order:
+            for s in range(PIECES):
+                swap(a, d, s).start()
+                load(a, d, s).start()
+    for grp in range(groups):
+        for i in range(2):
+            for path in range(2):
+                first(grp, path, i).start()
+                gload(grp, path, i).start()
+
+    def merge(a):
+        for d in order:
+            for s in range(PIECES):
+                swap(a, d, s).wait_recv()
+                load(a, d, s).wait()
+                add(acc.at[a, d, s], tin.at[a, d, s], piece)
+                pl.when((me == 0) & (d > 0))(lambda: stream(a, d, s, 1).start())
+                pl.when((me == ways - 1) & (d < ways - 1))(lambda: stream(a, d, s, 0).start())
+
+    def hop(a, k):
+        for s in range(PIECES):
+            for d in range(ways - 1, -1, -1):
+
+                @pl.when((me == k) & (d >= me))
+                def _():
+                    stream(a, d, s, 1).wait_recv()
+                    add(acc.at[a, d, s], lin.at[a, d, s], piece)
+                    pl.when(d > me)(lambda: stream(a, d, s, 1).start())
+
+            for d in range(ways):
+
+                @pl.when((me == ways - 1 - k) & (d <= me))
+                def _():
+                    stream(a, d, s, 0).wait_recv()
+                    add(acc.at[a, d, s], rin.at[a, d, s], piece)
+                    pl.when(d < me)(lambda: stream(a, d, s, 0).start())
+
+    def grads_first(grp):
+        for path in range(2):
+            first(grp, path, 0).wait_recv()
+            gload(grp, path, 0).wait()
+            add(gown.at[grp, path, 0], first_in.at[grp, path, 0], span)
+            second(grp, path).start()
+            first(grp, path, 1).wait_recv()
+            gload(grp, path, 1).wait()
+            add(gown.at[grp, path, 1], first_in.at[grp, path, 1], span)
+
+    def grads_second(grp):
+        for path in range(2):
+            second(grp, path).wait_recv()
+            add(gown.at[grp, path, 1], second_in.at[grp, path], span)
+            for k in range(1, ways):
+                share(grp, path, k).start()
+            keep(grp, path).start()
+
+    def last(a):
+        for s in range(PIECES):
+            out[a, part(core, s), :] = acc[a, me, s]
+            finish(a, s).start()
+
+    merge(0)
+    merge(1)
+    for k in range(1, ways):
+        hop(0, k)
+        if k - 1 < groups:
+            grads_first(k - 1)
+        hop(1, k)
+        if 0 <= k - 2 < groups:
+            grads_second(k - 2)
+    last(0)
+    last(1)
+    grads_second(groups - 1)
+
+    for a in range(2):
+        for s in range(PIECES):
+            finish(a, s).wait_send()
+            remote(
+                out.at[a, part(1 - core, s), :],
+                out.at[a, part(1 - core, s), :],
+                os.at[a, s],
+                orr.at[a, s],
+                (dp, me, 1 - core),
+            ).wait_recv()
+            for d in range(ways):
+                swap(a, d, s).wait_send()
+                pl.when(d > me)(lambda: stream(a, d, s, 1).wait_send())
+                pl.when(d < me)(lambda: stream(a, d, s, 0).wait_send())
+    for grp in range(groups):
+        for path in range(2):
+            for i in range(2):
+                first(grp, path, i).wait_send()
+            second(grp, path).wait_send()
+            keep(grp, path).wait()
+            for k in range(1, ways):
+                share(grp, path, k).wait()
+
+
+def scatter(out_part, normed_part, weight_part):
+    ways = lax.axis_size("ctx")
+    chips = lax.axis_size("dp")
+    width = out_part.shape[1]
+    rows = out_part.shape[0] // ways
+    groups, cols = weight_part.shape[0], weight_part.shape[-1]
+    span = width // chips
+    depth = span // ways
+    piece = rows // 2 // PIECES
+    lanes = cols // 2
+    dma = pltpu.SemaphoreType.DMA
+    anywhere = pl.BlockSpec(memory_space=pl.ANY)
+    inside = pl.BlockSpec(memory_space=pltpu.VMEM)
+    stack = pltpu.VMEM((2, ways, PIECES, piece, width), BF16)
+    out, gwo = pl.pallas_call(
+        functools.partial(scatter_body, ways),
+        in_specs=[anywhere] * 3,
+        out_specs=[inside, anywhere],
+        out_shape=[
+            jax.ShapeDtypeStruct((2, rows, width), BF16),
+            jax.ShapeDtypeStruct((groups, ways, depth, cols), BF16),
+        ],
+        scratch_shapes=[
+            stack,
+            stack,
+            stack,
+            stack,
+            pltpu.VMEM((groups, 2, 2, span, lanes), BF16),
+            pltpu.VMEM((groups, 2, 2, span, lanes), BF16),
+            pltpu.VMEM((groups, 2, span, lanes), BF16),
+            dma((2, ways, PIECES)),
+            dma((2, ways, PIECES)),
+            dma((2, 2, ways, PIECES)),
+            dma((2, 2, ways, PIECES)),
+            dma((groups, 2, 2)),
+            dma((groups, 2, 2)),
+            dma((groups, 2)),
+            dma((groups, 2)),
+            dma((groups, 2, ways)),
+            dma((groups, 2, ways)),
+            dma((2, PIECES)),
+            dma((2, PIECES)),
+            dma((2, ways, PIECES)),
+            dma((groups, 2, 2)),
+        ],
+        compiler_params=pltpu.CompilerParams(
+            collective_id=1, has_side_effects=True, vmem_limit_bytes=56 * MIB
+        ),
+    )(
+        out_part.reshape(ways, rows, width),
+        normed_part.reshape(ways, rows, width),
+        weight_part.reshape(groups, chips, span, cols),
+    )
+    return out[0].astype(F32), out[1].astype(F32), gwo.astype(F32)
+
+
 def layer_norm(x):
     xf = x.astype(F32)
     mean = jnp.mean(xf, -1, keepdims=True)
@@ -218,7 +700,9 @@
     att = jnp.concatenate([qkv.reshape(ways, depth, 3 * head_cols), dense], -1)
     wsrc = jnp.stack([fc1, fc2, att])
 
-    x_all, g_all, weights, places, segments = gather_plain(
+    fast = ways == 4 and lax.axis_size("dp") == 4 and rows % 64 == 0 and head_cols % 128 == 0
+    exchange_in, exchange_out = (gather, scatter) if fast else (gather_plain, scatter_plain)
+    x_all, g_all, weights, places, segments = exchange_in(
         x, g, wsrc, positions[0], segment_ids[0]
     )
     weights = weights.reshape(3, width, cols)
@@ -263,7 +747,7 @@
     qkv_bias_part = jnp.sum(proj_grad.astype(F32), 0).reshape(3, head_cols)
     fc1_bias_part = jnp.sum(hidden_grad.astype(F32), 0)
 
-    branches, normed_grad, weight_grads = scatter_plain(
+    branches, normed_grad, weight_grads = exchange_out(
         out_part, normed_part.astype(BF16), weight_part.reshape(3, -1, depth, cols)
     )
 

time: 1230 us -> 799 us (0.65)
  waiting for transfers between devices: 667 us -> 0 us
  Pallas kernels: 36.1 us -> 431 us
  blocking collectives: 298 us -> 120 us
  local copies, waits for them, and re-layouts: 58.6 us -> 88.4 us
  between operations: 15.6 us -> 1.38 us
    pallas_call x0 -> x2, Pallas kernels: none -> 385 us  [the longest x1 206 us: scatter(): pl.pallas_call(functools.partial(scatter_body, ways), in_specs=[anywhere]...]
    reduce_scatter x2 -> x0, waiting for transfers between devices: 283 us -> none  [scatter_plain(): lax.psum_scatter(t, 'ctx', scatter_dimension=0, tiled=True)]
    unnamed x8 -> x0, waiting for transfers between devices: 193 us -> none
    all_gather x3 -> x0, waiting for transfers between devices: 191 us -> none  [the longest x2 99.8 us: gather_plain(): along = lambda t: lax.all_gather(t, 'ctx', axis=0, tiled=True)]
    all_to_all x1 -> x0, blocking collectives: 156 us -> none  [gather_plain(): lax.all_to_all(wsrc, 'ctx', split_axis=1, concat_axis=1, tiled=True)]
    all_gather x2 -> x0, blocking collectives: 24.3 us -> none  [gather_plain(): along = lambda t: lax.all_gather(t, 'ctx', axis=0, tiled=True)]
  transfers between devices with their start and end apart: 8 -> 0, of which waited for: 5 -> 0; matrix products, arithmetic and copies ran while one was open for 8% -> 0% of each run, Pallas kernels for 0% -> 0%
where the time goes in v2:
time: 799 us; the launch traced here: 794 us
  Pallas kernels  431 us (54%)
  blocking collectives  120 us (15%)
  matrix products  112 us (14%)
  local copies, waits for them, and re-layouts  88.4 us (11%)
  other arithmetic  41.5 us (5%)
    pallas_call x1, Pallas kernels, scatter(): pl.pallas_call(functools.partial(scatter_body, ways), in_specs=[anywhere]...  206 us
    pallas_call x1, Pallas kernels, gather(): pl.pallas_call(functools.partial(gather_body, ways), in_specs=[anywhere]...  179 us
    psum x1, blocking collectives, per_device(): lax.psum((place(qkv_bias_part, (3, head_cols * ways), 1), place(fc1_bias_...  78.3 us
    dot_general x4, matrix products, dot_nt(): lax.dot_general(a, b, (((1,), (1,)), ((), ())), preferred_element_type=F32)  47 us
    pallas_call x1, Pallas kernels, attention(): pl.pallas_call(functools.partial(attention_body, 256), grid=(cols // 128,...  45.9 us
    psum x1, blocking collectives, per_device(): norm_small = lax.psum((gain_part, shift_part), ('dp', 'ctx', 'tp'))  41.4 us
    dot_general x4, matrix products, dot_nn(): lax.dot_general(a, b, (((1,), (0,)), ((), ())), preferred_element_type=F32)  34 us
    dot_general x4, matrix products, dot_tn(): lax.dot_general(a, b, (((0,), (0,)), ((), ())), preferred_element_type=F32)  31.2 us

profile of v2, /device:TPU:0, one launch (start us, length us, event | category | flops | bytes accessed | tf_op | source)
XLA Modules:
  0.0 793.8 jit_solution(4778636886132235732)
XLA Ops:
  18.2 179.0 %shard_map.212 = (bf16[4,384,2048]{2,1,0:T(8,128)(2,1)S(1)}, bf16[4,384,2048]{2,1,0:T(8,128)(2,1)S(1)}, bf16[3,4,4,128,1024]{4,3,2,1,0:T(8,128)(2,1)}, s32[4,8,384]{2,1,0:T(8,128)S(1)}) custom-call(bf16[384,2048]{1,0:T(8,128)(2,1)S(1)} %bitcast.106, bf16[384,2048]{1,0:T(8,128)(2,1)S(1)} %bitcast.107, bf16[3,4,128,1024]{3,2,1,0:T(8,128)(2,1)S(1)} %copy-done.4, ...), custom_call_target="tpu_custom_call" | custom-call | tf_op jit(solution)/shard_map/pallas_call | solution.py:372
  197.2 12.1 %fusion.40 = (bf16[1,4,4,128,1024]{4,3,2,1,0:T(8,128)(2,1)}, bf16[1,4,4,128,1024]{4,3,2,1,0:T(8,128)(2,1)}, bf16[1,4,4,128,1024]{4,3,2,1,0:T(8,128)(2,1)S(1)}) fusion(bf16[3,4,4,128,1024]{4,3,2,1,0:T(8,128)(2,1)} %get-tuple-element.46), kind=kLoop, calls=%fused_computation.86 | loop fusion | bytes 25165824 | tf_op jit(solution)/shard_map/slice | solution.py:709
  214.6 8.5 %fusion.42 = f32[1536,1024]{1,0:T(8,128)} fusion(bf16[1536,2048]{1,0:T(8,128)(2,1)S(1)} %bitcast.126, bf16[2048,1024]{1,0:T(8,128)(2,1)S(1)} %bitcast.132), kind=kOutput, calls=%fused_computation.88 | convolution fusion | flops 6442450944 | bytes 16777216 | tf_op jit(solution)/shard_map/dot_general | solution.py:21
  223.8 13.6 %fusion.37 = f32[1536,2048]{1,0:T(8,128)} fusion(bf16[2048,1024]{1,0:T(8,128)(2,1)} %bitcast.134, f32[1536,1024]{1,0:T(8,128)} %fusion.42, f32[1024]{0:T(1024)S(1)} %dynamic-slice_convert_fusion), kind=kOutput, calls=%fused_computation.84 | convolution fusion | flops 6458179584 | bytes 23072768 | tf_op jit(solution)/shard_map/dot_general | solution.py:25
  237.4 7.8 add_convert_fusion.2
  245.9 8.1 %convolution_add_fusion.1 = f32[1536,768]{1,0:T(8,128)S(1)} fusion(bf16[1536,2048]{1,0:T(8,128)(2,1)} %add_convert_fusion.2, bf16[2048,1024]{1,0:T(8,128)(2,1)} %bitcast.121, f32[768]{0:T(1024)S(1)} %reshape.330), kind=kOutput, calls=%fused_computation.32 | convolution fusion | flops 4833017856 | bytes 14158848 | tf_op jit(solution)/shard_map/dot_general | solution.py:21
  256.2 5.7 convolution_convert_fusion.2.mg
  262.0 4.3 multiply_sine_fusion
  276.5 5.1 concatenate.39.fl
  283.9 45.9 %shard_map.213 = (bf16[1536,256]{1,0:T(8,128)(2,1)S(1)}, bf16[1536,256]{1,0:T(8,128)(2,1)S(1)}, bf16[1536,256]{1,0:T(8,128)(2,1)S(1)}, bf16[1536,256]{1,0:T(8,128)(2,1)S(1)}) custom-call(f32[1536,256]{1,0:T(8,128)} %get-tuple-element.109.pq, f32[1536,256]{1,0:T(8,128)} %get-tuple-element.108.pk, f32[1536,256]{1,0:T(8,128)} %get-tuple-element.107.pv, ...), custom_call_target="tpu_custom_call" | custom-call | tf_op jit(solution)/shard_map/pallas_call | solution.py:101
  329.9 9.3 %add_convert_fusion = bf16[1536,2048]{1,0:T(8,128)(2,1)} fusion(f32[1536,2048]{1,0:T(8,128)} %fusion.37, bf16[1536,256]{1,0:T(8,128)(2,1)S(1)} %get-tuple-element.49, bf16[2048,1024]{1,0:T(8,128)(2,1)S(1)} %bitcast.123), kind=kOutput, calls=%fused_computation.4 | convolution fusion | flops 1616904192 | bytes 20709376 | tf_op jit(solution)/shard_map/dot_general | solution.py:25
  340.9 9.1 %fusion.24 = f32[1536,2048]{1,0:T(8,128)} fusion(bf16[1536,768]{1,0:T(8,128)(2,1)S(1)} %constant_dynamic-update-slice_fusion, bf16[2048,1024]{1,0:T(8,128)(2,1)S(1)} %bitcast.124), kind=kOutput, calls=%fused_computation.50 | convolution fusion | flops 4831838208 | bytes 18087936 | tf_op jit(solution)/shard_map/dot_general | solution.py:25
  350.1 11.7 %convert_reduce_fusion.1 = (f32[1024]{0:T(1024)S(1)}, bf16[1536,1024]{1,0:T(8,128)(2,1)}) fusion(f32[1536,1024]{1,0:T(8,128)S(1)} %bitcast.146, f32[1024]{0:T(1024)S(1)} %dynamic-slice_convert_fusion, bf16[1536,2048]{1,0:T(8,128)(2,1)S(1)} %bitcast.113, bf16[2048,1024]{1,0:T(8,128)(2,1)S(1)} %bitcast.135), kind=kOutput, calls=%fused_computation.19 | convolution fusion | flops 6478625792 | bytes 19931136 | tf_op jit(solution)/shard_map/dot_general | solution.py:21
  361.8 15.0 %fusion.38 = (f32[2048]{0:T(1024)S(1)}, f32[2048]{0:T(1024)S(1)}, bf16[1536,2048]{1,0:T(8,128)(2,1)}) fusion(f32[1536]{0:T(1024)S(1)} %rsqrt.21, f32[1536]{0:T(1024)S(1)} %div.26, bf16[4,384,2048]{2,1,0:T(8,128)(2,1)S(1)} %bitcast.105, f32[1536,2048]{1,0:T(8,128)} %fusion.24, bf16[1536,1024]{1,0:T(8,128)(2,1)} %get-tuple-element.98, ...), kind=kOutput, calls=%fused_computation.85 | convolution fusion | flops 6467612672 | bytes 32534528 | tf_op jit(solution)/shard_map/dot_general | solution.py:25
  376.8 8.7 %copy.73 = bf16[2048,1536]{1,0:T(8,128)(2,1)} copy(bf16[2048,1536]{0,1:T(8,128)(2,1)} %bitcast.109) | data formatting | bytes 12582912 | tf_op jit(solution)/shard_map/dot_general | solution.py:29
  385.5 4.6 fusion.31
  390.1 8.6 %copy.83 = bf16[2048,1536]{1,0:T(8,128)(2,1)} copy(bf16[2048,1536]{0,1:T(8,128)(2,1)} %bitcast.116) | data formatting | bytes 12582912 | tf_op jit(solution)/shard_map/reshape.231
  398.7 8.0 %convert_bitcast_fusion.1 = bf16[1,4,512,768]{3,2,1,0:T(8,128)(2,1)S(1)} fusion(bf16[4,512,1536]{2,1,0:T(8,128)(2,1)} %bitcast.127, bf16[1536,768]{1,0:T(8,128)(2,1)} %copy-done.11), kind=kOutput, calls=%fused_computation.49 | convolution fusion | flops 4833411072 | bytes 11796480 | tf_op jit(solution)/shard_map/dot_general | solution.py:29
  406.7 11.2 %convolution_convert_fusion = bf16[2048,1024]{1,0:T(8,128)(2,1)S(1)} fusion(bf16[1536,2048]{1,0:T(8,128)(2,1)} %bitcast.110, f32[1536,1024]{1,0:T(8,128)} %fusion.42, f32[1024]{0:T(1024)S(1)} %dynamic-slice_convert_fusion), kind=kOutput, calls=%fused_computation.28 | convolution fusion | flops 6460276736 | bytes 16781312 | tf_op jit(solution)/shard_map/dot_general | solution.py:29
  418.0 7.4 convolution_convert_fusion.1
  425.4 5.6 maximum_maximum_fusion.gw
  431.0 205.7 %shard_map.214 = (bf16[2,384,2048]{2,1,0:T(8,128)(2,1)}, bf16[3,4,128,1024]{3,2,1,0:T(8,128)(2,1)}) custom-call(bf16[4,384,2048]{2,1,0:T(8,128)(2,1)} %bitcast.119, bf16[4,384,2048]{2,1,0:T(8,128)(2,1)} %bitcast.128, bf16[3,4,512,1024]{3,2,1,0:T(8,128)(2,1)} %maximum_maximum_fusion.gw), custom_call_target="tpu_custom_call" | custom-call | tf_op jit(solution)/shard_map/pallas_call | solution.py:623
  643.3 41.4 %all-reduce.1 = (f32[2048]{0:T(1024)}, f32[2048]{0:T(1024)}) all-reduce(f32[2048]{0:T(1024)S(1)} %get-tuple-element.89, f32[2048]{0:T(1024)S(1)} %get-tuple-element.88), channel_id=1, replica_groups=mesh['dp'=4,'ctx'=4,'tp'=2] {'dp','ctx','tp'}, use_global_device_ids=true, to_apply=%region_7.0 | all-reduce | flops 4096 | bytes 32768 | tf_op jit(solution)/shard_map/psum | solution.py:774
  698.3 78.3 %all-reduce.2 = (f32[3,1024]{1,0:T(4,128)}, f32[4096]{0:T(1024)}, f32[2048]{0:T(1024)}) all-reduce(f32[3,1024]{1,0:T(4,128)S(1)} %constant_dynamic-update-slice_fusion.3, f32[4096]{0:T(1024)S(1)} %dynamic_update_slice.7, f32[2048]{0:T(1024)S(1)} %convert_reduce_fusion.4), channel_id=1, replica_groups=mesh['dp'=4,'ctx'=4,'tp'=2] {'dp','ctx'}, use_global_device_ids=true, to_apply=%region_11.0 | all-reduce | flops 9216 | bytes 73728 | tf_op jit(solution)/shard_map/psum | solution.py:766
  (123 shorter events, 77.8 us)
Async XLA Ops:
  5.4 10.8 %copy-start.16 = (s32[1,384]{1,0:T(1,128)S(1)}, s32[1,384]{1,0:T(1,128)}, u32[]{:S(2)}) copy-start(s32[1,384]{1,0:T(1,128)} %param.20) | copy-start | bytes 4612
  5.4 10.8 %copy-start.17 = (s32[1,384]{1,0:T(1,128)S(1)}, s32[1,384]{1,0:T(1,128)}, u32[]{:S(2)}) copy-start(s32[1,384]{1,0:T(1,128)} %param.19) | copy-start | bytes 4612
  5.4 10.9 %copy-start.1 = (bf16[1,384,2048]{2,1,0:T(8,128)(2,1)S(1)}, bf16[1,384,2048]{2,1,0:T(8,128)(2,1)}, u32[]{:S(2)}) copy-start(bf16[1,384,2048]{2,1,0:T(8,128)(2,1)} %param.17) | copy-start | bytes 4718596
  5.4 10.9 %copy-start.3 = (bf16[1,384,2048]{2,1,0:T(8,128)(2,1)S(1)}, bf16[1,384,2048]{2,1,0:T(8,128)(2,1)}, u32[]{:S(2)}) copy-start(bf16[1,384,2048]{2,1,0:T(8,128)(2,1)} %param.18) | copy-start | bytes 4718596
  197.2 12.1 %copy-start.5 = (bf16[4,384,2048]{2,1,0:T(8,128)(2,1)}, bf16[4,384,2048]{2,1,0:T(8,128)(2,1)S(1)}, u32[]{:S(2)}) copy-start(bf16[4,384,2048]{2,1,0:T(8,128)(2,1)S(1)} %get-tuple-element.47) | copy-start | bytes 18874372
  197.2 14.8 %copy-start = (bf16[4,384,2048]{2,1,0:T(8,128)(2,1)}, bf16[4,384,2048]{2,1,0:T(8,128)(2,1)S(1)}, u32[]{:S(2)}) copy-start(bf16[4,384,2048]{2,1,0:T(8,128)(2,1)S(1)} %get-tuple-element.45) | copy-start | bytes 18874372
  197.2 12.1 %copy-start.14 = (bf16[2048]{0:T(1024)(128)(2,1)S(1)}, bf16[2048]{0:T(1024)(128)(2,1)}, u32[]{:S(2)}) copy-start(bf16[2048]{0:T(1024)(128)(2,1)} %param.22) | copy-start | bytes 12292
  209.3 5.3 copy-start.12
  283.9 46.0 %copy-start.10 = (bf16[1,4,4,128,1024]{4,3,2,1,0:T(8,128)(2,1)S(1)}, bf16[1,4,4,128,1024]{4,3,2,1,0:T(8,128)(2,1)}, u32[]{:S(2)}) copy-start(bf16[1,4,4,128,1024]{4,3,2,1,0:T(8,128)(2,1)} %get-tuple-element.100) | copy-start | bytes 12582916
  329.9 9.3 %copy-start.6 = (bf16[1536,256]{1,0:T(8,128)(2,1)}, bf16[1536,256]{1,0:T(8,128)(2,1)S(1)}, u32[]{:S(2)}) copy-start(bf16[1536,256]{1,0:T(8,128)(2,1)S(1)} %get-tuple-element.49) | copy-start | bytes 2359300
  339.3 10.7 %slice-start.2 = ((s8[6291456]{0:T(1024)(128)(4,1)}), s8[4194304]{0:T(1024)(128)(4,1)S(1)}, s32[]{:S(2)}) async-start(s8[6291456]{0:T(1024)(128)(4,1)} %bitcast.111), calls=%async_computation.2 | async-start | bytes 8388608
  339.3 10.7 %slice-start.6 = ((s8[6291456]{0:T(1024)(128)(4,1)}), s8[4194304]{0:T(1024)(128)(4,1)S(1)}, s32[]{:S(2)}) async-start(s8[6291456]{0:T(1024)(128)(4,1)} %bitcast.145), calls=%async_computation.6 | async-start | bytes 8388608
  340.9 9.1 %slice-start.3 = ((s8[6291456]{0:T(1024)(128)(4,1)}), s8[2097152]{0:T(1024)(128)(4,1)S(1)}, s32[]{:S(2)}) async-start(s8[6291456]{0:T(1024)(128)(4,1)} %bitcast.111), calls=%async_computation.3 | async-start | bytes 4194304
  340.9 9.1 %copy-start.13 = (bf16[1,4,4,128,1024]{4,3,2,1,0:T(8,128)(2,1)S(1)}, bf16[1,4,4,128,1024]{4,3,2,1,0:T(8,128)(2,1)}, u32[]{:S(2)}) copy-start(bf16[1,4,4,128,1024]{4,3,2,1,0:T(8,128)(2,1)} %get-tuple-element.101) | copy-start | bytes 12582916
  340.9 9.1 %slice-start.7 = ((s8[6291456]{0:T(1024)(128)(4,1)}), s8[2097152]{0:T(1024)(128)(4,1)S(1)}, s32[]{:S(2)}) async-start(s8[6291456]{0:T(1024)(128)(4,1)} %bitcast.145), calls=%async_computation.7 | async-start | bytes 4194304
  340.9 20.9 %slice-start = ((s8[6291456]{0:T(1024)(128)(4,1)}), s8[4194304]{0:T(1024)(128)(4,1)S(1)}, s32[]{:S(2)}) async-start(s8[6291456]{0:T(1024)(128)(4,1)} %bitcast.104), calls=%async_computation | async-start | bytes 8388608
  350.1 11.7 %slice-start.1 = ((s8[6291456]{0:T(1024)(128)(4,1)}), s8[2097152]{0:T(1024)(128)(4,1)S(1)}, s32[]{:S(2)}) async-start(s8[6291456]{0:T(1024)(128)(4,1)} %bitcast.104), calls=%async_computation.1 | async-start | bytes 4194304
  376.8 8.7 %copy-start.7 = (bf16[1536,256]{1,0:T(8,128)(2,1)S(1)}, bf16[1536,256]{1,0:T(8,128)(2,1)}, u32[]{:S(2)}) copy-start(bf16[1536,256]{1,0:T(8,128)(2,1)} %copy-done.6) | copy-start | bytes 2359300
  398.7 19.3 %slice-start.4 = ((s8[6291456]{0:T(1024)(128)(4,1)}), s8[4194304]{0:T(1024)(128)(4,1)S(1)}, s32[]{:S(2)}) async-start(s8[6291456]{0:T(1024)(128)(4,1)} %bitcast.117), calls=%async_computation.4 | async-start | bytes 8388608
  406.7 11.3 %slice-start.5 = ((s8[6291456]{0:T(1024)(128)(4,1)}), s8[2097152]{0:T(1024)(128)(4,1)S(1)}, s32[]{:S(2)}) async-start(s8[6291456]{0:T(1024)(128)(4,1)} %bitcast.117), calls=%async_computation.5 | async-start | bytes 4194304
  406.7 11.3 %copy-start.18 = (bf16[1536,1024]{1,0:T(8,128)(2,1)S(1)}, bf16[1536,1024]{1,0:T(8,128)(2,1)}, u32[]{:S(2)}) copy-start(bf16[1536,1024]{1,0:T(8,128)(2,1)} %get-tuple-element.98) | copy-start | bytes 9437188
  431.0 205.7 %copy-start.2 = (bf16[1,384,2048]{2,1,0:T(8,128)(2,1)S(1)}, bf16[1,384,2048]{2,1,0:T(8,128)(2,1)}, u32[]{:S(2)}) copy-start(bf16[1,384,2048]{2,1,0:T(8,128)(2,1)} %param.17) | copy-start | bytes 4718596
  636.7 3.3 copy-start.15
  636.7 3.3 copy-start.9
  (3 other events, 4.5 us)

commit v3 on v2

--- a/solution.py
+++ b/solution.py
@@ -205,14 +205,29 @@
 PIECES = 2
 
 
-def gather_body(
-    ways, x, g, w, ids, xo, go, wo, ido, zs, zr, ts, tr, ws, wr, ls, lr, ds, dr, ids_s, ids_r, own
+def gelu_and_slope(v):
+    c = math.sqrt(2.0 / math.pi)
+    square = v * v
+    tanh = jnp.tanh(c * v * (1.0 + 0.044715 * square))
+    half = 0.5 * (1.0 + tanh)
+    slope = half + 0.5 * c * v * (1.0 - tanh * tanh) * (1.0 + 3.0 * 0.044715 * square)
+    return v * half, slope
+
+
+def forward_body(
+    ways, x, g, w, ids, gain, shift, fc1_shift, qkv_shift,
+    go, ido, no, xho, ho, hgo, outo, ngo, pro, mgo, wao, biaso,
+    xo, wv, norm, xb, gb, pre, hid, slope, hgb, ob, nb, pb, mb,
+    zs, zr, ts, tr, ws, wr, ls, lr, ds, dr, ids_s, ids_r, own, ls_in, ls_out,
 ):
     dp, me, core, dpx, dpy = place_of()
-    rows = x.shape[0]
+    rows, width = x.shape
     piece = rows // 2 // PIECES
-    groups = w.shape[0]
+    groups, unused, depth, cols = w.shape
+    head_cols = cols // 4
     srcs, outs = (x, g), (xo, go)
+    blocks = [me, 1 + me % 2, None, 3 * (1 - me // 2)]
+    blocks[2] = 6 - me - blocks[1] - blocks[3]
 
     def part(which, s):
         return pl.ds(pl.multiple_of(which * (rows // 2) + s * piece, 16), piece)
@@ -233,10 +248,13 @@
         ref = outs[a].at[owner, at, :]
         return remote(ref, ref, ts.at[a, owner, s], tr.at[a, owner, s], (dp, me, 1 - core))
 
+    def rows_of(chip, j):
+        return pl.ds(pl.multiple_of((chip * ways + j) * depth, 16), depth)
+
     def share(grp, k):
         return remote(
             w.at[grp, (me + k) % ways],
-            wo.at[grp, dp, me],
+            wv.at[grp, rows_of(dp, me), :],
             ws.at[grp, k],
             wr.at[grp, k],
             (dp, (me + k) % ways, core),
@@ -246,10 +264,10 @@
         return (me - k + ways) % ways
 
     def spread(grp, k, axis):
-        src = w.at[grp, me] if k == 0 else wo.at[grp, dp, source(k)]
+        at = rows_of(dp, source(k))
         return remote(
-            src,
-            wo.at[grp, dp, source(k)],
+            w.at[grp, me] if k == 0 else wv.at[grp, at, :],
+            wv.at[grp, at, :],
             ls.at[axis, grp, k],
             lr.at[axis, grp, k],
             ((dpx, dpy)[axis], me, core),
@@ -257,20 +275,11 @@
 
     def corner(grp, k):
         axis = (grp + k) % 2
-        ref = wo.at[grp, (dpx, dpy)[axis], source(k)]
+        ref = wv.at[grp, rows_of((dpx, dpy)[axis], source(k)), :]
         return remote(ref, ref, ds.at[grp, k], dr.at[grp, k], ((dpy, dpx)[axis], me, core))
 
     def labels(k):
-        return remote(
-            ids, ido.at[me], ids_s.at[k], ids_r.at[k], (dp, (me + k) % ways, core)
-        )
-
-    greet(ways)
-    local = [
-        pltpu.make_async_copy(x, xo.at[me], own.at[0]),
-        pltpu.make_async_copy(g, go.at[me], own.at[1]),
-        pltpu.make_async_copy(ids, ido.at[me], own.at[2]),
-    ] + [pltpu.make_async_copy(w.at[i], wo.at[i, dp, me], own.at[3 + i]) for i in range(0)]
+        return remote(ids, ido.at[me], ids_s.at[k], ids_r.at[k], (dp, (me + k) % ways, core))
 
     def send_own(a):
         for s in range(PIECES):
@@ -308,31 +317,181 @@
         spread(grp, k, axis).wait_recv()
         corner(grp, k).start()
 
+    def settle(grp):
+        keeps[grp].wait()
+        for k in range(ways):
+            spread(grp, k, 1 - (grp + k) % 2).wait_recv()
+            corner(grp, k).wait_recv()
+
+    def arrive(a, t):
+        if t:
+            for s in range(PIECES):
+                across(a, blocks[t], s, 1 - core).wait_recv()
+
+    def loop(count, body):
+        lax.fori_loop(0, count, lambda i, c: (body(i), c)[1], 0)
+
+    def load_x(t):
+        src = x if t == 0 else xo.at[blocks[t]]
+        return pltpu.make_async_copy(src, xb.at[t % 2], ls_in.at[0, t])
+
+    def load_g(t):
+        src = g if t == 0 else go.at[blocks[t]]
+        return pltpu.make_async_copy(src, gb.at[t % 2], ls_in.at[1, t])
+
+    def store(which, t):
+        o = blocks[t]
+        src, dst = (
+            (xb.at[t % 2], xho.at[o]),
+            (norm.at[o], no.at[o]),
+            (hid.at[o], ho.at[o]),
+            (ob.at[t % 2], outo.at[o]),
+            (nb.at[t % 2], ngo.at[o]),
+            (hgb.at[t % 2], hgo.at[o]),
+            (pb.at[t % 2], pro.at[o]),
+            (mb.at[t], mgo.at[o]),
+        )[which]
+        return pltpu.make_async_copy(src, dst, ls_out.at[which, t])
+
+    def normalise(t):
+        arrive(0, t)
+        if t >= 2:
+            store(0, t - 2).wait()
+        load_x(t).start()
+        load_x(t).wait()
+        step = 32
+
+        def body(i):
+            at = pl.ds(pl.multiple_of(i * step, step), step)
+            xf = xb[t % 2, at, :].astype(F32)
+            centred = xf - jnp.mean(xf, -1, keepdims=True)
+            inv_std = lax.rsqrt(jnp.mean(centred * centred, -1, keepdims=True) + EPS)
+            x_hat = centred * inv_std
+            norm[blocks[t], at, :] = (x_hat * gain[...] + shift[...]).astype(BF16)
+            xb[t % 2, at, :] = x_hat.astype(BF16)
+
+        loop(rows // step, body)
+        store(0, t).start()
+        store(1, t).start()
+
+    wide = 512
+
+    def span(i):
+        return pl.ds(pl.multiple_of(i * wide, wide), wide)
+
+    def up(t):
+        o = blocks[t]
+
+        def mul(i):
+            pre[:, span(i)] = dot_nn(norm[o], wv[0, :, span(i)]) + fc1_shift[:, span(i)]
+
+        loop(cols // wide, mul)
+
+        def act(i):
+            at = pl.ds(pl.multiple_of(i * 16, 16), 16)
+            value, grad = gelu_and_slope(pre[at, :])
+            hid[o, at, :] = value.astype(BF16)
+            slope[o, at, :] = grad
+
+        loop(rows // 16, act)
+        store(2, t).start()
+
+    def project(t):
+        if t >= 2:
+            store(6, t - 2).wait()
+        o = blocks[t]
+        pb[t % 2] = dot_nn(norm[o], wv[2, :, : 3 * head_cols]) + qkv_shift[...]
+        store(6, t).start()
+
+    def down(t):
+        if t >= 2:
+            store(3, t - 2).wait()
+        o = blocks[t]
+
+        def mul(i):
+            ob[t % 2, :, span(i)] = dot_nt(hid[o], wv[1, span(i), :]).astype(BF16)
+
+        loop(width // wide, mul)
+        store(3, t).start()
+
+    def back(t):
+        arrive(1, t)
+        load_g(t).start()
+        if t >= 2:
+            store(4, t - 2).wait()
+            store(5, t - 2).wait()
+        load_g(t).wait()
+        o = blocks[t]
+
+        def mul(i):
+            act = dot_nn(gb[t % 2], wv[1, :, span(i)])
+            grad = (act * slope[o, :, span(i)]).astype(BF16)
+            hgb[t % 2, :, span(i)] = grad
+            total = jnp.sum(grad.astype(F32), 0, keepdims=True)
+            biaso[:, span(i)] = total if t == 0 else biaso[:, span(i)] + total
+
+        loop(cols // wide, mul)
+        store(5, t).start()
+
+        def mul_back(i):
+            nb[t % 2, :, span(i)] = dot_nt(hgb[t % 2], wv[0, span(i), :]).astype(BF16)
+
+        loop(width // wide, mul_back)
+        store(4, t).start()
+        mb[t] = dot_nn(gb[t % 2], wv[2, :, 3 * head_cols :]).astype(BF16)
+        store(7, t).start()
+
+    greet(ways)
+    send_own(0)
+    send_shares(0)
+    send_shares(1)
     for k in range(1, ways):
         labels(k).start()
-    send_own(0)
-    send_shares(0)
-    for copy in local:
+    keeps = [
+        pltpu.make_async_copy(w.at[i, me], wv.at[i, rows_of(dp, me), :], own.at[i])
+        for i in range(groups)
+    ] + [
+        pltpu.make_async_copy(g, go.at[me], own.at[groups]),
+        pltpu.make_async_copy(ids, ido.at[me], own.at[groups + 1]),
+    ]
+    for copy in keeps:
         copy.start()
-    mine = [pltpu.make_async_copy(w.at[i, me], wo.at[i, dp, me], own.at[3 + i]) for i in range(groups)]
-    for copy in mine:
-        copy.start()
-    send_shares(1)
-    send_own(1)
-    send_shares(2)
-    for k in range(1, ways):
-        pass_on(0, k)
-        for grp in range(groups):
-            spread_on(grp, k)
-            corner_on(grp, k - 1)
-        pass_on(1, k)
-    for grp in range(groups):
-        corner_on(grp, ways - 1)
+    wa_out = pltpu.make_async_copy(wv.at[2], wao, own.at[groups + 2])
+    steps = dict(
+        S=send_shares,
+        G=lambda: send_own(1),
+        W=wa_out.start,
+        x=lambda k: pass_on(0, k),
+        g=lambda k: pass_on(1, k),
+        s=spread_on,
+        c=corner_on,
+        e=settle,
+        n=normalise,
+        u=up,
+        p=project,
+        d=down,
+        b=back,
+    )
+    plan = (
+        "n0", "s01", "c00", "x1", "S2", "n1", "s02", "c01", "s03", "c02", "x2", "G", "n2", "c03",
+        "s11", "c10", "s12", "c11", "s13", "c12", "x3", "n3", "e0", "u0", "c13", "s21", "c20",
+        "u1", "s22", "c21", "g1", "u2", "s23", "c22", "u3", "c23", "e1", "d0", "d1", "g2", "e2",
+        "W", "p0", "b0", "p1", "b1", "d2", "p2", "g3", "b2", "d3", "p3", "b3",
+    )
+    for word in plan:
+        steps[word[0]](*(int(digit) for digit in word[1:]))
+    for copy in keeps[groups:]:
+        copy.wait()
 
     for k in range(1, ways):
         labels(k).wait()
-    for copy in local + mine:
-        copy.wait()
+    wa_out.wait()
+    for t in range(4):
+        for which in (1, 2, 7):
+            store(which, t).wait()
+        if t >= 2:
+            for which in (0, 3, 4, 5, 6):
+                store(which, t).wait()
     for a in range(2):
         for owner in range(ways):
             for s in range(PIECES):
@@ -340,7 +499,6 @@
                 @pl.when(owner != me)
                 def _():
                     across(a, owner, s, core).wait_send()
-                    across(a, owner, s, 1 - core).wait_recv()
 
                 @pl.when((me > 0) & (owner >= me))
                 def _():
@@ -352,34 +510,56 @@
 
     for grp in range(groups):
         for k in range(ways):
-            axis = (grp + k) % 2
             if k:
                 share(grp, k).wait_send()
-            for ax in range(2):
-                spread(grp, k, ax).wait_send()
-            spread(grp, k, 1 - axis).wait_recv()
-            corner(grp, k).wait()
-
-
-def gather(x, g, wsrc, places, segments):
+            for axis in range(2):
+                spread(grp, k, axis).wait_send()
+            corner(grp, k).wait_send()
+
+
+def forward(x, g, wsrc, places, segments, gain, shift, fc1_shift, qkv_shift):
     ways = lax.axis_size("ctx")
-    chips = lax.axis_size("dp")
     rows, width = x.shape
     groups, unused, depth, cols = wsrc.shape
+    head_cols = cols // 4
     ids = jnp.zeros((8, rows), jnp.int32).at[0].set(places).at[1].set(segments)
     dma = pltpu.SemaphoreType.DMA
+    vmem = pltpu.VMEM
     anywhere = pl.BlockSpec(memory_space=pl.ANY)
-    xo, go, wo, ido = pl.pallas_call(
-        functools.partial(gather_body, ways),
-        in_specs=[anywhere] * 4,
-        out_specs=[anywhere] * 4,
+    inside = pl.BlockSpec(memory_space=pltpu.VMEM)
+    seq = lambda n, dtype=BF16: jax.ShapeDtypeStruct((ways, rows, n), dtype)
+    outs = pl.pallas_call(
+        functools.partial(forward_body, ways),
+        in_specs=[anywhere] * 4 + [inside] * 4,
+        out_specs=[anywhere] * 11 + [inside, anywhere],
         out_shape=[
-            jax.ShapeDtypeStruct((ways, rows, width), BF16),
-            jax.ShapeDtypeStruct((ways, rows, width), BF16),
-            jax.ShapeDtypeStruct((groups, chips, ways, depth, cols), BF16),
+            seq(width),
             jax.ShapeDtypeStruct((ways, 8, rows), jnp.int32),
+            seq(width),
+            seq(width),
+            seq(cols),
+            seq(cols),
+            seq(width),
+            seq(width),
+            seq(3 * head_cols, F32),
+            seq(head_cols),
+            jax.ShapeDtypeStruct((width, cols), BF16),
+            jax.ShapeDtypeStruct((1, cols), F32),
+            seq(width),
         ],
         scratch_shapes=[
+            vmem((groups, width, cols), BF16),
+            vmem((ways, rows, width), BF16),
+            vmem((2, rows, width), BF16),
+            vmem((2, rows, width), BF16),
+            vmem((rows, cols), F32),
+            vmem((ways, rows, cols), BF16),
+            vmem((ways, rows, cols), F32),
+            vmem((2, rows, cols), BF16),
+            vmem((2, rows, width), BF16),
+            vmem((2, rows, width), BF16),
+            vmem((2, rows, 3 * head_cols), F32),
+            vmem((ways, rows, head_cols), BF16),
             dma((2, 2, ways, PIECES)),
             dma((2, ways, PIECES)),
             dma((2, ways, PIECES)),
@@ -393,20 +573,25 @@
             dma((ways,)),
             dma((ways,)),
             dma((3 + groups,)),
+            dma((2, ways)),
+            dma((8, ways)),
         ],
         compiler_params=pltpu.CompilerParams(
-            collective_id=0, has_side_effects=True, vmem_limit_bytes=32 * MIB
+            collective_id=0, has_side_effects=True, vmem_limit_bytes=60 * MIB
         ),
-    )(x, g, wsrc, ids)
-    ids_all = ido[:, :2].transpose(1, 0, 2).reshape(2, ways * rows)
-    flat = lambda t: t.reshape(ways * rows, width)
-    return flat(xo), flat(go), wo, ids_all[0], ids_all[1]
+    )(
+        x, g, wsrc, ids,
+        gain.reshape(1, width), shift.reshape(1, width), fc1_shift.reshape(1, cols),
+        qkv_shift.reshape(1, 3 * head_cols),
+    )
+    return outs
 
 
 def scatter_body(
-    ways, p0, p1, gw, out, gwo,
+    ways, p0, p1, gw, small, out, gwo, smallo,
     acc, tin, lin, rin, gown, first_in, second_in,
     tps, tpr, zs, zr, fs, fr, ss, sr, ws, wr, os, orr, loc, gloc,
+    sum_in, sum_out, sms, smr,
 ):
     dp, me, core, dpx, dpy = place_of()
     rows, width = out.shape[1:]
@@ -506,7 +691,32 @@
 
         lax.fori_loop(0, height // step, body, 0)
 
+    def small_send(i):
+        src = small if i == 0 else sum_out.at[i - 1]
+        device = ((dp, me, 1 - core), (dpx, me, core), (dpy, me, core))[i]
+        return remote(src, sum_in.at[i], sms.at[i], smr.at[i], device)
+
+    def small_all(k):
+        device = (dp, (me + k) % ways, core)
+        return remote(sum_out.at[2], smallo.at[me], sms.at[2 + k], smr.at[2 + k], device)
+
+    def small_step(i):
+        small_send(i).wait_recv()
+        before = small[...] if i == 0 else sum_out[i - 1]
+        after = before + sum_in[i]
+        if i == 0:
+            row = lax.broadcasted_iota(jnp.int32, after.shape, 0)
+            after = jnp.where(row < 2, after, before)
+        sum_out[i] = after
+        if i < 2:
+            small_send(i + 1).start()
+        else:
+            for k in range(1, ways):
+                small_all(k).start()
+            smallo[me] = after
+
     greet(ways)
+    small_send(0).start()
     order = [0, 3, 1, 2] if ways == 4 else list(range(ways))
     for a in range(2):
         for d in order:
@@ -570,9 +780,13 @@
             finish(a, s).start()
 
     merge(0)
+    small_step(0)
     merge(1)
+    small_step(1)
     for k in range(1, ways):
         hop(0, k)
+        if k == 1:
+            small_step(2)
         if k - 1 < groups:
             grads_first(k - 1)
         hop(1, k)
@@ -582,6 +796,10 @@
     last(1)
     grads_second(groups - 1)
 
+    for i in range(3):
+        small_send(i).wait_send()
+    for k in range(1, ways):
+        small_all(k).wait()
     for a in range(2):
         for s in range(PIECES):
             finish(a, s).wait_send()
@@ -606,7 +824,7 @@
                 share(grp, path, k).wait()
 
 
-def scatter(out_part, normed_part, weight_part):
+def scatter(out_part, normed_part, weight_part, small):
     ways = lax.axis_size("ctx")
     chips = lax.axis_size("dp")
     width = out_part.shape[1]
@@ -620,13 +838,14 @@
     anywhere = pl.BlockSpec(memory_space=pl.ANY)
     inside = pl.BlockSpec(memory_space=pltpu.VMEM)
     stack = pltpu.VMEM((2, ways, PIECES, piece, width), BF16)
-    out, gwo = pl.pallas_call(
+    out, gwo, smallo = pl.pallas_call(
         functools.partial(scatter_body, ways),
-        in_specs=[anywhere] * 3,
-        out_specs=[inside, anywhere],
+        in_specs=[anywhere] * 3 + [inside],
+        out_specs=[inside, anywhere, inside],
         out_shape=[
             jax.ShapeDtypeStruct((2, rows, width), BF16),
             jax.ShapeDtypeStruct((groups, ways, depth, cols), BF16),
+            jax.ShapeDtypeStruct((ways,) + small.shape, F32),
         ],
         scratch_shapes=[
             stack,
@@ -650,6 +869,10 @@
             dma((2, PIECES)),
             dma((2, ways, PIECES)),
             dma((groups, 2, 2)),
+            pltpu.VMEM((3,) + small.shape, F32),
+            pltpu.VMEM((3,) + small.shape, F32),
+            dma((2 + ways,)),
+            dma((2 + ways,)),
         ],
         compiler_params=pltpu.CompilerParams(
             collective_id=1, has_side_effects=True, vmem_limit_bytes=56 * MIB
@@ -658,8 +881,9 @@
         out_part.reshape(ways, rows, width),
         normed_part.reshape(ways, rows, width),
         weight_part.reshape(groups, chips, span, cols),
-    )
-    return out[0].astype(F32), out[1].astype(F32), gwo.astype(F32)
+        small,
+    )
+    return out[0].astype(F32), out[1].astype(F32), gwo.astype(F32), smallo
 
 
 def layer_norm(x):
@@ -668,6 +892,123 @@
     centred = xf - mean
     inv_std = lax.rsqrt(jnp.mean(centred * centred, -1, keepdims=True) + EPS)
     return centred * inv_std, inv_std
+
+
+def plain_work(x, g, wsrc, places, segments, gain, shift, fc1_shift, qkv_shift):
+    me, ways = lax.axis_index("ctx"), lax.axis_size("ctx")
+    width = x.shape[1]
+    unused, unused, depth, cols = wsrc.shape
+    head_cols = cols // 4
+    x_all, g_all, weights, places, segments = gather_plain(x, g, wsrc, places, segments)
+    weights = weights.reshape(3, width, cols)
+    w1, w2, wa = weights[0], weights[1], weights[2]
+    wp, wd = wa[:, : 3 * head_cols], wa[:, 3 * head_cols :]
+    x_hat, unused = layer_norm(x_all)
+    normed = (x_hat * gain + shift).astype(BF16)
+    projected = dot_nn(normed, wp) + qkv_shift.reshape(1, 3 * head_cols)
+    mix_grad = dot_nn(g_all, wd).astype(BF16)
+    attend = attention if head_cols % 128 == 0 else attention_plain
+    mixture, gq, gk, gv = attend(
+        projected[:, :head_cols],
+        projected[:, head_cols : 2 * head_cols],
+        projected[:, 2 * head_cols :],
+        mix_grad,
+        places,
+        segments,
+    )
+    proj_grad = jnp.concatenate([gq, gk, gv], 1)
+
+    hidden_pre = dot_nn(normed, w1) + fc1_shift
+    hidden, slope = gelu_and_slope(hidden_pre)
+    hidden = hidden.astype(BF16)
+    hidden_grad = (dot_nn(g_all, w2) * slope).astype(BF16)
+
+    out_part = (dot_nt(mixture, wd) + dot_nt(hidden, w2)).astype(BF16)
+    normed_part = dot_nt(proj_grad, wp) + dot_nt(hidden_grad, w1)
+    weight_part = jnp.stack(
+        [
+            dot_tn(normed, hidden_grad).astype(BF16),
+            dot_tn(g_all, hidden).astype(BF16),
+            jnp.concatenate([dot_tn(normed, proj_grad), dot_tn(g_all, mixture)], 1).astype(BF16),
+        ]
+    )
+    qkv_bias_part = jnp.sum(proj_grad.astype(F32), 0).reshape(3, head_cols)
+    fc1_bias_part = jnp.sum(hidden_grad.astype(F32), 0)
+    branches, normed_grad, weight_grads = scatter_plain(
+        out_part, normed_part.astype(BF16), weight_part.reshape(3, -1, depth, cols)
+    )
+    place = lambda t, whole, axis: lax.dynamic_update_slice_in_dim(
+        jnp.zeros(whole, F32), t, me * t.shape[axis], axis
+    )
+    small = lax.psum(
+        (
+            place(qkv_bias_part, (3, head_cols * ways), 1),
+            place(fc1_bias_part, (cols * ways,), 0),
+            jnp.sum(g.astype(F32), 0),
+        ),
+        ("dp", "ctx"),
+    )
+    norms = lax.psum(
+        (jnp.sum(normed_part * x_hat, 0), jnp.sum(normed_part, 0)), ("dp", "ctx", "tp")
+    )
+    return branches, normed_grad, weight_grads, norms + small
+
+
+def fast_work(x, g, wsrc, places, segments, gain, shift, fc1_shift, qkv_shift):
+    ways = lax.axis_size("ctx")
+    rows, width = x.shape
+    unused, unused, depth, cols = wsrc.shape
+    head_cols = cols // 4
+    g_all, ids, normed, x_hat, hidden, hidden_grad, out_mlp, back_mlp, projected, mix_grad, wa, fc1_sum, unused = forward(
+        x, g, wsrc, places, segments, gain, shift, fc1_shift, qkv_shift
+    )
+    flat = lambda t: t.reshape(ways * rows, t.shape[-1])
+    g_all, normed, x_hat, hidden, hidden_grad = map(flat, (g_all, normed, x_hat, hidden, hidden_grad))
+    out_mlp, back_mlp, projected, mix_grad = map(flat, (out_mlp, back_mlp, projected, mix_grad))
+    ids = ids[:, :2].transpose(1, 0, 2).reshape(2, ways * rows)
+    wp, wd = wa[:, : 3 * head_cols], wa[:, 3 * head_cols :]
+    mixture, gq, gk, gv = attention(
+        projected[:, :head_cols],
+        projected[:, head_cols : 2 * head_cols],
+        projected[:, 2 * head_cols :],
+        mix_grad,
+        ids[0],
+        ids[1],
+    )
+    proj_grad = jnp.concatenate([gq, gk, gv], 1)
+    out_part = (dot_nt(mixture, wd) + out_mlp.astype(F32)).astype(BF16)
+    normed_part = dot_nt(proj_grad, wp) + back_mlp.astype(F32)
+    weight_part = jnp.stack(
+        [
+            dot_tn(normed, hidden_grad).astype(BF16),
+            dot_tn(g_all, hidden).astype(BF16),
+            jnp.concatenate([dot_tn(normed, proj_grad), dot_tn(g_all, mixture)], 1).astype(BF16),
+        ]
+    )
+    qkv_sum = jnp.sum(proj_grad.astype(F32), 0)
+    line = lambda t: jnp.pad(t.reshape(-1), (0, width - t.size))
+    small = jnp.stack(
+        [
+            jnp.sum(normed_part * x_hat.astype(F32), 0),
+            jnp.sum(normed_part, 0),
+            jnp.sum(g.astype(F32), 0),
+            line(fc1_sum),
+            line(qkv_sum),
+        ]
+        + [jnp.zeros((width,), F32)] * 3
+    )
+    branches, normed_grad, weight_grads, sums = scatter(
+        out_part, normed_part.astype(BF16), weight_part, small
+    )
+    total = jnp.sum(sums[:, :3], 0)
+    fc1_bias_sum = sums[:, 3, :cols].reshape(ways * cols)
+    qkv_bias_sum = sums[:, 4, : 3 * head_cols].reshape(ways, 3, head_cols).transpose(1, 0, 2)
+    return (
+        branches,
+        normed_grad,
+        weight_grads,
+        (total[0], total[1], qkv_bias_sum.reshape(3, ways * head_cols), fc1_bias_sum, total[2]),
+    )
 
 
 def per_device(
@@ -700,55 +1041,13 @@
     att = jnp.concatenate([qkv.reshape(ways, depth, 3 * head_cols), dense], -1)
     wsrc = jnp.stack([fc1, fc2, att])
 
+    gain, shift = norm_gain.astype(F32), norm_bias.astype(F32)
+    qkv_shift = lax.dynamic_slice_in_dim(qkv_bias, me * head_cols, head_cols, 1).astype(F32)
+    fc1_shift = lax.dynamic_slice_in_dim(fc1_bias, me * cols, cols, 0).astype(F32)
     fast = ways == 4 and lax.axis_size("dp") == 4 and rows % 64 == 0 and head_cols % 128 == 0
-    exchange_in, exchange_out = (gather, scatter) if fast else (gather_plain, scatter_plain)
-    x_all, g_all, weights, places, segments = exchange_in(
-        x, g, wsrc, positions[0], segment_ids[0]
-    )
-    weights = weights.reshape(3, width, cols)
-    w1, w2, wa = weights[0], weights[1], weights[2]
-    wp, wd = wa[:, : 3 * head_cols], wa[:, 3 * head_cols :]
-
-    gain, shift = norm_gain.astype(F32), norm_bias.astype(F32)
-    x_hat, unused = layer_norm(x_all)
-    normed = (x_hat * gain + shift).astype(BF16)
-
-    qkv_shift = lax.dynamic_slice_in_dim(qkv_bias, me * head_cols, head_cols, 1)
-    fc1_shift = lax.dynamic_slice_in_dim(fc1_bias, me * cols, cols, 0)
-    projected = dot_nn(normed, wp) + qkv_shift.astype(F32).reshape(1, 3 * head_cols)
-    mix_grad = dot_nn(g_all, wd).astype(BF16)
-    attend = attention if head_cols % 128 == 0 else attention_plain
-    mixture, gq, gk, gv = attend(
-        projected[:, :head_cols],
-        projected[:, head_cols : 2 * head_cols],
-        projected[:, 2 * head_cols :],
-        mix_grad,
-        places,
-        segments,
-    )
-    proj_grad = jnp.concatenate([gq, gk, gv], 1)
-
-    hidden_pre = dot_nn(normed, w1) + fc1_shift.astype(F32)
-    hidden, gelu_back = jax.vjp(lambda t: jax.nn.gelu(t, approximate=True), hidden_pre)
-    hidden = hidden.astype(BF16)
-    hidden_grad = gelu_back(dot_nn(g_all, w2))[0].astype(BF16)
-
-    out_part = (dot_nt(mixture, wd) + dot_nt(hidden, w2)).astype(BF16)
-    normed_part = dot_nt(proj_grad, wp) + dot_nt(hidden_grad, w1)
-    weight_part = jnp.stack(
-        [
-            dot_tn(normed, hidden_grad).astype(BF16),
-            dot_tn(g_all, hidden).astype(BF16),
-            jnp.concatenate([dot_tn(normed, proj_grad), dot_tn(g_all, mixture)], 1).astype(BF16),
-        ]
-    )
-    gain_part = jnp.sum(normed_part * x_hat, 0)
-    shift_part = jnp.sum(normed_part, 0)
-    qkv_bias_part = jnp.sum(proj_grad.astype(F32), 0).reshape(3, head_cols)
-    fc1_bias_part = jnp.sum(hidden_grad.astype(F32), 0)
-
-    branches, normed_grad, weight_grads = exchange_out(
-        out_part, normed_part.astype(BF16), weight_part.reshape(3, -1, depth, cols)
+    work = fast_work if fast else plain_work
+    branches, normed_grad, weight_grads, sums = work(
+        x, g, wsrc, positions[0], segment_ids[0], gain, shift, fc1_shift, qkv_shift
     )
 
     gf = g.astype(F32)
@@ -760,18 +1059,7 @@
         - jnp.mean(scaled, -1, keepdims=True)
         - own_hat * jnp.mean(scaled * own_hat, -1, keepdims=True)
     )
-    place = lambda t, whole, axis: lax.dynamic_update_slice_in_dim(
-        jnp.zeros(whole, F32), t, me * t.shape[axis], axis
-    )
-    small = lax.psum(
-        (
-            place(qkv_bias_part, (3, head_cols * ways), 1),
-            place(fc1_bias_part, (cols * ways,), 0),
-            jnp.sum(gf, 0),
-        ),
-        ("dp", "ctx"),
-    )
-    norm_small = lax.psum((gain_part, shift_part), ("dp", "ctx", "tp"))
+    gain_sum, shift_sum, qkv_bias_sum, fc1_bias_sum, out_bias_sum = sums
 
     grad_fc1 = weight_grads[0].transpose(1, 0, 2).reshape(depth, ways * cols)
     grad_fc2 = weight_grads[1].transpose(0, 2, 1).reshape(ways * cols, depth)
@@ -781,15 +1069,15 @@
     return (
         output[None],
         grad_input.astype(BF16)[None],
-        norm_small[0],
-        norm_small[1],
+        gain_sum,
+        shift_sum,
         grad_qkv,
-        small[0],
+        qkv_bias_sum,
         grad_dense,
         grad_fc1,
-        small[1],
+        fc1_bias_sum,
         grad_fc2,
-        small[2],
+        out_bias_sum,
     )
 
 

time: 799 us -> 626 us (0.78)
  blocking collectives: 120 us -> 0 us
  matrix products: 112 us -> 47.3 us
  Pallas kernels: 431 us -> 476 us
  local copies, waits for them, and re-layouts: 88.4 us -> 70.5 us
  other arithmetic: 41.5 us -> 26.2 us
    psum x2 -> x0, blocking collectives: 120 us -> none  [the longest x1 78.3 us: per_device(): lax.psum((place(qkv_bias_part, (3, head_cols * ways), 1), place(fc1_bias_...]
    pallas_call x1, Pallas kernels: 179 us -> 216 us  [forward(): pl.pallas_call(functools.partial(forward_body, ways), in_specs=[anywhere]...]
    dot_general x4 -> x0, matrix products: 34 us -> none  [dot_nn(): lax.dot_general(a, b, (((1,), (0,)), ((), ())), preferred_element_type=F32)]
    dot_general x4 -> x2, matrix products: 47 us -> 16.7 us  [dot_nt(): lax.dot_general(a, b, (((1,), (1,)), ((), ())), preferred_element_type=F32)]
    pallas_call x1, Pallas kernels: 206 us -> 225 us  [scatter(): pl.pallas_call(functools.partial(scatter_body, ways), in_specs=[anywhere]...]
    convert_element_type x4 -> x1, other arithmetic: 13.7 us -> 2.64 us  [scatter(): return (out[0].astype(F32), out[1].astype(F32), gwo.astype(F32), smallo)]
    pallas_call x1, Pallas kernels: 45.9 us -> 35.7 us  [attention(): pl.pallas_call(functools.partial(attention_body, 256), grid=(cols // 128,...]
    dot_general x1 -> x2, local copies, waits for them, and re-layouts: 8.69 us -> 17.2 us  [dot_tn(): lax.dot_general(a, b, (((0,), (0,)), ((), ())), preferred_element_type=F32)]
where the time goes in v3:
time: 626 us; the launch traced here: 621 us
  Pallas kernels  476 us (76%)
  local copies, waits for them, and re-layouts  70.5 us (11%)
  matrix products  47.3 us (8%)
  other arithmetic  26.2 us (4%)
    pallas_call x1, Pallas kernels, scatter(): pl.pallas_call(functools.partial(scatter_body, ways), in_specs=[anywhere]...  225 us
    pallas_call x1, Pallas kernels, forward(): pl.pallas_call(functools.partial(forward_body, ways), in_specs=[anywhere]...  216 us
    pallas_call x1, Pallas kernels, attention(): pl.pallas_call(functools.partial(attention_body, 256), grid=(cols // 128,...  35.7 us
    dot_general x4, matrix products, dot_tn(): lax.dot_general(a, b, (((0,), (0,)), ((), ())), preferred_element_type=F32)  30.6 us
    dot_general x2, local copies, waits for them, and re-layouts, dot_tn(): lax.dot_general(a, b, (((0,), (0,)), ((), ())), preferred_element_type=F32)  17.2 us
    dot_general x2, matrix products, dot_nt(): lax.dot_general(a, b, (((1,), (1,)), ((), ())), preferred_element_type=F32)  16.7 us

profile of v3, /device:TPU:0, one launch (start us, length us, event | category | flops | bytes accessed | tf_op | source)
XLA Modules:
  0.0 621.1 jit_solution(16421663293741148058)
XLA Ops:
  11.1 3.2 pad_maximum_fusion.w
  15.0 215.5 %shard_map.212 = (bf16[4,384,2048]{2,1,0:T(8,128)(2,1)}, s32[4,8,384]{2,1,0:T(8,128)}, bf16[4,384,2048]{2,1,0:T(8,128)(2,1)}, bf16[4,384,2048]{2,1,0:T(8,128)(2,...) custom-call(bf16[384,2048]{1,0:T(8,128)(2,1)} %bitcast.125, ...), custom_call_target="tpu_custom_call" | custom-call | tf_op jit(solution)/shard_map/pallas_call | solution.py:531
  231.4 4.3 multiply_sine_fusion
  235.9 3.1 concatenate.38.fr
  238.9 3.9 concatenate.39.fl
  244.6 4.7 fusion.29
  250.5 35.7 %shard_map.213 = (bf16[1536,256]{1,0:T(8,128)(2,1)S(1)}, bf16[1536,256]{1,0:T(8,128)(2,1)S(1)}, bf16[1536,256]{1,0:T(8,128)(2,1)S(1)}, bf16[1536,256]{1,0:T(8,128)(2,1)S(1)}) custom-call(f32[1536,256]{1,0:T(8,128)} %get-tuple-element.117.pq, f32[1536,256]{1,0:T(8,128)} %get-tuple-element.116.pk, f32[1536,256]{1,0:T(8,128)} %get-tuple-element.115.pv, ...), custom_call_target="tpu_custom_call" | custom-call | tf_op jit(solution)/shard_map/pallas_call | solution.py:101
  288.4 11.0 %fusion.28 = (f32[2048]{0:T(1024)S(1)}, f32[2048]{0:T(1024)S(1)}, bf16[1536,2048]{1,0:T(8,128)(2,1)}) fusion(bf16[4,384,2048]{2,1,0:T(8,128)(2,1)} %get-tuple-element.68, bf16[1536,2048]{1,0:T(8,128)(2,1)} %bitcast.167, bf16[1536,768]{1,0:T(8,128)(2,1)S(1)} %constant_dynamic-update-slice_fusion, bf16[2048,1024]{1,0:T(8,128)(2,1)S(1)} %copy-done.7), kind=kOutput, calls=%fused_computation.62 | convolution fusion | flops 4853854208 | bytes 24395776 | tf_op jit(solution)/shard_map/dot_general | solution.py:25
  301.9 8.6 %copy.83 = bf16[2048,1536]{1,0:T(8,128)(2,1)} copy(bf16[2048,1536]{0,1:T(8,128)(2,1)} %bitcast.134) | data formatting | bytes 12582912 | tf_op jit(solution)/shard_map/dot_general | solution.py:29
  310.4 9.2 %convert_bitcast_fusion.1 = bf16[1,4,512,768]{3,2,1,0:T(8,128)(2,1)} fusion(bf16[4,512,1536]{2,1,0:T(8,128)(2,1)} %bitcast.135, bf16[1536,768]{1,0:T(8,128)(2,1)S(1)} %constant_dynamic-update-slice_fusion), kind=kOutput, calls=%fused_computation.33 | convolution fusion | flops 4833411072 | bytes 11796480 | tf_op jit(solution)/shard_map/dot_general | solution.py:29
  319.7 8.6 %copy.84 = bf16[2048,1536]{1,0:T(8,128)(2,1)} copy(bf16[2048,1536]{0,1:T(8,128)(2,1)} %bitcast.131) | data formatting | bytes 12582912 | tf_op jit(solution)/shard_map/dot_general | solution.py:29
  328.3 4.7 fusion.23
  333.0 9.2 %bitcast_convert_fusion.1 = bf16[2048,1024]{1,0:T(8,128)(2,1)S(1)} fusion(bf16[4,384,2048]{2,1,0:T(8,128)(2,1)} %get-tuple-element.64, bf16[4,384,1024]{2,1,0:T(8,128)(2,1)S(1)} %copy-done.18), kind=kOutput, calls=%fused_computation.7 | convolution fusion | flops 6444548096 | bytes 13631488 | tf_op jit(solution)/shard_map/dot_general | solution.py:29
  342.3 7.4 %bitcast_convert_fusion = bf16[2048,1024]{1,0:T(8,128)(2,1)S(1)} fusion(bf16[4,384,2048]{2,1,0:T(8,128)(2,1)S(1)} %bitcast.133, bf16[4,384,1024]{2,1,0:T(8,128)(2,1)S(1)} %copy-done.17), kind=kOutput, calls=%fused_computation.6 | convolution fusion | flops 6444548096 | bytes 13631488 | tf_op jit(solution)/shard_map/dot_general | solution.py:29
  349.7 6.2 maximum_maximum_fusion.gw
  356.0 5.7 fusion.1
  361.6 224.5 %shard_map.214 = (bf16[2,384,2048]{2,1,0:T(8,128)(2,1)}, bf16[3,4,128,1024]{3,2,1,0:T(8,128)(2,1)}, f32[4,8,2048]{2,1,0:T(8,128)}) custom-call(bf16[4,384,2048]{2,1,0:T(8,128)(2,1)} %bitcast.124, bf16[4,384,2048]{2,1,0:T(8,128)(2,1)} %bitcast.137, bf16[3,4,512,1024]{3,2,1,0:T(8,128)(2,1)} %maximum_maximum_fusion.gw, f32[8,2048]{1,0:T(8,128)} %stack.56.small), custom_call_target="tpu_custom_call" | custom-call | tf_op jit(solution)/shard_map/pallas_call | solution.py:841
  586.2 2.6 convert_element_type.129
  588.8 2.6 slice_bitcast_fusion
  595.1 2.9 copy.91
  598.0 2.8 slice.125
  600.8 2.2 reshape_squeeze.9
  606.5 3.0 reshape.313
  615.7 3.3 fusion.14
  (102 shorter events, 34.7 us)
Async XLA Ops:
  0.6 5.8 copy-start.8
  11.1 3.2 copy-start.15
  11.1 3.2 copy-start.16
  11.1 3.3 copy-start.12
  14.4 0.6 copy-start.11
  244.5 5.9 copy-start
  286.2 2.2 copy-start.7
  288.4 11.5 %copy-start.14 = (f32[1,1024]{1,0:T(1,128)S(1)}, f32[1,1024]{1,0:T(1,128)}, u32[]{:S(2)}) copy-start(f32[1,1024]{1,0:T(1,128)} %get-tuple-element.69) | copy-start | bytes 12292
  299.4 1.4 copy-start.2
  328.3 4.7 copy-start.18
  328.3 14.0 %slice-start.2 = ((s8[6291456]{0:T(1024)(128)(4,1)}), s8[4194304]{0:T(1024)(128)(4,1)S(1)}, s32[]{:S(2)}) async-start(s8[6291456]{0:T(1024)(128)(4,1)} %bitcast.132), calls=%async_computation.2 | async-start | bytes 8388608
  333.0 9.2 %slice-start.3 = ((s8[6291456]{0:T(1024)(128)(4,1)}), s8[2097152]{0:T(1024)(128)(4,1)S(1)}, s32[]{:S(2)}) async-start(s8[6291456]{0:T(1024)(128)(4,1)} %bitcast.132), calls=%async_computation.3 | async-start | bytes 4194304
  333.0 9.2 %copy-start.17 = (bf16[4,384,1024]{2,1,0:T(8,128)(2,1)S(1)}, bf16[4,384,1024]{2,1,0:T(8,128)(2,1)}, u32[]{:S(2)}) copy-start(bf16[4,384,1024]{2,1,0:T(8,128)(2,1)} %get-tuple-element.67) | copy-start | bytes 9437188
  342.3 7.4 %copy-start.6 = (bf16[1,4,512,768]{3,2,1,0:T(8,128)(2,1)S(1)}, bf16[1,4,512,768]{3,2,1,0:T(8,128)(2,1)}, u32[]{:S(2)}) copy-start(bf16[1,4,512,768]{3,2,1,0:T(8,128)(2,1)} %convert_bitcast_fusion.1) | copy-start | bytes 9437188
  349.7 6.2 %slice-start = ((s8[6291456]{0:T(1024)(128)(4,1)}), s8[4194304]{0:T(1024)(128)(4,1)S(1)}, s32[]{:S(2)}) async-start(s8[6291456]{0:T(1024)(128)(4,1)} %bitcast.126), calls=%async_computation | async-start | bytes 8388608
  349.7 6.3 %slice-start.1 = ((s8[6291456]{0:T(1024)(128)(4,1)}), s8[2097152]{0:T(1024)(128)(4,1)S(1)}, s32[]{:S(2)}) async-start(s8[6291456]{0:T(1024)(128)(4,1)} %bitcast.126), calls=%async_computation.1 | async-start | bytes 4194304
  603.0 1.3 copy-start.4
  606.5 6.2 %copy-start.1 = (bf16[1,384,2048]{2,1,0:T(8,128)(2,1)S(1)}, bf16[1,384,2048]{2,1,0:T(8,128)(2,1)}, u32[]{:S(2)}) copy-start(bf16[1,384,2048]{2,1,0:T(8,128)(2,1)} %param.17) | copy-start | bytes 4718596
  609.6 4.1 copy-start.9
  612.8 1.9 copy-start.5
  612.8 2.9 copy-start.13
  612.8 2.9 copy-start.3
  615.7 3.3 copy-start.10

commit v4 on v3

--- a/solution.py
+++ b/solution.py
@@ -29,89 +29,30 @@
     return lax.dot_general(a, b, (((0,), (0,)), ((), ())), preferred_element_type=F32)
 
 
-def rotary_tables(places):
+QUERIES = 256
+
+
+def frequencies():
     half = ROT // 2
-    frequency = 10000.0 ** (-(jnp.arange(half, dtype=F32) * 2.0 / ROT))
-    angles = places.astype(F32)[:, None] * frequency[None, :]
-    cos, sin = jnp.cos(angles), jnp.sin(angles)
-    rows = places.shape[0]
-    zero = jnp.zeros((rows, half), F32)
-    rest0 = jnp.zeros((rows, HD - ROT), F32)
-    rest1 = jnp.ones((rows, HD - ROT), F32)
-    keep = jnp.concatenate([cos, cos, rest1] * 2, 1)
-    from_right = jnp.concatenate([-sin, zero, rest0] * 2, 1)
-    from_left = jnp.concatenate([zero, sin, rest0] * 2, 1)
-    return keep, from_right, from_left
-
-
-def turn(v, keep, from_right, from_left):
+    one = jnp.concatenate(
+        [10000.0 ** (-(jnp.arange(half, dtype=F32) * 2.0 / ROT))] * 2 + [jnp.zeros(HD - ROT, F32)]
+    )
+    return jnp.concatenate([one, one])[None, :]
+
+
+def turn(v, cos, sin):
     half = ROT // 2
-    return v * keep + pltpu.roll(v, 128 - half, 1) * from_right + pltpu.roll(v, half, 1) * from_left
-
-
-def attention_body(
-    block_rows, pq, pk, pv, mg, keep, fr, fl, seg_row, seg_col, mix, gq, gk, gv, q, k, v, dq, dk, dv
-):
-    rows = pq.shape[0]
-    scale = 1.0 / math.sqrt(HD)
-    q[...] = (turn(pq[...], keep[...], fr[...], fl[...]).astype(BF16) * scale).astype(BF16)
-    k[...] = turn(pk[...], keep[...], fr[...], fl[...]).astype(BF16)
-    v[...] = pv[...].astype(BF16)
-    dk[...] = jnp.zeros_like(dk)
-    dv[...] = jnp.zeros_like(dv)
-    first = lax.broadcasted_iota(jnp.int32, (block_rows, 128), 1) < HD
-    for i in range(rows // block_rows):
-        here = pl.ds(i * block_rows, block_rows)
-        seen = pl.ds(0, (i + 1) * block_rows)
-        keys, values = k[seen, :], v[seen, :]
-        shape = (block_rows, (i + 1) * block_rows)
-        row_index = lax.broadcasted_iota(jnp.int32, shape, 0) + i * block_rows
-        col_index = lax.broadcasted_iota(jnp.int32, shape, 1)
-        allowed = (col_index <= row_index) & (seg_col[here, :] == seg_row[:, seen])
-        parts = []
-        for sub in range(2):
-            mine = first if sub == 0 else ~first
-            qi = jnp.where(mine, q[here, :], 0)
-            mi = jnp.where(mine, mg[here, :], 0)
-            scores = jnp.where(allowed, dot_nt(qi, keys), -1e30)
-            top = jnp.max(scores, 1, keepdims=True)
-            expo = jnp.exp(scores - top)
-            probs = expo * (1.0 / jnp.sum(expo, 1, keepdims=True))
-            low = probs.astype(BF16)
-            out = dot_nn(low, values)
-            prob_grad = dot_nt(mi, values)
-            delta = jnp.sum(probs * prob_grad, 1, keepdims=True)
-            score_grad = (probs * (prob_grad - delta)).astype(BF16)
-            dqi = dot_nn(score_grad, keys) * scale
-            dk[seen, :] += dot_tn(score_grad, qi)
-            dv[seen, :] += dot_tn(low, mi)
-            parts.append((out, dqi))
-        mix[here, :] = jnp.where(first, parts[0][0], parts[1][0]).astype(BF16)
-        dq[here, :] = jnp.where(first, parts[0][1], parts[1][1])
-    gq[...] = turn(dq[...], keep[...], -fr[...], -fl[...]).astype(BF16)
-    gk[...] = turn(dk[...], keep[...], -fr[...], -fl[...]).astype(BF16)
-    gv[...] = dv[...].astype(BF16)
-
-
-def attention(pq, pk, pv, mg, places, segments):
-    rows, cols = pq.shape
-    keep, fr, fl = rotary_tables(places)
-    pair = pl.BlockSpec((rows, 128), lambda h: (0, h))
-    whole = pl.BlockSpec((rows, 128), lambda h: (0, 0))
-    return pl.pallas_call(
-        functools.partial(attention_body, 256),
-        grid=(cols // 128,),
-        in_specs=[pair] * 4
-        + [whole] * 3
-        + [
-            pl.BlockSpec((1, rows), lambda h: (0, 0)),
-            pl.BlockSpec((rows, 1), lambda h: (0, 0)),
-        ],
-        out_specs=[pair] * 4,
-        out_shape=[jax.ShapeDtypeStruct((rows, cols), BF16)] * 4,
-        scratch_shapes=[pltpu.VMEM((rows, 128), BF16)] * 3 + [pltpu.VMEM((rows, 128), F32)] * 3,
-        compiler_params=pltpu.CompilerParams(vmem_limit_bytes=48 * MIB),
-    )(pq, pk, pv, mg, keep, fr, fl, segments[None, :], segments[:, None])
+    lane = lax.broadcasted_iota(jnp.int32, v.shape, 1) % HD
+    left, right = pltpu.roll(v, 128 - half, 1), pltpu.roll(v, half, 1)
+    return v * cos + jnp.where(lane < half, -left, right) * sin
+
+
+def allowed_keys(labr, labc, i):
+    shape = (QUERIES, (i + 1) * QUERIES)
+    row = lax.broadcasted_iota(jnp.int32, shape, 0) + i * QUERIES
+    col = lax.broadcasted_iota(jnp.int32, shape, 1)
+    here = pl.ds(i * QUERIES, QUERIES)
+    return (col <= row) & (labc[here, 1:2] == labr[1:2, 0 : (i + 1) * QUERIES])
 
 
 def attention_plain(pq, pk, pv, mg, places, segments):
@@ -215,10 +156,10 @@
 
 
 def forward_body(
-    ways, x, g, w, ids, gain, shift, fc1_shift, qkv_shift,
-    go, ido, no, xho, ho, hgo, outo, ngo, pro, mgo, wao, biaso,
-    xo, wv, norm, xb, gb, pre, hid, slope, hgb, ob, nb, pb, mb,
-    zs, zr, ts, tr, ws, wr, ls, lr, ds, dr, ids_s, ids_r, own, ls_in, ls_out,
+    ways, x, g, w, ids, gain, shift, fc1_shift, qkv_shift, freq,
+    go, no, xho, ho, hgo, outo, ngo, mgo, wao, qo, ko, vo, mixo, lseo, coso, sino, ido, biaso,
+    xo, wv, norm, xb, gb, pre, hid, slope, hgb, ob, nb, mb, qb, kb, vb, mixb, lse, cosb, sinb, labr, labc,
+    zs, zr, ts, tr, ws, wr, ls, lr, ds, dr, ids_s, ids_r, own, ls_in, ls_out, keep_out,
 ):
     dp, me, core, dpx, dpy = place_of()
     rows, width = x.shape
@@ -348,7 +289,6 @@
             (ob.at[t % 2], outo.at[o]),
             (nb.at[t % 2], ngo.at[o]),
             (hgb.at[t % 2], hgo.at[o]),
-            (pb.at[t % 2], pro.at[o]),
             (mb.at[t], mgo.at[o]),
         )[which]
         return pltpu.make_async_copy(src, dst, ls_out.at[which, t])
@@ -396,20 +336,67 @@
         loop(rows // 16, act)
         store(2, t).start()
 
+    def tables():
+        for k in range(1, ways):
+            labels(k).wait_recv()
+        keeps[groups + 1].wait()
+        lse[...] = jnp.zeros_like(lse)
+        for o in range(ways):
+            at = slice(o * rows, (o + 1) * rows)
+            rows_here = ido[o].astype(F32)
+            labr[:, at] = rows_here
+            columns = jnp.transpose(rows_here)
+            labc[at, :] = columns
+            angles = columns[:, 0:1] * freq[...]
+            cosb[at, :] = jnp.cos(angles)
+            sinb[at, :] = jnp.sin(angles)
+        for copy in table_stores:
+            copy.start()
+
     def project(t):
-        if t >= 2:
-            store(6, t - 2).wait()
         o = blocks[t]
-        pb[t % 2] = dot_nn(norm[o], wv[2, :, : 3 * head_cols]) + qkv_shift[...]
-        store(6, t).start()
+        at = pl.ds(pl.multiple_of(o * rows, 16), rows)
+        cos, sin = cosb[at, :], sinb[at, :]
+        for pair in range(head_cols // 128):
+            lanes = pl.ds(pair * 128, 128)
+            for which, ref in enumerate((qb, kb, vb)):
+                wide_lanes = pl.ds(which * head_cols + pair * 128, 128)
+                v = dot_nn(norm[o], wv[2, :, wide_lanes]) + qkv_shift[:, wide_lanes]
+                if which < 2:
+                    v = turn(v, cos, sin)
+                v = v.astype(BF16)
+                ref[at, lanes] = v * BF16(1.0 / math.sqrt(HD)) if which == 0 else v
+
+    def attend(pair, i):
+        lanes = pl.ds(pair * 128, 128)
+        here, seen = pl.ds(i * QUERIES, QUERIES), pl.ds(0, (i + 1) * QUERIES)
+        allowed = allowed_keys(labr, labc, i)
+        first = lax.broadcasted_iota(jnp.int32, (QUERIES, 128), 1) < HD
+        lane = lax.broadcasted_iota(jnp.int32, (QUERIES, 128), 1)
+        keys, values = kb[seen, lanes], vb[seen, lanes]
+        outs_of, logs = [], lse[here, :]
+        for sub in range(2):
+            mine = first if sub == 0 else ~first
+            scores = dot_nt(jnp.where(mine, qb[here, lanes], 0), keys)
+            scores = jnp.where(allowed, scores, -1e30)
+            top = jnp.max(scores, 1, keepdims=True)
+            expo = jnp.exp(scores - top)
+            total = jnp.sum(expo, 1, keepdims=True)
+            outs_of.append(dot_nn((expo * (1.0 / total)).astype(BF16), values))
+            logs = jnp.where(lane == pair * 2 + sub, top + jnp.log(total), logs)
+        lse[here, :] = logs
+        mixb[here, lanes] = jnp.where(first, outs_of[0], outs_of[1]).astype(BF16)
 
     def down(t):
         if t >= 2:
             store(3, t - 2).wait()
         o = blocks[t]
+        at = pl.ds(pl.multiple_of(o * rows, 16), rows)
 
         def mul(i):
-            ob[t % 2, :, span(i)] = dot_nt(hid[o], wv[1, span(i), :]).astype(BF16)
+            total = dot_nt(hid[o], wv[1, span(i), :])
+            total = total + dot_nt(mixb[at, :], wv[2, span(i), 3 * head_cols :])
+            ob[t % 2, :, span(i)] = total.astype(BF16)
 
         loop(width // wide, mul)
         store(3, t).start()
@@ -439,7 +426,7 @@
         loop(width // wide, mul_back)
         store(4, t).start()
         mb[t] = dot_nn(gb[t % 2], wv[2, :, 3 * head_cols :]).astype(BF16)
-        store(7, t).start()
+        store(6, t).start()
 
     greet(ways)
     send_own(0)
@@ -457,40 +444,52 @@
     for copy in keeps:
         copy.start()
     wa_out = pltpu.make_async_copy(wv.at[2], wao, own.at[groups + 2])
+    stores = [
+        pltpu.make_async_copy(src, dst, keep_out.at[i])
+        for i, (src, dst) in enumerate(
+            ((cosb, coso), (sinb, sino), (qb, qo), (kb, ko), (vb, vo), (mixb, mixo), (lse, lseo))
+        )
+    ]
+    table_stores, state_stores = stores[:2], stores[2:]
     steps = dict(
         S=send_shares,
         G=lambda: send_own(1),
         W=wa_out.start,
+        Z=lambda: [copy.start() for copy in state_stores],
         x=lambda k: pass_on(0, k),
         g=lambda k: pass_on(1, k),
         s=spread_on,
         c=corner_on,
         e=settle,
+        l=tables,
         n=normalise,
         u=up,
         p=project,
+        a=attend,
         d=down,
         b=back,
     )
     plan = (
         "n0", "s01", "c00", "x1", "S2", "n1", "s02", "c01", "s03", "c02", "x2", "G", "n2", "c03",
-        "s11", "c10", "s12", "c11", "s13", "c12", "x3", "n3", "e0", "u0", "c13", "s21", "c20",
-        "u1", "s22", "c21", "g1", "u2", "s23", "c22", "u3", "c23", "e1", "d0", "d1", "g2", "e2",
-        "W", "p0", "b0", "p1", "b1", "d2", "p2", "g3", "b2", "d3", "p3", "b3",
+        "l", "s11", "c10", "s12", "c11", "s13", "c12", "x3", "n3", "e0", "u0", "c13", "s21", "c20",
+        "u1", "s22", "c21", "u2", "g1", "s23", "c22", "u3", "c23", "e2", "W", "p0", "p1", "p2",
+        "p3", "a00", "a01", "a02", "a03", "g2", "a04", "a05", "a10", "a11", "a12", "a13", "a14",
+        "a15", "Z", "e1", "d0", "b0", "d1", "b1", "g3", "d2", "d3", "b2", "b3",
     )
     for word in plan:
         steps[word[0]](*(int(digit) for digit in word[1:]))
-    for copy in keeps[groups:]:
+    keeps[groups].wait()
+
+    for k in range(1, ways):
+        labels(k).wait_send()
+    for copy in table_stores + state_stores:
         copy.wait()
-
-    for k in range(1, ways):
-        labels(k).wait()
     wa_out.wait()
     for t in range(4):
-        for which in (1, 2, 7):
+        for which in (1, 2, 6):
             store(which, t).wait()
         if t >= 2:
-            for which in (0, 3, 4, 5, 6):
+            for which in (0, 3, 4, 5):
                 store(which, t).wait()
     for a in range(2):
         for owner in range(ways):
@@ -517,33 +516,40 @@
             corner(grp, k).wait_send()
 
 
-def forward(x, g, wsrc, places, segments, gain, shift, fc1_shift, qkv_shift):
+def forward(x, g, wsrc, ids, gain, shift, fc1_shift, qkv_shift):
     ways = lax.axis_size("ctx")
     rows, width = x.shape
     groups, unused, depth, cols = wsrc.shape
     head_cols = cols // 4
-    ids = jnp.zeros((8, rows), jnp.int32).at[0].set(places).at[1].set(segments)
     dma = pltpu.SemaphoreType.DMA
     vmem = pltpu.VMEM
     anywhere = pl.BlockSpec(memory_space=pl.ANY)
     inside = pl.BlockSpec(memory_space=pltpu.VMEM)
     seq = lambda n, dtype=BF16: jax.ShapeDtypeStruct((ways, rows, n), dtype)
+    tokens = ways * rows
+    line = lambda n, dtype: jax.ShapeDtypeStruct((tokens, n), dtype)
     outs = pl.pallas_call(
         functools.partial(forward_body, ways),
-        in_specs=[anywhere] * 4 + [inside] * 4,
-        out_specs=[anywhere] * 11 + [inside, anywhere],
+        in_specs=[anywhere] * 4 + [inside] * 5,
+        out_specs=[anywhere] * 16 + [inside] * 2 + [anywhere],
         out_shape=[
             seq(width),
-            jax.ShapeDtypeStruct((ways, 8, rows), jnp.int32),
             seq(width),
             seq(width),
             seq(cols),
             seq(cols),
             seq(width),
             seq(width),
-            seq(3 * head_cols, F32),
             seq(head_cols),
             jax.ShapeDtypeStruct((width, cols), BF16),
+            line(head_cols, BF16),
+            line(head_cols, BF16),
+            line(head_cols, BF16),
+            line(head_cols, BF16),
+            line(128, F32),
+            line(128, F32),
+            line(128, F32),
+            jax.ShapeDtypeStruct((ways, 8, rows), jnp.int32),
             jax.ShapeDtypeStruct((1, cols), F32),
             seq(width),
         ],
@@ -558,8 +564,16 @@
             vmem((2, rows, cols), BF16),
             vmem((2, rows, width), BF16),
             vmem((2, rows, width), BF16),
-            vmem((2, rows, 3 * head_cols), F32),
             vmem((ways, rows, head_cols), BF16),
+            vmem((tokens, head_cols), BF16),
+            vmem((tokens, head_cols), BF16),
+            vmem((tokens, head_cols), BF16),
+            vmem((tokens, head_cols), BF16),
+            vmem((tokens, 128), F32),
+            vmem((tokens, 128), F32),
+            vmem((tokens, 128), F32),
+            vmem((8, tokens), F32),
+            vmem((tokens, 8), F32),
             dma((2, 2, ways, PIECES)),
             dma((2, ways, PIECES)),
             dma((2, ways, PIECES)),
@@ -574,135 +588,346 @@
             dma((ways,)),
             dma((3 + groups,)),
             dma((2, ways)),
-            dma((8, ways)),
+            dma((7, ways)),
+            dma((7,)),
         ],
         compiler_params=pltpu.CompilerParams(
-            collective_id=0, has_side_effects=True, vmem_limit_bytes=60 * MIB
+            collective_id=0, has_side_effects=True, vmem_limit_bytes=62 * MIB
         ),
     )(
         x, g, wsrc, ids,
         gain.reshape(1, width), shift.reshape(1, width), fc1_shift.reshape(1, cols),
-        qkv_shift.reshape(1, 3 * head_cols),
+        qkv_shift.reshape(1, 3 * head_cols), frequencies(),
     )
     return outs
 
 
-def scatter_body(
-    ways, p0, p1, gw, small, out, gwo, smallo,
-    acc, tin, lin, rin, gown, first_in, second_in,
-    tps, tpr, zs, zr, fs, fr, ss, sr, ws, wr, os, orr, loc, gloc,
-    sum_in, sum_out, sms, smr,
+def backward_body(
+    ways,
+    p0, ngm, normed, xh, g, hg, hidden, q, k, v, mg, mix, lse, cos, sin, wa, labels, small,
+    out, gwo, tin, smallo,
+    lt, ra, rb, wp, qv, kv, vv, mgv, lsev, cosv, sinv, dkv, dvv, labr, labc,
+    acc, zin, tst, ngi, xhi, ngs, gown, gsend, first_in, second_in, sums, sum_in, sum_out,
+    tps, tpr, zs, zr, fs, fr, ss, sr, ws, wr, os, orr, loc, tloc, sms, smr, ins, lts, ngl,
 ):
     dp, me, core, dpx, dpy = place_of()
     rows, width = out.shape[1:]
     half = rows // 2
     piece = half // PIECES
-    groups = gw.shape[0]
-    span = gw.shape[2]
-    lanes = gw.shape[3] // 2
-    depth = span // ways
-    parts = (p0, p1)
+    groups = first_in.shape[0]
+    span_rows = gown.shape[3]
+    lanes = gown.shape[4]
+    depth = span_rows // ways
+    head_cols = q.shape[1]
     nxt = (dpx, dpy)
     far = dpx + dpy - dp
+    scale = 1.0 / math.sqrt(HD)
+
+    order = (0, 3, 1, 2)
 
     def part(which, s):
         return pl.ds(pl.multiple_of(which * half + s * piece, 16), piece)
 
+    def loop(count, body):
+        lax.fori_loop(0, count, lambda i, c: (body(i), c)[1], 0)
+
+    def add(dst, src, height):
+        step = 32
+
+        def body(i):
+            at = pl.ds(pl.multiple_of(i * step, step), step)
+            dst[at, :] = dst[at, :] + src[at, :]
+
+        loop(height // step, body)
+
     def swap(a, d, s):
+        at = pl.ds(s * piece, piece)
+        src = p0.at[d, part(1 - core, s), :] if a == 0 else ngs.at[order.index(d) % 2, at, :]
         return remote(
-            parts[a].at[d, part(1 - core, s), :],
-            tin.at[a, d, s],
-            tps.at[a, d, s],
-            tpr.at[a, d, s],
-            (dp, me, 1 - core),
+            src, tin.at[a, d, s], tps.at[a, d, s], tpr.at[a, d, s], (dp, me, 1 - core)
         )
 
-    def load(a, d, s):
-        return pltpu.make_async_copy(parts[a].at[d, part(core, s), :], acc.at[a, d, s], loc.at[a, d, s])
+    def load(d, s):
+        return pltpu.make_async_copy(p0.at[d, part(core, s), :], acc.at[0, d, s], loc.at[d, s])
+
+    def load_swapped(a, d, s):
+        return pltpu.make_async_copy(tin.at[a, d, s], tst.at[s], tloc.at[a, d, s])
+
+    def slot(d, side):
+        if side:
+            return d
+        here = 1 - jnp.minimum(jnp.abs(me - 1 - d), 1)
+        return d + here * (ways - d)
+
+    def came(d, side):
+        if side:
+            return d
+        here = 1 - jnp.minimum(jnp.abs(me - d), 1)
+        return d + here * (ways - d)
 
     def stream(a, d, s, side):
         return remote(
             acc.at[a, d, s],
-            (rin, lin)[side].at[a, d, s],
-            zs.at[side, a, d, s],
-            zr.at[side, a, d, s],
+            zin.at[a, slot(d, side), s],
+            zs.at[a, d, s],
+            zr.at[a, slot(d, side), s],
             (dp, me - 1 + 2 * side, core),
         )
 
-    def finish(a, s):
-        ref = out.at[a, part(core, s), :]
-        return remote(ref, ref, os.at[a, s], orr.at[a, s], (dp, me, 1 - core))
-
-    def quarter(path, which):
-        return ((nxt[path], far), (nxt[1 - path], dp))[which]
+    def arrived(a, d, s, side):
+        ref = zin.at[a, came(d, side), s]
+        return remote(
+            ref, ref, zs.at[a, d, s], zr.at[a, came(d, side), s], (dp, me - 1 + 2 * side, core)
+        )
+
+    def finish(a, s, which):
+        ref = out.at[a, part(which, s), :]
+        return remote(acc.at[a, me, s], ref, os.at[0, a, s], orr.at[a, s], (dp, me, 1 - core))
+
+    def finish_here(a, s):
+        return pltpu.make_async_copy(acc.at[a, me, s], out.at[a, part(core, s), :], os.at[1, a, s])
+
+    def merge(a, d):
+        for s in range(PIECES):
+            swap(a, d, s).wait_recv()
+            load_swapped(a, d, s).start()
+        for s in range(PIECES):
+            load_swapped(a, d, s).wait()
+            if a == 0:
+                load(d, s).wait()
+            add(acc.at[a, d, s], tst.at[s], piece)
+            pl.when((me == 0) & (d > 0))(lambda: stream(a, d, s, 1).start())
+            pl.when((me == ways - 1) & (d < ways - 1))(lambda: stream(a, d, s, 0).start())
+
+    def hop(a, far_by, j):
+        for s in range(PIECES):
+            d = ways - 1 - j
+
+            @pl.when(me == far_by)
+            def _():
+                arrived(a, d, s, 1).wait_recv()
+                add(acc.at[a, d, s], zin.at[a, came(d, 1), s], piece)
+                if d > far_by:
+                    stream(a, d, s, 1).start()
+
+            @pl.when(me == ways - 1 - far_by)
+            def _():
+                arrived(a, j, s, 0).wait_recv()
+                add(acc.at[a, j, s], zin.at[a, came(j, 0), s], piece)
+                if j < ways - 1 - far_by:
+                    stream(a, j, s, 0).start()
+
+    def last(a):
+        for s in range(PIECES):
+            finish(a, s, core).start()
+            finish_here(a, s).start()
 
     def lanes_of(path):
         return pl.ds(path * lanes, lanes)
 
     def first(grp, path, i):
-        q = quarter(path, 0)[1 - i]
         return remote(
-            gw.at[grp, q, :, lanes_of(path)],
+            gsend.at[2 * i + path],
             first_in.at[grp, path, i],
             fs.at[grp, path, i],
             fr.at[grp, path, i],
             (nxt[path], me, core),
         )
 
-    def gload(grp, path, i):
-        q = quarter(path, 1)[i]
-        return pltpu.make_async_copy(
-            gw.at[grp, q, :, lanes_of(path)], gown.at[grp, path, i], gloc.at[grp, path, i]
-        )
-
     def second(grp, path):
         return remote(
-            gown.at[grp, path, 0],
+            gown.at[grp % 2, path, 0],
             second_in.at[grp, path],
             ss.at[grp, path],
             sr.at[grp, path],
             (nxt[1 - path], me, core),
         )
 
-    def share(grp, path, k):
-        d = (me + k) % ways
+    def share(grp, path, i):
+        d = (me + i) % ways
         return remote(
-            gown.at[grp, path, 1, pl.ds(pl.multiple_of(d * depth, 16), depth), :],
+            gown.at[grp % 2, path, 1, pl.ds(pl.multiple_of(d * depth, 16), depth), :],
             gwo.at[grp, me, :, lanes_of(path)],
-            ws.at[grp, path, k],
-            wr.at[grp, path, k],
+            ws.at[grp, path, i],
+            wr.at[grp, path, i],
             (dp, d, core),
         )
 
     def keep(grp, path):
         return pltpu.make_async_copy(
-            gown.at[grp, path, 1, pl.ds(pl.multiple_of(me * depth, 16), depth), :],
+            gown.at[grp % 2, path, 1, pl.ds(pl.multiple_of(me * depth, 16), depth), :],
             gwo.at[grp, me, :, lanes_of(path)],
             ws.at[grp, path, 0],
         )
 
-    def add(dst, src, height):
-        step = 32
-
-        def body(i, carry):
-            at = pl.ds(pl.multiple_of(i * step, step), step)
-            dst[at, :] = dst[at, :] + src[at, :]
-            return carry
-
-        lax.fori_loop(0, height // step, body, 0)
+    quarters = (far, dpx, dpy, dp)
+
+    def load_left(grp, r, which=0):
+        at = pl.ds(pl.multiple_of(quarters[r] * span_rows, 128), span_rows)
+        src = (normed, g, normed)[grp] if which == 0 else g
+        into = (4 * grp + r) % 2 if grp < 2 else which
+        return pltpu.make_async_copy(src.at[:, at], lt.at[into], lts.at[grp, r, which])
+
+    def products(grp, r):
+        load_left(grp, r).wait()
+        if grp == 2:
+            load_left(grp, r, 1).wait()
+        elif 4 * grp + r < 7:
+            after = 4 * grp + r + 1
+            load_left(after // 4, after % 4).start()
+        left = (4 * grp + r) % 2 if grp < 2 else 0
+        for path in range(2):
+            if r == 0:
+                dst = gsend.at[path]
+                i = 0
+            elif r == 1 + path:
+                dst = gsend.at[2 + path]
+                i = 1
+            else:
+                dst = gown.at[grp % 2, path, 1 if r == 3 else 0]
+                i = None
+            if i is not None and grp:
+                first(grp - 1, path, i).wait_send()
+            if i is None and grp == 2:
+                if r == 3:
+                    keep(0, path).wait()
+                    for n in range(1, ways):
+                        share(0, path, n).wait_send()
+                else:
+                    second(0, path).wait_send()
+            right = (ra, rb, ra)[grp]
+            if grp == 2 and path == 1:
+                dst[:, :head_cols] = dot_tn(lt[0], right[:, 2 * head_cols : 3 * head_cols]).astype(BF16)
+                dst[:, head_cols:] = dot_tn(lt[1], right[:, 3 * head_cols :]).astype(BF16)
+            else:
+                dst[...] = dot_tn(lt[left], right[:, lanes_of(path)]).astype(BF16)
+            if i is not None:
+                first(grp, path, i).start()
+        if grp == 2 and r < 3:
+            load_left(grp, r + 1).start()
+            load_left(grp, r + 1, 1).start()
+
+    def first_sum(grp, path):
+        first(grp, path, 0).wait_recv()
+        add(gown.at[grp % 2, path, 0], first_in.at[grp, path, 0], span_rows)
+        second(grp, path).start()
+        first(grp, path, 1).wait_recv()
+        add(gown.at[grp % 2, path, 1], first_in.at[grp, path, 1], span_rows)
+
+    def second_sum(grp, path):
+        second(grp, path).wait_recv()
+        add(gown.at[grp % 2, path, 1], second_in.at[grp, path], span_rows)
+        for i in range(1, ways):
+            share(grp, path, i).start()
+        keep(grp, path).start()
+
+    pairs = (
+        (hg, ra), (hidden, rb), (wa.at[:, pl.ds(0, 3 * head_cols)], wp),
+        (q, qv), (k, kv), (v, vv), (mg, mgv), (lse, lsev), (cos, cosv), (sin, sinv),
+    )
+
+    def copy_in(i):
+        return pltpu.make_async_copy(*pairs[i], ins.at[i])
+
+    mix_in = pltpu.make_async_copy(mix, ra.at[:, pl.ds(3 * head_cols, head_cols)], ins.at[10])
+
+    def begin():
+        for i in range(3, 10):
+            copy_in(i).wait()
+        mix_in.start()
+        for o in range(ways):
+            at = slice(o * rows, (o + 1) * rows)
+            rows_here = labels[o].astype(F32)
+            labr[:, at] = rows_here
+            labc[at, :] = jnp.transpose(rows_here)
+
+    def turned_back(value, at):
+        return turn(value, cosv[at, :], -sinv[at, :]).astype(BF16)
+
+    def attend_back(pair, i):
+        at = pl.ds(pair * 128, 128)
+        here, seen = pl.ds(i * QUERIES, QUERIES), pl.ds(0, (i + 1) * QUERIES)
+        allowed = allowed_keys(labr, labc, i)
+        head = lax.broadcasted_iota(jnp.int32, (QUERIES, 128), 1) < HD
+        if i == 0:
+            dkv[...] = jnp.zeros_like(dkv)
+            dvv[...] = jnp.zeros_like(dvv)
+        keys, values = kv[seen, at], vv[seen, at]
+        parts = []
+        for sub in range(2):
+            mine = head if sub == 0 else ~head
+            qi = jnp.where(mine, qv[here, at], 0)
+            mi = jnp.where(mine, mgv[here, at], 0)
+            log = lsev[here, pair * 2 + sub : pair * 2 + sub + 1]
+            probs = jnp.where(allowed, jnp.exp(dot_nt(qi, keys) - log), 0.0)
+            prob_grad = dot_nt(mi, values)
+            delta = jnp.sum(probs * prob_grad, 1, keepdims=True)
+            score_grad = (probs * (prob_grad - delta)).astype(BF16)
+            parts.append(dot_nn(score_grad, keys))
+            dkv[seen, :] += dot_tn(score_grad, qi)
+            dvv[seen, :] += dot_tn(probs.astype(BF16), mi)
+        ra[here, at] = turned_back(jnp.where(head, parts[0], parts[1]) * scale, here)
+        if i == rows * ways // QUERIES - 1:
+            ra[:, pl.ds(head_cols + pair * 128, 128)] = turned_back(dkv[...], slice(None))
+            ra[:, pl.ds(2 * head_cols + pair * 128, 128)] = dvv[...].astype(BF16)
+
+    def load_back(d, own):
+        at = pl.ds(pl.multiple_of((core if own else 1 - core) * half, 16), half)
+        return [
+            pltpu.make_async_copy(ngm.at[d, at, :], ngi.at[own], ngl.at[0, d, own]),
+            pltpu.make_async_copy(xh.at[d, at, :], xhi.at[own], ngl.at[1, d, own]),
+        ]
+
+    def normed_back(n):
+        d = order[n]
+        if n == 0:
+            copy_in(2).wait()
+            sums[...] = small[...]
+        if n >= 2:
+            for s in range(PIECES):
+                swap(1, order[n - 2], s).wait_send()
+        wide = 512
+        for own in range(2):
+            for copy in load_back(d, own):
+                copy.wait()
+            at = pl.ds(pl.multiple_of(d * rows + (core if own else 1 - core) * half, 16), half)
+
+            def mul(i):
+                cols = pl.ds(pl.multiple_of(i * wide, wide), wide)
+                tile = dot_nt(ra[at, : 3 * head_cols], wp[cols, :]) + ngi[own, :, cols].astype(F32)
+                sums[0:1, cols] += jnp.sum(tile * xhi[own, :, cols].astype(F32), 0, keepdims=True)
+                sums[1:2, cols] += jnp.sum(tile, 0, keepdims=True)
+                tile = tile.astype(BF16)
+                for s in range(PIECES):
+                    if own:
+                        acc[1, d, s, :, cols] = tile[s * piece : (s + 1) * piece]
+                    else:
+                        ngs[n % 2, s * piece : (s + 1) * piece, cols] = tile[s * piece : (s + 1) * piece]
+
+            loop(width // wide, mul)
+            if not own:
+                for s in range(PIECES):
+                    swap(1, d, s).start()
+            if n < ways - 1:
+                for copy in load_back(order[n + 1], own):
+                    copy.start()
 
     def small_send(i):
-        src = small if i == 0 else sum_out.at[i - 1]
+        src = sums if i == 0 else sum_out.at[i - 1]
         device = ((dp, me, 1 - core), (dpx, me, core), (dpy, me, core))[i]
         return remote(src, sum_in.at[i], sms.at[i], smr.at[i], device)
 
-    def small_all(k):
-        device = (dp, (me + k) % ways, core)
-        return remote(sum_out.at[2], smallo.at[me], sms.at[2 + k], smr.at[2 + k], device)
+    def small_all(i):
+        device = (dp, (me + i) % ways, core)
+        return remote(sum_out.at[2], smallo.at[me], sms.at[2 + i], smr.at[2 + i], device)
+
+    def small_begin():
+        sums[4:5, : 3 * head_cols] = jnp.sum(ra[:, : 3 * head_cols].astype(F32), 0, keepdims=True)
+        small_send(0).start()
 
     def small_step(i):
         small_send(i).wait_recv()
-        before = small[...] if i == 0 else sum_out[i - 1]
+        before = sums[...] if i == 0 else sum_out[i - 1]
         after = before + sum_in[i]
         if i == 0:
             row = lax.broadcasted_iota(jnp.int32, after.shape, 0)
@@ -711,177 +936,161 @@
         if i < 2:
             small_send(i + 1).start()
         else:
-            for k in range(1, ways):
-                small_all(k).start()
+            for n in range(1, ways):
+                small_all(n).start()
             smallo[me] = after
 
     greet(ways)
-    small_send(0).start()
-    order = [0, 3, 1, 2] if ways == 4 else list(range(ways))
-    for a in range(2):
-        for d in order:
-            for s in range(PIECES):
-                swap(a, d, s).start()
-                load(a, d, s).start()
-    for grp in range(groups):
-        for i in range(2):
-            for path in range(2):
-                first(grp, path, i).start()
-                gload(grp, path, i).start()
-
-    def merge(a):
-        for d in order:
-            for s in range(PIECES):
-                swap(a, d, s).wait_recv()
-                load(a, d, s).wait()
-                add(acc.at[a, d, s], tin.at[a, d, s], piece)
-                pl.when((me == 0) & (d > 0))(lambda: stream(a, d, s, 1).start())
-                pl.when((me == ways - 1) & (d < ways - 1))(lambda: stream(a, d, s, 0).start())
-
-    def hop(a, k):
+    for d in order:
         for s in range(PIECES):
-            for d in range(ways - 1, -1, -1):
-
-                @pl.when((me == k) & (d >= me))
-                def _():
-                    stream(a, d, s, 1).wait_recv()
-                    add(acc.at[a, d, s], lin.at[a, d, s], piece)
-                    pl.when(d > me)(lambda: stream(a, d, s, 1).start())
-
-            for d in range(ways):
-
-                @pl.when((me == ways - 1 - k) & (d <= me))
-                def _():
-                    stream(a, d, s, 0).wait_recv()
-                    add(acc.at[a, d, s], rin.at[a, d, s], piece)
-                    pl.when(d < me)(lambda: stream(a, d, s, 0).start())
-
-    def grads_first(grp):
-        for path in range(2):
-            first(grp, path, 0).wait_recv()
-            gload(grp, path, 0).wait()
-            add(gown.at[grp, path, 0], first_in.at[grp, path, 0], span)
-            second(grp, path).start()
-            first(grp, path, 1).wait_recv()
-            gload(grp, path, 1).wait()
-            add(gown.at[grp, path, 1], first_in.at[grp, path, 1], span)
-
-    def grads_second(grp):
-        for path in range(2):
-            second(grp, path).wait_recv()
-            add(gown.at[grp, path, 1], second_in.at[grp, path], span)
-            for k in range(1, ways):
-                share(grp, path, k).start()
-            keep(grp, path).start()
-
-    def last(a):
-        for s in range(PIECES):
-            out[a, part(core, s), :] = acc[a, me, s]
-            finish(a, s).start()
-
-    merge(0)
-    small_step(0)
-    merge(1)
-    small_step(1)
-    for k in range(1, ways):
-        hop(0, k)
-        if k == 1:
-            small_step(2)
-        if k - 1 < groups:
-            grads_first(k - 1)
-        hop(1, k)
-        if 0 <= k - 2 < groups:
-            grads_second(k - 2)
-    last(0)
-    last(1)
-    grads_second(groups - 1)
+            swap(0, d, s).start()
+            load(d, s).start()
+    load_left(0, 0).start()
+    for i in range(len(pairs)):
+        copy_in(i).start()
+    for own in range(2):
+        for copy in load_back(order[0], own):
+            copy.start()
+    copy_in(0).wait()
+    copy_in(1).wait()
+
+    def last_left():
+        mix_in.wait()
+        load_left(2, 0).start()
+        load_left(2, 0, 1).start()
+
+    steps = dict(
+        t=products,
+        f=first_sum,
+        h=second_sum,
+        m=merge,
+        z=hop,
+        o=last,
+        B=begin,
+        a=attend_back,
+        L=last_left,
+        n=normed_back,
+        Y=small_begin,
+        y=small_step,
+    )
+    plan = (
+        "t00", "m00", "m03", "m01", "m02", "t01", "t02", "t03", "t10", "z010", "t11", "t12", "t13",
+        "B", "f00", "f01", "z011", "z020", "a00", "a01", "a02", "h00", "h01", "a03", "z012",
+        "z021", "a04", "z030", "a05", "o0", "f10", "f11", "a10", "a11", "h10", "h11", "a12", "a13",
+        "a14", "a15", "L", "n0", "n1", "m10", "m13", "n2", "n3", "m11", "m12", "Y", "t20", "y0",
+        "t21", "y1", "z110", "t22", "y2", "t23", "z111", "z120", "f20", "f21", "h20", "h21",
+        "z112", "z121", "z130", "o1",
+    )
+    for word in plan:
+        steps[word[0]](*(int(digit) for digit in word[1:]))
 
     for i in range(3):
         small_send(i).wait_send()
-    for k in range(1, ways):
-        small_all(k).wait()
+    for i in range(1, ways):
+        small_all(i).wait()
     for a in range(2):
         for s in range(PIECES):
-            finish(a, s).wait_send()
-            remote(
-                out.at[a, part(1 - core, s), :],
-                out.at[a, part(1 - core, s), :],
-                os.at[a, s],
-                orr.at[a, s],
-                (dp, me, 1 - core),
-            ).wait_recv()
-            for d in range(ways):
-                swap(a, d, s).wait_send()
+            finish(a, s, core).wait_send()
+            finish_here(a, s).wait()
+            finish(a, s, 1 - core).wait_recv()
+            for n, d in enumerate(order):
+                if a == 0 or n >= 2:
+                    swap(a, d, s).wait_send()
                 pl.when(d > me)(lambda: stream(a, d, s, 1).wait_send())
                 pl.when(d < me)(lambda: stream(a, d, s, 0).wait_send())
     for grp in range(groups):
         for path in range(2):
-            for i in range(2):
-                first(grp, path, i).wait_send()
-            second(grp, path).wait_send()
-            keep(grp, path).wait()
-            for k in range(1, ways):
-                share(grp, path, k).wait()
-
-
-def scatter(out_part, normed_part, weight_part, small):
-    ways = lax.axis_size("ctx")
+            if grp == 2:
+                for i in range(2):
+                    first(grp, path, i).wait_send()
+            if grp:
+                second(grp, path).wait_send()
+                keep(grp, path).wait()
+            for i in range(1, ways):
+                share(grp, path, i).wait_recv()
+                if grp:
+                    share(grp, path, i).wait_send()
+
+
+def backward(p0, ngm, normed, xh, g, hg, hidden, q, k, v, mg, mix, lse, cos, sin, wa, labels, small):
+    ways, rows, width = p0.shape
     chips = lax.axis_size("dp")
-    width = out_part.shape[1]
-    rows = out_part.shape[0] // ways
-    groups, cols = weight_part.shape[0], weight_part.shape[-1]
+    tokens = ways * rows
+    groups, cols, head_cols = 3, hg.shape[-1], q.shape[-1]
     span = width // chips
-    depth = span // ways
+    lanes = cols // 2
     piece = rows // 2 // PIECES
-    lanes = cols // 2
+    half = rows // 2
     dma = pltpu.SemaphoreType.DMA
+    vmem = pltpu.VMEM
     anywhere = pl.BlockSpec(memory_space=pl.ANY)
     inside = pl.BlockSpec(memory_space=pltpu.VMEM)
-    stack = pltpu.VMEM((2, ways, PIECES, piece, width), BF16)
-    out, gwo, smallo = pl.pallas_call(
-        functools.partial(scatter_body, ways),
-        in_specs=[anywhere] * 3 + [inside],
-        out_specs=[inside, anywhere, inside],
+    flat = lambda t: t.reshape(tokens, t.shape[-1])
+    out, gwo, unused, smallo = pl.pallas_call(
+        functools.partial(backward_body, ways),
+        in_specs=[anywhere] * 16 + [inside] * 2,
+        out_specs=[anywhere] * 3 + [inside],
         out_shape=[
             jax.ShapeDtypeStruct((2, rows, width), BF16),
-            jax.ShapeDtypeStruct((groups, ways, depth, cols), BF16),
+            jax.ShapeDtypeStruct((groups, ways, span // ways, cols), BF16),
+            jax.ShapeDtypeStruct((2, ways, PIECES, piece, width), BF16),
             jax.ShapeDtypeStruct((ways,) + small.shape, F32),
         ],
         scratch_shapes=[
-            stack,
-            stack,
-            stack,
-            stack,
-            pltpu.VMEM((groups, 2, 2, span, lanes), BF16),
-            pltpu.VMEM((groups, 2, 2, span, lanes), BF16),
-            pltpu.VMEM((groups, 2, span, lanes), BF16),
+            vmem((2, tokens, span), BF16),
+            vmem((tokens, cols), BF16),
+            vmem((tokens, cols), BF16),
+            vmem((width, 3 * head_cols), BF16),
+            vmem((tokens, head_cols), BF16),
+            vmem((tokens, head_cols), BF16),
+            vmem((tokens, head_cols), BF16),
+            vmem((tokens, head_cols), BF16),
+            vmem((tokens, 128), F32),
+            vmem((tokens, 128), F32),
+            vmem((tokens, 128), F32),
+            vmem((tokens, 128), F32),
+            vmem((tokens, 128), F32),
+            vmem((8, tokens), F32),
+            vmem((tokens, 8), F32),
+            vmem((2, ways, PIECES, piece, width), BF16),
+            vmem((2, ways + 1, PIECES, piece, width), BF16),
+            vmem((PIECES, piece, width), BF16),
+            vmem((2, half, width), BF16),
+            vmem((2, half, width), BF16),
+            vmem((2, half, width), BF16),
+            vmem((2, 2, 2, span, lanes), BF16),
+            vmem((4, span, lanes), BF16),
+            vmem((groups, 2, 2, span, lanes), BF16),
+            vmem((groups, 2, span, lanes), BF16),
+            vmem(small.shape, F32),
+            vmem((3,) + small.shape, F32),
+            vmem((3,) + small.shape, F32),
             dma((2, ways, PIECES)),
             dma((2, ways, PIECES)),
-            dma((2, 2, ways, PIECES)),
-            dma((2, 2, ways, PIECES)),
+            dma((2, ways, PIECES)),
+            dma((2, ways + 1, PIECES)),
             dma((groups, 2, 2)),
             dma((groups, 2, 2)),
             dma((groups, 2)),
             dma((groups, 2)),
             dma((groups, 2, ways)),
             dma((groups, 2, ways)),
+            dma((2, 2, PIECES)),
             dma((2, PIECES)),
-            dma((2, PIECES)),
+            dma((ways, PIECES)),
             dma((2, ways, PIECES)),
-            dma((groups, 2, 2)),
-            pltpu.VMEM((3,) + small.shape, F32),
-            pltpu.VMEM((3,) + small.shape, F32),
             dma((2 + ways,)),
             dma((2 + ways,)),
+            dma((11,)),
+            dma((groups, 4, 2)),
+            dma((2, ways, 2)),
         ],
         compiler_params=pltpu.CompilerParams(
-            collective_id=1, has_side_effects=True, vmem_limit_bytes=56 * MIB
+            collective_id=1, has_side_effects=True, vmem_limit_bytes=63 * MIB
         ),
     )(
-        out_part.reshape(ways, rows, width),
-        normed_part.reshape(ways, rows, width),
-        weight_part.reshape(groups, chips, span, cols),
-        small,
+        p0, ngm, flat(normed), xh, flat(g), flat(hg), flat(hidden), q, k, v, flat(mg), mix,
+        lse, cos, sin, wa, labels, small,
     )
     return out[0].astype(F32), out[1].astype(F32), gwo.astype(F32), smallo
 
@@ -907,8 +1116,7 @@
     normed = (x_hat * gain + shift).astype(BF16)
     projected = dot_nn(normed, wp) + qkv_shift.reshape(1, 3 * head_cols)
     mix_grad = dot_nn(g_all, wd).astype(BF16)
-    attend = attention if head_cols % 128 == 0 else attention_plain
-    mixture, gq, gk, gv = attend(
+    mixture, gq, gk, gv = attention_plain(
         projected[:, :head_cols],
         projected[:, head_cols : 2 * head_cols],
         projected[:, 2 * head_cols :],
@@ -957,48 +1165,21 @@
 def fast_work(x, g, wsrc, places, segments, gain, shift, fc1_shift, qkv_shift):
     ways = lax.axis_size("ctx")
     rows, width = x.shape
-    unused, unused, depth, cols = wsrc.shape
+    cols = wsrc.shape[-1]
     head_cols = cols // 4
-    g_all, ids, normed, x_hat, hidden, hidden_grad, out_mlp, back_mlp, projected, mix_grad, wa, fc1_sum, unused = forward(
-        x, g, wsrc, places, segments, gain, shift, fc1_shift, qkv_shift
-    )
-    flat = lambda t: t.reshape(ways * rows, t.shape[-1])
-    g_all, normed, x_hat, hidden, hidden_grad = map(flat, (g_all, normed, x_hat, hidden, hidden_grad))
-    out_mlp, back_mlp, projected, mix_grad = map(flat, (out_mlp, back_mlp, projected, mix_grad))
-    ids = ids[:, :2].transpose(1, 0, 2).reshape(2, ways * rows)
-    wp, wd = wa[:, : 3 * head_cols], wa[:, 3 * head_cols :]
-    mixture, gq, gk, gv = attention(
-        projected[:, :head_cols],
-        projected[:, head_cols : 2 * head_cols],
-        projected[:, 2 * head_cols :],
-        mix_grad,
-        ids[0],
-        ids[1],
-    )
-    proj_grad = jnp.concatenate([gq, gk, gv], 1)
-    out_part = (dot_nt(mixture, wd) + out_mlp.astype(F32)).astype(BF16)
-    normed_part = dot_nt(proj_grad, wp) + back_mlp.astype(F32)
-    weight_part = jnp.stack(
-        [
-            dot_tn(normed, hidden_grad).astype(BF16),
-            dot_tn(g_all, hidden).astype(BF16),
-            jnp.concatenate([dot_tn(normed, proj_grad), dot_tn(g_all, mixture)], 1).astype(BF16),
-        ]
-    )
-    qkv_sum = jnp.sum(proj_grad.astype(F32), 0)
-    line = lambda t: jnp.pad(t.reshape(-1), (0, width - t.size))
-    small = jnp.stack(
-        [
-            jnp.sum(normed_part * x_hat.astype(F32), 0),
-            jnp.sum(normed_part, 0),
-            jnp.sum(g.astype(F32), 0),
-            line(fc1_sum),
-            line(qkv_sum),
-        ]
-        + [jnp.zeros((width,), F32)] * 3
-    )
-    branches, normed_grad, weight_grads, sums = scatter(
-        out_part, normed_part.astype(BF16), weight_part, small
+    ids = jnp.zeros((8, rows), jnp.int32).at[0].set(places).at[1].set(segments)
+    (
+        g_all, normed, x_hat, hidden, hidden_grad, out_part, back_mlp, mix_grad, wa,
+        q, k, v, mixture, lse, cos, sin, labels, fc1_sum, unused,
+    ) = forward(x, g, wsrc, ids, gain, shift, fc1_shift, qkv_shift)
+    line = lambda t: jnp.pad(t.reshape(1, -1), ((0, 0), (0, width - t.size)))
+    none = jnp.zeros((1, width), F32)
+    small = jnp.concatenate(
+        [none, none, jnp.sum(g.astype(F32), 0, keepdims=True), line(fc1_sum)] + [none] * 4
+    )
+    branches, normed_grad, weight_grads, sums = backward(
+        out_part, back_mlp, normed, x_hat, g_all, hidden_grad, hidden,
+        q, k, v, mix_grad, mixture, lse, cos, sin, wa, labels, small,
     )
     total = jnp.sum(sums[:, :3], 0)
     fc1_bias_sum = sums[:, 3, :cols].reshape(ways * cols)

time: 626 us -> 505 us (0.81)
  the two profiles are of different devices: /device:TPU:0 before, /device:TPU:24 now
where the time goes in v4:
time: 505 us; the launch traced here: 498 us
  Pallas kernels  448 us (89%)
  local copies, waits for them, and re-layouts  32.9 us (7%)
  other arithmetic  15.4 us (3%)
    pallas_call x1, Pallas kernels, backward(): pl.pallas_call(functools.partial(backward_body, ways), in_specs=[anywhere...  225 us
    pallas_call x1, Pallas kernels, forward(): pl.pallas_call(functools.partial(forward_body, ways), in_specs=[anywhere]...  223 us

profile of v4, /device:TPU:24, one launch (start us, length us, event | category | flops | bytes accessed | tf_op | source)
XLA Modules:
  0.0 498.0 jit_solution(11678074932513708206)
XLA Ops:
  2.0 1.3 dynamic-slice_convert_fusion
  3.2 1.3 convert_element_type.51
  4.5 1.5 copy.42
  6.7 1.6 copy.39
  8.9 1.5 copy.41
  10.4 2.0 pad_maximum_fusion.w
  13.7 223.2 %shard_map.212 = (bf16[4,384,2048]{2,1,0:T(8,128)(2,1)}, bf16[4,384,2048]{2,1,0:T(8,128)(2,1)}, bf16[4,384,2048]{2,1,0:T(8,128)(2,1)}, bf16[4,384,1024]{2,1,0:T(...) custom-call(bf16[384,2048]{1,0:T(8,128)(2,1)} %bitcast.73, ...), custom_call_target="tpu_custom_call" | custom-call | tf_op jit(solution)/shard_map/pallas_call | solution.py:531
  237.3 1.4 fusion.16.small
  238.7 225.1 %shard_map.213 = (bf16[2,384,2048]{2,1,0:T(8,128)(2,1)}, bf16[3,4,128,1024]{3,2,1,0:T(8,128)(2,1)}, bf16[2,4,2,96,2048]{4,3,2,1,0:T(8,128)(2,1)}, f32[4,8,2048]{2,1,0:T(8,128)}) custom-call(bf16[4,384,2048]{2,1,0:T(8,128)(2,1)} %get-tuple-element.56.p0, bf16[4,384,2048]{2,1,0:T(8,128)(2,1)} %get-tuple-element.57.ngm, bf16[1536,2048]{1,0:T(8,128)(2,1)} %bitcast.77, ...), custom_call_target="tpu_custom_call" | custom-call | tf_op jit(solution)/shard_map/pallas_call | solution.py:1029
  463.8 2.6 convert_element_type.62
  466.4 2.6 slice_bitcast_fusion
  469.0 2.1 copy.49
  471.2 1.8 copy.51
  473.0 3.0 copy.50
  476.0 1.6 slice.83
  477.6 2.2 reshape_squeeze.9
  480.2 1.0 copy-done.3
  481.1 2.2 copy.46
  483.3 3.0 reshape.222
  486.3 2.1 slice.85
  488.5 1.0 copy.53
  490.4 1.0 copy-done.5
  491.4 1.0 fusion.15
  492.4 3.3 fusion.12
  (57 shorter events, 7.2 us)
Async XLA Ops:
  0.6 5.8 %copy-start.6 = (bf16[1024,128]{1,0:T(8,128)(2,1)S(1)}, bf16[1024,128]{1,0:T(8,128)(2,1)}, u32[]{:S(2)}) copy-start(bf16[1024,128]{1,0:T(8,128)(2,1)} %param.25) | copy-start | bytes 786436
  10.3 2.0 copy-start.12
  10.4 2.0 copy-start.13
  10.4 2.1 copy-start.10
  12.5 1.2 copy-start.9
  13.7 223.2 %copy-start.1 = (bf16[1,384,2048]{2,1,0:T(8,128)(2,1)S(1)}, bf16[1,384,2048]{2,1,0:T(8,128)(2,1)}, u32[]{:S(2)}) copy-start(bf16[1,384,2048]{2,1,0:T(8,128)(2,1)} %param.18) | copy-start | bytes 4718596
  473.0 3.0 copy-start.4
  479.8 1.3 copy-start.3
  483.3 6.2 %copy-start = (bf16[1,384,2048]{2,1,0:T(8,128)(2,1)S(1)}, bf16[1,384,2048]{2,1,0:T(8,128)(2,1)}, u32[]{:S(2)}) copy-start(bf16[1,384,2048]{2,1,0:T(8,128)(2,1)} %param.17) | copy-start | bytes 4718596
  486.3 4.1 copy-start.7
  489.5 1.9 copy-start.5
  489.5 2.9 copy-start.11
  489.5 2.9 copy-start.2
  492.4 3.3 copy-start.8

commit v5 on v4

--- a/solution.py
+++ b/solution.py
@@ -156,16 +156,16 @@
 
 
 def forward_body(
-    ways, x, g, w, ids, gain, shift, fc1_shift, qkv_shift, freq,
+    ways, x, g, w1, w2, wq, wd, ids, gain, shift, fc1_shift, qkv_shift, freq,
     go, no, xho, ho, hgo, outo, ngo, mgo, wao, qo, ko, vo, mixo, lseo, coso, sino, ido, biaso,
-    xo, wv, norm, xb, gb, pre, hid, slope, hgb, ob, nb, mb, qb, kb, vb, mixb, lse, cosb, sinb, labr, labc,
+    xo, w1v, w2v, wqv, wdv, norm, xb, gb, pre, hid, slope, hgb, ob, nb, mb, qb, kb, vb, mixb, lse, cosb, sinb, labr, labc,
     zs, zr, ts, tr, ws, wr, ls, lr, ds, dr, ids_s, ids_r, own, ls_in, ls_out, keep_out,
 ):
     dp, me, core, dpx, dpy = place_of()
     rows, width = x.shape
     piece = rows // 2 // PIECES
-    groups, unused, depth, cols = w.shape
-    head_cols = cols // 4
+    groups, depth = ws.shape[0], w1.shape[0]
+    cols, head_cols = w1v.shape[1], wdv.shape[0]
     srcs, outs = (x, g), (xo, go)
     blocks = [me, 1 + me % 2, None, 3 * (1 - me // 2)]
     blocks[2] = 6 - me - blocks[1] - blocks[3]
@@ -189,80 +189,109 @@
         ref = outs[a].at[owner, at, :]
         return remote(ref, ref, ts.at[a, owner, s], tr.at[a, owner, s], (dp, me, 1 - core))
 
-    def rows_of(chip, j):
-        return pl.ds(pl.multiple_of((chip * ways + j) * depth, 16), depth)
+    def here(chip, j, height=None):
+        return pl.ds(pl.multiple_of((chip * ways + j) * depth, depth), depth)
+
+    def held(grp, chip, j):
+        at = here(chip, j)
+        return ([w1v.at[at, :]], [w2v.at[:, at]], [wqv.at[at, :], wdv.at[:, at]])[grp]
+
+    def given(grp, d):
+        at = here(dp, me)
+        mine = pl.ds(pl.multiple_of(d * cols, 128), cols)
+        if grp == 0:
+            return [(w1.at[:, mine], w1v.at[at, :])]
+        if grp == 1:
+            return [(w2.at[mine, :], w2v.at[:, at])]
+        mine = pl.ds(pl.multiple_of(d * head_cols, 128), head_cols)
+        return [
+            (wq.at[c, :, mine], wqv.at[at, pl.ds(c * head_cols, head_cols)]) for c in range(3)
+        ] + [(wd.at[mine, :], wdv.at[:, at])]
 
     def share(grp, k):
-        return remote(
-            w.at[grp, (me + k) % ways],
-            wv.at[grp, rows_of(dp, me), :],
-            ws.at[grp, k],
-            wr.at[grp, k],
-            (dp, (me + k) % ways, core),
-        )
+        d = (me + k) % ways
+        return [
+            remote(src, dst, ws.at[grp, k, i], wr.at[grp, k, i], (dp, d, core))
+            for i, (src, dst) in enumerate(given(grp, d))
+        ]
+
+    def keep(grp):
+        return [
+            pltpu.make_async_copy(src, dst, ws.at[grp, 0, i])
+            for i, (src, dst) in enumerate(given(grp, me))
+        ]
 
     def source(k):
         return (me - k + ways) % ways
 
     def spread(grp, k, axis):
-        at = rows_of(dp, source(k))
-        return remote(
-            w.at[grp, me] if k == 0 else wv.at[grp, at, :],
-            wv.at[grp, at, :],
-            ls.at[axis, grp, k],
-            lr.at[axis, grp, k],
-            ((dpx, dpy)[axis], me, core),
-        )
+        return [
+            remote(ref, ref, ls.at[axis, grp, k, i], lr.at[axis, grp, k, i], ((dpx, dpy)[axis], me, core))
+            for i, ref in enumerate(held(grp, dp, source(k)))
+        ]
 
     def corner(grp, k):
         axis = (grp + k) % 2
-        ref = wv.at[grp, rows_of((dpx, dpy)[axis], source(k)), :]
-        return remote(ref, ref, ds.at[grp, k], dr.at[grp, k], ((dpy, dpx)[axis], me, core))
+        return [
+            remote(ref, ref, ds.at[grp, k, i], dr.at[grp, k, i], ((dpy, dpx)[axis], me, core))
+            for i, ref in enumerate(held(grp, (dpx, dpy)[axis], source(k)))
+        ]
+
+    def start(copies):
+        for copy in copies:
+            copy.start()
+
+    def wait_recv(copies):
+        for copy in copies:
+            copy.wait_recv()
+
+    def wait_send(copies):
+        for copy in copies:
+            copy.wait_send()
 
     def labels(k):
         return remote(ids, ido.at[me], ids_s.at[k], ids_r.at[k], (dp, (me + k) % ways, core))
 
-    def send_own(a):
-        for s in range(PIECES):
-            pl.when(me > 0)(lambda: along(a, me, s, 0, True).start())
-            pl.when(me < ways - 1)(lambda: along(a, me, s, 1, True).start())
-
-    def send_shares(grp):
-        for k in range(1, ways):
-            share(grp, k).start()
+    def send_own(a, s):
+        pl.when(me > 0)(lambda: along(a, me, s, 0, True).start())
+        pl.when(me < ways - 1)(lambda: along(a, me, s, 1, True).start())
+
+    def send_share(grp, k):
+        if k:
+            start(share(grp, k))
+            return
+        start(keep(grp))
+        for copy in keep(grp):
+            copy.wait()
         for axis in range(2):
-            spread(grp, 0, axis).start()
-
-    def pass_on(a, k):
-        for s in range(PIECES):
-
-            @pl.when(me + k < ways)
-            def _():
-                along(a, me + k, s, 0).wait_recv()
-                pl.when(me > 0)(lambda: along(a, me + k, s, 0).start())
-                across(a, me + k, s, core).start()
-
-            @pl.when(me - k >= 0)
-            def _():
-                along(a, me - k, s, 1).wait_recv()
-                pl.when(me < ways - 1)(lambda: along(a, me - k, s, 1).start())
-                across(a, me - k, s, core).start()
+            start(spread(grp, 0, axis))
+
+    def pass_on(a, k, s):
+        @pl.when(me + k < ways)
+        def _():
+            along(a, me + k, s, 0).wait_recv()
+            pl.when(me > 0)(lambda: along(a, me + k, s, 0).start())
+            across(a, me + k, s, core).start()
+
+        @pl.when(me - k >= 0)
+        def _():
+            along(a, me - k, s, 1).wait_recv()
+            pl.when(me < ways - 1)(lambda: along(a, me - k, s, 1).start())
+            across(a, me - k, s, core).start()
 
     def spread_on(grp, k):
-        share(grp, k).wait_recv()
+        wait_recv(share(grp, k))
         for axis in range(2):
-            spread(grp, k, axis).start()
+            start(spread(grp, k, axis))
 
     def corner_on(grp, k):
-        axis = (grp + k) % 2
-        spread(grp, k, axis).wait_recv()
-        corner(grp, k).start()
+        wait_recv(spread(grp, k, (grp + k) % 2))
+        start(corner(grp, k))
 
     def settle(grp):
-        keeps[grp].wait()
         for k in range(ways):
-            spread(grp, k, 1 - (grp + k) % 2).wait_recv()
-            corner(grp, k).wait_recv()
+            wait_recv(spread(grp, k, 1 - (grp + k) % 2))
+            wait_recv(corner(grp, k))
 
     def arrive(a, t):
         if t:
@@ -323,7 +352,7 @@
         o = blocks[t]
 
         def mul(i):
-            pre[:, span(i)] = dot_nn(norm[o], wv[0, :, span(i)]) + fc1_shift[:, span(i)]
+            pre[:, span(i)] = dot_nn(norm[o], w1v[:, span(i)]) + fc1_shift[:, span(i)]
 
         loop(cols // wide, mul)
 
@@ -339,7 +368,7 @@
     def tables():
         for k in range(1, ways):
             labels(k).wait_recv()
-        keeps[groups + 1].wait()
+        keeps[1].wait()
         lse[...] = jnp.zeros_like(lse)
         for o in range(ways):
             at = slice(o * rows, (o + 1) * rows)
@@ -361,7 +390,7 @@
             lanes = pl.ds(pair * 128, 128)
             for which, ref in enumerate((qb, kb, vb)):
                 wide_lanes = pl.ds(which * head_cols + pair * 128, 128)
-                v = dot_nn(norm[o], wv[2, :, wide_lanes]) + qkv_shift[:, wide_lanes]
+                v = dot_nn(norm[o], wqv[:, wide_lanes]) + qkv_shift[:, wide_lanes]
                 if which < 2:
                     v = turn(v, cos, sin)
                 v = v.astype(BF16)
@@ -394,8 +423,8 @@
         at = pl.ds(pl.multiple_of(o * rows, 16), rows)
 
         def mul(i):
-            total = dot_nt(hid[o], wv[1, span(i), :])
-            total = total + dot_nt(mixb[at, :], wv[2, span(i), 3 * head_cols :])
+            total = dot_nn(hid[o], w2v[:, span(i)])
+            total = total + dot_nn(mixb[at, :], wdv[:, span(i)])
             ob[t % 2, :, span(i)] = total.astype(BF16)
 
         loop(width // wide, mul)
@@ -405,13 +434,12 @@
         arrive(1, t)
         load_g(t).start()
         if t >= 2:
-            store(4, t - 2).wait()
             store(5, t - 2).wait()
         load_g(t).wait()
         o = blocks[t]
 
         def mul(i):
-            act = dot_nn(gb[t % 2], wv[1, :, span(i)])
+            act = dot_nt(gb[t % 2], w2v[span(i), :])
             grad = (act * slope[o, :, span(i)]).astype(BF16)
             hgb[t % 2, :, span(i)] = grad
             total = jnp.sum(grad.astype(F32), 0, keepdims=True)
@@ -420,30 +448,28 @@
         loop(cols // wide, mul)
         store(5, t).start()
 
+    def back_on(t):
+        if t >= 2:
+            store(4, t - 2).wait()
+
         def mul_back(i):
-            nb[t % 2, :, span(i)] = dot_nt(hgb[t % 2], wv[0, span(i), :]).astype(BF16)
+            nb[t % 2, :, span(i)] = dot_nt(hgb[t % 2], w1v[span(i), :]).astype(BF16)
 
         loop(width // wide, mul_back)
         store(4, t).start()
-        mb[t] = dot_nn(gb[t % 2], wv[2, :, 3 * head_cols :]).astype(BF16)
+        mb[t] = dot_nt(gb[t % 2], wdv[...]).astype(BF16)
         store(6, t).start()
 
     greet(ways)
-    send_own(0)
-    send_shares(0)
-    send_shares(1)
     for k in range(1, ways):
         labels(k).start()
     keeps = [
-        pltpu.make_async_copy(w.at[i, me], wv.at[i, rows_of(dp, me), :], own.at[i])
-        for i in range(groups)
-    ] + [
-        pltpu.make_async_copy(g, go.at[me], own.at[groups]),
-        pltpu.make_async_copy(ids, ido.at[me], own.at[groups + 1]),
+        pltpu.make_async_copy(g, go.at[me], own.at[0]),
+        pltpu.make_async_copy(ids, ido.at[me], own.at[1]),
     ]
     for copy in keeps:
         copy.start()
-    wa_out = pltpu.make_async_copy(wv.at[2], wao, own.at[groups + 2])
+    wa_out = pltpu.make_async_copy(wqv, wao, own.at[2])
     stores = [
         pltpu.make_async_copy(src, dst, keep_out.at[i])
         for i, (src, dst) in enumerate(
@@ -452,12 +478,13 @@
     ]
     table_stores, state_stores = stores[:2], stores[2:]
     steps = dict(
-        S=send_shares,
-        G=lambda: send_own(1),
+        X=lambda s: send_own(0, s),
+        G=lambda s: send_own(1, s),
+        S=send_share,
         W=wa_out.start,
         Z=lambda: [copy.start() for copy in state_stores],
-        x=lambda k: pass_on(0, k),
-        g=lambda k: pass_on(1, k),
+        x=lambda k, s: pass_on(0, k, s),
+        g=lambda k, s: pass_on(1, k, s),
         s=spread_on,
         c=corner_on,
         e=settle,
@@ -468,17 +495,20 @@
         a=attend,
         d=down,
         b=back,
+        r=back_on,
     )
     plan = (
-        "n0", "s01", "c00", "x1", "S2", "n1", "s02", "c01", "s03", "c02", "x2", "G", "n2", "c03",
-        "l", "s11", "c10", "s12", "c11", "s13", "c12", "x3", "n3", "e0", "u0", "c13", "s21", "c20",
-        "u1", "s22", "c21", "u2", "g1", "s23", "c22", "u3", "c23", "e2", "W", "p0", "p1", "p2",
-        "p3", "a00", "a01", "a02", "a03", "g2", "a04", "a05", "a10", "a11", "a12", "a13", "a14",
-        "a15", "Z", "e1", "d0", "b0", "d1", "b1", "g3", "d2", "d3", "b2", "b3",
+        "S03", "S20", "X0", "S10", "l", "S01", "S00", "S02", "n0", "s01", "X1", "c10", "c20",
+        "s03", "x10", "S21", "S23", "s02", "c00", "c01", "c03", "S22", "x11", "s21", "x20", "n1",
+        "c02", "s23", "e0", "S11", "s22", "S13", "u0", "c21", "c23", "u1", "c22", "x21", "n2",
+        "u2", "x30", "S12", "e2", "p0", "s13", "p1", "s11", "W", "p2", "x31", "G0", "G1", "n3",
+        "p3", "a11", "s12", "a12", "a05", "a01", "c13", "a14", "a15", "u3", "c12", "c11", "g10",
+        "a04", "a02", "a00", "a03", "a13", "g11", "e1", "b0", "a10", "r0", "b1", "g20", "Z", "d0",
+        "d1", "d2", "g21", "r1", "g30", "b2", "r2", "g31", "d3", "b3", "r3",
     )
     for word in plan:
         steps[word[0]](*(int(digit) for digit in word[1:]))
-    keeps[groups].wait()
+    keeps[0].wait()
 
     for k in range(1, ways):
         labels(k).wait_send()
@@ -510,17 +540,16 @@
     for grp in range(groups):
         for k in range(ways):
             if k:
-                share(grp, k).wait_send()
+                wait_send(share(grp, k))
             for axis in range(2):
-                spread(grp, k, axis).wait_send()
-            corner(grp, k).wait_send()
-
-
-def forward(x, g, wsrc, ids, gain, shift, fc1_shift, qkv_shift):
+                wait_send(spread(grp, k, axis))
+            wait_send(corner(grp, k))
+
+
+def forward(x, g, w1, w2, wq, wd, ids, gain, shift, fc1_shift, qkv_shift):
     ways = lax.axis_size("ctx")
     rows, width = x.shape
-    groups, unused, depth, cols = wsrc.shape
-    head_cols = cols // 4
+    groups, cols, head_cols = 3, w1.shape[1] // ways, wd.shape[0] // ways
     dma = pltpu.SemaphoreType.DMA
     vmem = pltpu.VMEM
     anywhere = pl.BlockSpec(memory_space=pl.ANY)
@@ -530,7 +559,7 @@
     line = lambda n, dtype: jax.ShapeDtypeStruct((tokens, n), dtype)
     outs = pl.pallas_call(
         functools.partial(forward_body, ways),
-        in_specs=[anywhere] * 4 + [inside] * 5,
+        in_specs=[anywhere] * 7 + [inside] * 5,
         out_specs=[anywhere] * 16 + [inside] * 2 + [anywhere],
         out_shape=[
             seq(width),
@@ -541,7 +570,7 @@
             seq(width),
             seq(width),
             seq(head_cols),
-            jax.ShapeDtypeStruct((width, cols), BF16),
+            jax.ShapeDtypeStruct((width, 3 * head_cols), BF16),
             line(head_cols, BF16),
             line(head_cols, BF16),
             line(head_cols, BF16),
@@ -554,7 +583,10 @@
             seq(width),
         ],
         scratch_shapes=[
-            vmem((groups, width, cols), BF16),
+            vmem((width, cols), BF16),
+            vmem((cols, width), BF16),
+            vmem((width, 3 * head_cols), BF16),
+            vmem((head_cols, width), BF16),
             vmem((ways, rows, width), BF16),
             vmem((2, rows, width), BF16),
             vmem((2, rows, width), BF16),
@@ -578,15 +610,15 @@
             dma((2, ways, PIECES)),
             dma((2, ways, PIECES)),
             dma((2, ways, PIECES)),
-            dma((groups, ways)),
-            dma((groups, ways)),
-            dma((2, groups, ways)),
-            dma((2, groups, ways)),
-            dma((groups, ways)),
-            dma((groups, ways)),
+            dma((groups, ways, 4)),
+            dma((groups, ways, 4)),
+            dma((2, groups, ways, 2)),
+            dma((2, groups, ways, 2)),
+            dma((groups, ways, 2)),
+            dma((groups, ways, 2)),
             dma((ways,)),
             dma((ways,)),
-            dma((3 + groups,)),
+            dma((3,)),
             dma((2, ways)),
             dma((7, ways)),
             dma((7,)),
@@ -595,7 +627,7 @@
             collective_id=0, has_side_effects=True, vmem_limit_bytes=62 * MIB
         ),
     )(
-        x, g, wsrc, ids,
+        x, g, w1, w2, wq, wd, ids,
         gain.reshape(1, width), shift.reshape(1, width), fc1_shift.reshape(1, cols),
         qkv_shift.reshape(1, 3 * head_cols), frequencies(),
     )
@@ -605,7 +637,7 @@
 def backward_body(
     ways,
     p0, ngm, normed, xh, g, hg, hidden, q, k, v, mg, mix, lse, cos, sin, wa, labels, small,
-    out, gwo, tin, smallo,
+    out, g1, g2, gq, gd, tin, smallo,
     lt, ra, rb, wp, qv, kv, vv, mgv, lsev, cosv, sinv, dkv, dvv, labr, labc,
     acc, zin, tst, ngi, xhi, ngs, gown, gsend, first_in, second_in, sums, sum_in, sum_out,
     tps, tpr, zs, zr, fs, fr, ss, sr, ws, wr, os, orr, loc, tloc, sms, smr, ins, lts, ngl,
@@ -618,7 +650,7 @@
     span_rows = gown.shape[3]
     lanes = gown.shape[4]
     depth = span_rows // ways
-    head_cols = q.shape[1]
+    cols, head_cols = hg.shape[1], q.shape[1]
     nxt = (dpx, dpy)
     far = dpx + dpy - dp
     scale = 1.0 / math.sqrt(HD)
@@ -699,23 +731,22 @@
             pl.when((me == 0) & (d > 0))(lambda: stream(a, d, s, 1).start())
             pl.when((me == ways - 1) & (d < ways - 1))(lambda: stream(a, d, s, 0).start())
 
-    def hop(a, far_by, j):
-        for s in range(PIECES):
-            d = ways - 1 - j
-
-            @pl.when(me == far_by)
-            def _():
-                arrived(a, d, s, 1).wait_recv()
-                add(acc.at[a, d, s], zin.at[a, came(d, 1), s], piece)
-                if d > far_by:
-                    stream(a, d, s, 1).start()
-
-            @pl.when(me == ways - 1 - far_by)
-            def _():
-                arrived(a, j, s, 0).wait_recv()
-                add(acc.at[a, j, s], zin.at[a, came(j, 0), s], piece)
-                if j < ways - 1 - far_by:
-                    stream(a, j, s, 0).start()
+    def hop(a, far_by, j, s):
+        d = ways - 1 - j
+
+        @pl.when(me == far_by)
+        def _():
+            arrived(a, d, s, 1).wait_recv()
+            add(acc.at[a, d, s], zin.at[a, came(d, 1), s], piece)
+            if d > far_by:
+                stream(a, d, s, 1).start()
+
+        @pl.when(me == ways - 1 - far_by)
+        def _():
+            arrived(a, j, s, 0).wait_recv()
+            add(acc.at[a, j, s], zin.at[a, came(j, 0), s], piece)
+            if j < ways - 1 - far_by:
+                stream(a, j, s, 0).start()
 
     def last(a):
         for s in range(PIECES):
@@ -743,22 +774,56 @@
             (nxt[1 - path], me, core),
         )
 
+    def pieces(grp, path, d):
+        ref = gown.at[grp % 2, path, 1]
+        across = pl.ds(pl.multiple_of(me * cols + path * lanes, 128), lanes)
+        heads = pl.ds(pl.multiple_of(me * head_cols, 128), head_cols)
+        rows_of_d = pl.ds(pl.multiple_of(d * depth, 128), depth)
+        if grp == 0:
+            return [(ref.at[rows_of_d, :], g1.at[:, across])]
+        if grp == 1:
+            return [(ref.at[:, rows_of_d], g2.at[across, :])]
+        if path == 0:
+            return [
+                (ref.at[rows_of_d, pl.ds(c * head_cols, head_cols)], gq.at[c, :, heads])
+                for c in range(2)
+            ]
+        per = head_cols // depth
+        dense_rows = pl.ds(pl.multiple_of(d // per * head_cols, 128), head_cols)
+        dense_lanes = pl.ds(pl.multiple_of(head_cols + d % per * depth, 128), depth)
+        return [
+            (ref.at[rows_of_d, pl.ds(0, head_cols)], gq.at[2, :, heads]),
+            (ref.at[dense_rows, dense_lanes], gd.at[heads, :]),
+        ]
+
     def share(grp, path, i):
         d = (me + i) % ways
-        return remote(
-            gown.at[grp % 2, path, 1, pl.ds(pl.multiple_of(d * depth, 16), depth), :],
-            gwo.at[grp, me, :, lanes_of(path)],
-            ws.at[grp, path, i],
-            wr.at[grp, path, i],
-            (dp, d, core),
-        )
+        return [
+            remote(src, dst, ws.at[grp, path, i, n], wr.at[grp, path, i, n], (dp, d, core))
+            for n, (src, dst) in enumerate(pieces(grp, path, d))
+        ]
 
     def keep(grp, path):
-        return pltpu.make_async_copy(
-            gown.at[grp % 2, path, 1, pl.ds(pl.multiple_of(me * depth, 16), depth), :],
-            gwo.at[grp, me, :, lanes_of(path)],
-            ws.at[grp, path, 0],
-        )
+        return [
+            pltpu.make_async_copy(src, dst, ws.at[grp, path, 0, n])
+            for n, (src, dst) in enumerate(pieces(grp, path, me))
+        ]
+
+    def start(copies):
+        for copy in copies:
+            copy.start()
+
+    def wait(copies):
+        for copy in copies:
+            copy.wait()
+
+    def wait_recv(copies):
+        for copy in copies:
+            copy.wait_recv()
+
+    def wait_send(copies):
+        for copy in copies:
+            copy.wait_send()
 
     quarters = (far, dpx, dpy, dp)
 
@@ -790,15 +855,19 @@
                 first(grp - 1, path, i).wait_send()
             if i is None and grp == 2:
                 if r == 3:
-                    keep(0, path).wait()
+                    wait(keep(0, path))
                     for n in range(1, ways):
-                        share(0, path, n).wait_send()
+                        wait_send(share(0, path, n))
                 else:
                     second(0, path).wait_send()
             right = (ra, rb, ra)[grp]
-            if grp == 2 and path == 1:
+            if grp == 1:
+                dst[...] = dot_tn(right[:, lanes_of(path)], lt[left]).astype(BF16)
+            elif grp == 2 and path == 1:
                 dst[:, :head_cols] = dot_tn(lt[0], right[:, 2 * head_cols : 3 * head_cols]).astype(BF16)
-                dst[:, head_cols:] = dot_tn(lt[1], right[:, 3 * head_cols :]).astype(BF16)
+                dense = dot_tn(right[:, 3 * head_cols :], lt[1]).astype(BF16)
+                dst[:head_cols, head_cols:] = dense[:, :head_cols]
+                dst[head_cols:, head_cols:] = dense[:, head_cols:]
             else:
                 dst[...] = dot_tn(lt[left], right[:, lanes_of(path)]).astype(BF16)
             if i is not None:
@@ -807,10 +876,12 @@
             load_left(grp, r + 1).start()
             load_left(grp, r + 1, 1).start()
 
-    def first_sum(grp, path):
+    def pass_sum(grp, path):
         first(grp, path, 0).wait_recv()
         add(gown.at[grp % 2, path, 0], first_in.at[grp, path, 0], span_rows)
         second(grp, path).start()
+
+    def first_sum(grp, path):
         first(grp, path, 1).wait_recv()
         add(gown.at[grp % 2, path, 1], first_in.at[grp, path, 1], span_rows)
 
@@ -818,11 +889,11 @@
         second(grp, path).wait_recv()
         add(gown.at[grp % 2, path, 1], second_in.at[grp, path], span_rows)
         for i in range(1, ways):
-            share(grp, path, i).start()
-        keep(grp, path).start()
+            start(share(grp, path, i))
+        start(keep(grp, path))
 
     pairs = (
-        (hg, ra), (hidden, rb), (wa.at[:, pl.ds(0, 3 * head_cols)], wp),
+        (hg, ra), (hidden, rb), (wa, wp),
         (q, qv), (k, kv), (v, vv), (mg, mgv), (lse, lsev), (cos, cosv), (sin, sinv),
     )
 
@@ -961,7 +1032,8 @@
 
     steps = dict(
         t=products,
-        f=first_sum,
+        f=pass_sum,
+        F=first_sum,
         h=second_sum,
         m=merge,
         z=hop,
@@ -974,12 +1046,14 @@
         y=small_step,
     )
     plan = (
-        "t00", "m00", "m03", "m01", "m02", "t01", "t02", "t03", "t10", "z010", "t11", "t12", "t13",
-        "B", "f00", "f01", "z011", "z020", "a00", "a01", "a02", "h00", "h01", "a03", "z012",
-        "z021", "a04", "z030", "a05", "o0", "f10", "f11", "a10", "a11", "h10", "h11", "a12", "a13",
-        "a14", "a15", "L", "n0", "n1", "m10", "m13", "n2", "n3", "m11", "m12", "Y", "t20", "y0",
-        "t21", "y1", "z110", "t22", "y2", "t23", "z111", "z120", "f20", "f21", "h20", "h21",
-        "z112", "z121", "z130", "o1",
+        "t00", "m00", "m03", "t01", "t02", "m01", "t03", "f01", "z0100", "B", "a00", "a01", "a02",
+        "z0101", "a03", "a04", "a05", "F01", "F00", "t10", "m02", "z0200", "a10", "h01", "a11",
+        "t11", "a12", "t12", "z0110", "a13", "f00", "a14", "a15", "n0", "n1", "z0111", "m10",
+        "m13", "h00", "n2", "f10", "z0300", "n3", "f11", "m12", "m11", "z0201", "t13", "F10",
+        "z1100", "L", "Y", "z1101", "y0", "z0210", "z0120", "z0121", "F11", "h10", "z0211", "y1",
+        "t20", "y2", "h11", "z1200", "z1110", "z0301", "t21", "t22", "f21", "z1120", "z1121",
+        "f20", "z1201", "z1300", "z1301", "t23", "z1111", "F20", "h20", "z1210", "z1211", "o1",
+        "o0", "F21", "h21",
     )
     for word in plan:
         steps[word[0]](*(int(digit) for digit in word[1:]))
@@ -1005,11 +1079,11 @@
                     first(grp, path, i).wait_send()
             if grp:
                 second(grp, path).wait_send()
-                keep(grp, path).wait()
+                wait(keep(grp, path))
             for i in range(1, ways):
-                share(grp, path, i).wait_recv()
+                wait_recv(share(grp, path, i))
                 if grp:
-                    share(grp, path, i).wait_send()
+                    wait_send(share(grp, path, i))
 
 
 def backward(p0, ngm, normed, xh, g, hg, hidden, q, k, v, mg, mix, lse, cos, sin, wa, labels, small):
@@ -1026,13 +1100,17 @@
     anywhere = pl.BlockSpec(memory_space=pl.ANY)
     inside = pl.BlockSpec(memory_space=pltpu.VMEM)
     flat = lambda t: t.reshape(tokens, t.shape[-1])
-    out, gwo, unused, smallo = pl.pallas_call(
+    depth = span // ways
+    out, g1, g2, gq, gd, unused, smallo = pl.pallas_call(
         functools.partial(backward_body, ways),
         in_specs=[anywhere] * 16 + [inside] * 2,
-        out_specs=[anywhere] * 3 + [inside],
+        out_specs=[anywhere] * 6 + [inside],
         out_shape=[
             jax.ShapeDtypeStruct((2, rows, width), BF16),
-            jax.ShapeDtypeStruct((groups, ways, span // ways, cols), BF16),
+            jax.ShapeDtypeStruct((depth, ways * cols), BF16),
+            jax.ShapeDtypeStruct((ways * cols, depth), BF16),
+            jax.ShapeDtypeStruct((3, depth, ways * head_cols), BF16),
+            jax.ShapeDtypeStruct((ways * head_cols, depth), BF16),
             jax.ShapeDtypeStruct((2, ways, PIECES, piece, width), BF16),
             jax.ShapeDtypeStruct((ways,) + small.shape, F32),
         ],
@@ -1073,8 +1151,8 @@
             dma((groups, 2, 2)),
             dma((groups, 2)),
             dma((groups, 2)),
-            dma((groups, 2, ways)),
-            dma((groups, 2, ways)),
+            dma((groups, 2, ways, 2)),
+            dma((groups, 2, ways, 2)),
             dma((2, 2, PIECES)),
             dma((2, PIECES)),
             dma((ways, PIECES)),
@@ -1092,7 +1170,8 @@
         p0, ngm, flat(normed), xh, flat(g), flat(hg), flat(hidden), q, k, v, flat(mg), mix,
         lse, cos, sin, wa, labels, small,
     )
-    return out[0].astype(F32), out[1].astype(F32), gwo.astype(F32), smallo
+    grads = tuple(t.astype(F32) for t in (gq, gd, g1, g2))
+    return out[0].astype(F32), out[1].astype(F32), grads, smallo
 
 
 def layer_norm(x):
@@ -1103,11 +1182,19 @@
     return centred * inv_std, inv_std
 
 
-def plain_work(x, g, wsrc, places, segments, gain, shift, fc1_shift, qkv_shift):
+def plain_work(
+    x, g, w_qkv, w_dense, w_fc1, w_fc2, places, segments, gain, shift, fc1_shift, qkv_shift
+):
     me, ways = lax.axis_index("ctx"), lax.axis_size("ctx")
     width = x.shape[1]
-    unused, unused, depth, cols = wsrc.shape
-    head_cols = cols // 4
+    depth = w_fc1.shape[0]
+    cols, head_cols = w_fc1.shape[1] // ways, w_dense.shape[0] // ways
+    fc1 = w_fc1.reshape(depth, ways, cols).transpose(1, 0, 2)
+    fc2 = w_fc2.reshape(ways, cols, depth).transpose(0, 2, 1)
+    qkv = w_qkv.reshape(3, depth, ways, head_cols).transpose(2, 1, 0, 3)
+    dense = w_dense.reshape(ways, head_cols, depth).transpose(0, 2, 1)
+    att = jnp.concatenate([qkv.reshape(ways, depth, 3 * head_cols), dense], -1)
+    wsrc = jnp.stack([fc1, fc2, att])
     x_all, g_all, weights, places, segments = gather_plain(x, g, wsrc, places, segments)
     weights = weights.reshape(3, width, cols)
     w1, w2, wa = weights[0], weights[1], weights[2]
@@ -1159,19 +1246,26 @@
     norms = lax.psum(
         (jnp.sum(normed_part * x_hat, 0), jnp.sum(normed_part, 0)), ("dp", "ctx", "tp")
     )
+    grad_fc1 = weight_grads[0].transpose(1, 0, 2).reshape(depth, ways * cols)
+    grad_fc2 = weight_grads[1].transpose(0, 2, 1).reshape(ways * cols, depth)
+    grad_att = weight_grads[2].reshape(ways, depth, 4, head_cols)
+    grad_qkv = grad_att[:, :, :3].transpose(2, 1, 0, 3).reshape(3, depth, ways * head_cols)
+    grad_dense = grad_att[:, :, 3].transpose(0, 2, 1).reshape(ways * head_cols, depth)
+    weight_grads = (grad_qkv, grad_dense, grad_fc1, grad_fc2)
     return branches, normed_grad, weight_grads, norms + small
 
 
-def fast_work(x, g, wsrc, places, segments, gain, shift, fc1_shift, qkv_shift):
+def fast_work(
+    x, g, w_qkv, w_dense, w_fc1, w_fc2, places, segments, gain, shift, fc1_shift, qkv_shift
+):
     ways = lax.axis_size("ctx")
     rows, width = x.shape
-    cols = wsrc.shape[-1]
-    head_cols = cols // 4
+    cols, head_cols = w_fc1.shape[1] // ways, w_dense.shape[0] // ways
     ids = jnp.zeros((8, rows), jnp.int32).at[0].set(places).at[1].set(segments)
     (
         g_all, normed, x_hat, hidden, hidden_grad, out_part, back_mlp, mix_grad, wa,
         q, k, v, mixture, lse, cos, sin, labels, fc1_sum, unused,
-    ) = forward(x, g, wsrc, ids, gain, shift, fc1_shift, qkv_shift)
+    ) = forward(x, g, w_fc1, w_fc2, w_qkv, w_dense, ids, gain, shift, fc1_shift, qkv_shift)
     line = lambda t: jnp.pad(t.reshape(1, -1), ((0, 0), (0, width - t.size)))
     none = jnp.zeros((1, width), F32)
     small = jnp.concatenate(
@@ -1211,24 +1305,16 @@
     me = lax.axis_index("ctx")
     x, g = block_input[0], cotangent[0]
     rows, width = x.shape
-    depth = w_fc1.shape[0]
-    cols = w_fc1.shape[1] // ways
-    head_cols = w_qkv.shape[2] // ways
-
-    fc1 = w_fc1.reshape(depth, ways, cols).transpose(1, 0, 2)
-    fc2 = w_fc2.reshape(ways, cols, depth).transpose(0, 2, 1)
-    qkv = w_qkv.reshape(3, depth, ways, head_cols).transpose(2, 1, 0, 3)
-    dense = w_dense.reshape(ways, head_cols, depth).transpose(0, 2, 1)
-    att = jnp.concatenate([qkv.reshape(ways, depth, 3 * head_cols), dense], -1)
-    wsrc = jnp.stack([fc1, fc2, att])
+    cols, head_cols = w_fc1.shape[1] // ways, w_dense.shape[0] // ways
 
     gain, shift = norm_gain.astype(F32), norm_bias.astype(F32)
     qkv_shift = lax.dynamic_slice_in_dim(qkv_bias, me * head_cols, head_cols, 1).astype(F32)
     fc1_shift = lax.dynamic_slice_in_dim(fc1_bias, me * cols, cols, 0).astype(F32)
-    fast = ways == 4 and lax.axis_size("dp") == 4 and rows % 64 == 0 and head_cols % 128 == 0
+    fast = ways == 4 and lax.axis_size("dp") == 4 and rows % 128 == 0
+    fast = fast and head_cols == 256 and x.shape[1] == 8 * head_cols
     work = fast_work if fast else plain_work
     branches, normed_grad, weight_grads, sums = work(
-        x, g, wsrc, positions[0], segment_ids[0], gain, shift, fc1_shift, qkv_shift
+        x, g, w_qkv, w_dense, w_fc1, w_fc2, positions[0], segment_ids[0], gain, shift, fc1_shift, qkv_shift
     )
 
     gf = g.astype(F32)
@@ -1242,11 +1328,7 @@
     )
     gain_sum, shift_sum, qkv_bias_sum, fc1_bias_sum, out_bias_sum = sums
 
-    grad_fc1 = weight_grads[0].transpose(1, 0, 2).reshape(depth, ways * cols)
-    grad_fc2 = weight_grads[1].transpose(0, 2, 1).reshape(ways * cols, depth)
-    grad_att = weight_grads[2].reshape(ways, depth, 4, head_cols)
-    grad_qkv = grad_att[:, :, :3].transpose(2, 1, 0, 3).reshape(3, depth, ways * head_cols)
-    grad_dense = grad_att[:, :, 3].transpose(0, 2, 1).reshape(ways * head_cols, depth)
+    grad_qkv, grad_dense, grad_fc1, grad_fc2 = weight_grads
     return (
         output[None],
         grad_input.astype(BF16)[None],

time: 505 us -> 401 us (0.79)
  the two profiles are of different devices: /device:TPU:24 before, /device:TPU:0 now
where the time goes in v5:
time: 401 us; the launch traced here: 395 us
  Pallas kernels  368 us (92%)
  other arithmetic  21.3 us (5%)
  local copies, waits for them, and re-layouts  4.59 us (1%)
    pallas_call x1, Pallas kernels, backward(): pl.pallas_call(functools.partial(backward_body, ways), in_specs=[anywhere...  186 us
    pallas_call x1, Pallas kernels, forward(): pl.pallas_call(functools.partial(forward_body, ways), in_specs=[anywhere]...  182 us

profile of v5, /device:TPU:0, one launch (start us, length us, event | category | flops | bytes accessed | tf_op | source)
XLA Modules:
  0.0 394.9 jit_solution(17474912313743627982)
XLA Ops:
  0.6 0.7 convert_bitcast_fusion.1
  1.3 0.6 copy.26
  1.9 1.3 dynamic-slice_convert_fusion
  3.2 1.3 convert_element_type.60
  4.5 0.7 scatter.6
  5.2 0.7 scatter.9.ids
  5.9 1.3 reshape.191
  7.2 0.6 concatenate.18
  7.8 182.0 %shard_map.212 = (bf16[4,384,2048]{2,1,0:T(8,128)(2,1)}, bf16[4,384,2048]{2,1,0:T(8,128)(2,1)}, bf16[4,384,2048]{2,1,0:T(8,128)(2,1)}, bf16[4,384,1024]{2,1,0:T(...) custom-call(bf16[384,2048]{1,0:T(8,128)(2,1)} %bitcast.37, ...), custom_call_target="tpu_custom_call" | custom-call | tf_op jit(solution)/shard_map/pallas_call | solution.py:560
  189.8 0.3 convert_reduce_fusion.1
  190.1 0.1 pad.13.clone
  190.1 1.4 fusion.16.small
  191.5 186.0 %shard_map.213 = (bf16[2,384,2048]{2,1,0:T(8,128)(2,1)}, bf16[128,4096]{1,0:T(8,128)(2,1)}, bf16[4096,128]{1,0:T(8,128)(2,1)}, bf16[3,128,1024]{2,1,0:T(8,128)(2...) custom-call(bf16[4,384,2048]{2,1,0:T(8,128)(2,1)} %get-tuple-element.59.p0, ...), custom_call_target="tpu_custom_call" | custom-call | tf_op jit(solution)/shard_map/pallas_call | solution.py:1104
  377.6 1.8 convert_reduce_fusion
  379.4 2.4 fusion.2
  381.8 2.4 fusion.15
  384.3 3.3 fusion.12
  387.6 1.5 convert_element_type.73
  389.1 1.5 convert_element_type.74
  390.6 1.3 convert_element_type.71
  391.9 0.8 convert_element_type.72
  392.8 0.6 fusion.18
  393.4 0.6 copy.27
  394.0 0.6 slice.59
  (36 shorter events, 0.1 us)
Async XLA Ops:
  5.9 1.9 copy-start.10
  7.8 182.0 %copy-start.1 = (bf16[1,384,2048]{2,1,0:T(8,128)(2,1)S(1)}, bf16[1,384,2048]{2,1,0:T(8,128)(2,1)}, u32[]{:S(2)}) copy-start(bf16[1,384,2048]{2,1,0:T(8,128)(2,1)} %param.18) | copy-start | bytes 4718596
  377.5 4.3 %copy-start = (bf16[1,384,2048]{2,1,0:T(8,128)(2,1)S(1)}, bf16[1,384,2048]{2,1,0:T(8,128)(2,1)}, u32[]{:S(2)}) copy-start(bf16[1,384,2048]{2,1,0:T(8,128)(2,1)} %param.17) | copy-start | bytes 4718596
  377.5 4.3 %copy-start.8 = (f32[2048]{0:T(1024)S(1)}, f32[2048]{0:T(1024)}, u32[]{:S(2)}) copy-start(f32[2048]{0:T(1024)} %convert_element_type.60) | copy-start | bytes 24580
  377.5 6.7 %copy-start.11 = (bf16[2048]{0:T(1024)(128)(2,1)S(1)}, bf16[2048]{0:T(1024)(128)(2,1)}, u32[]{:S(2)}) copy-start(bf16[2048]{0:T(1024)(128)(2,1)} %param.29) | copy-start | bytes 12292
  377.5 6.7 %copy-start.2 = (bf16[1,384,2048]{2,1,0:T(8,128)(2,1)S(1)}, bf16[1,384,2048]{2,1,0:T(8,128)(2,1)}, u32[]{:S(2)}) copy-start(bf16[1,384,2048]{2,1,0:T(8,128)(2,1)} %param.18) | copy-start | bytes 4718596
  377.5 6.7 %copy-start.3 = (bf16[2,384,2048]{2,1,0:T(8,128)(2,1)S(1)}, bf16[2,384,2048]{2,1,0:T(8,128)(2,1)}, u32[]{:S(2)}) copy-start(bf16[2,384,2048]{2,1,0:T(8,128)(2,1)} %get-tuple-element.77) | copy-start | bytes 9437188
  384.3 3.3 copy-start.5
  387.6 1.5 copy-start.4
  387.6 3.0 copy-start.6
  389.1 2.8 copy-start.7
  389.1 3.6 copy-start.9

commit v6 on v5

--- a/solution.py
+++ b/solution.py
@@ -3,6 +3,7 @@
 
 import jax
 import jax.numpy as jnp
+import numpy as np
 from jax import lax
 from jax.experimental import pallas as pl
 from jax.experimental.pallas import tpu as pltpu
@@ -34,10 +35,9 @@
 
 def frequencies():
     half = ROT // 2
-    one = jnp.concatenate(
-        [10000.0 ** (-(jnp.arange(half, dtype=F32) * 2.0 / ROT))] * 2 + [jnp.zeros(HD - ROT, F32)]
-    )
-    return jnp.concatenate([one, one])[None, :]
+    some = 10000.0 ** (-(np.arange(half, dtype=np.float32) * np.float32(2.0 / ROT)))
+    one = np.concatenate([some, some, np.zeros(HD - ROT)]).astype(np.float32)
+    return np.concatenate([one, one])[None, :]
 
 
 def turn(v, cos, sin):
@@ -156,8 +156,8 @@
 
 
 def forward_body(
-    ways, x, g, w1, w2, wq, wd, ids, gain, shift, fc1_shift, qkv_shift, freq,
-    go, no, xho, ho, hgo, outo, ngo, mgo, wao, qo, ko, vo, mixo, lseo, coso, sino, ido, biaso,
+    ways, x, g, w1, w2, wq, wd, ids, lines, freq,
+    go, no, xho, ho, hgo, outo, ngo, mgo, wao, qo, ko, vo, mixo, lseo, coso, sino, ido, small,
     xo, w1v, w2v, wqv, wdv, norm, xb, gb, pre, hid, slope, hgb, ob, nb, mb, qb, kb, vb, mixb, lse, cosb, sinb, labr, labc,
     zs, zr, ts, tr, ws, wr, ls, lr, ds, dr, ids_s, ids_r, own, ls_in, ls_out, keep_out,
 ):
@@ -166,6 +166,8 @@
     piece = rows // 2 // PIECES
     groups, depth = ws.shape[0], w1.shape[0]
     cols, head_cols = w1v.shape[1], wdv.shape[0]
+    gain, shift = lines.at[0:1, :], lines.at[1:2, :]
+    fc1_shift, qkv_shift = lines.at[2:3, 0:cols], lines.at[3:4, 0 : 3 * head_cols]
     srcs, outs = (x, g), (xo, go)
     blocks = [me, 1 + me % 2, None, 3 * (1 - me // 2)]
     blocks[2] = 6 - me - blocks[1] - blocks[3]
@@ -322,13 +324,23 @@
         )[which]
         return pltpu.make_async_copy(src, dst, ls_out.at[which, t])
 
-    def normalise(t):
+    def fetch_x(t):
         arrive(0, t)
         if t >= 2:
             store(0, t - 2).wait()
         load_x(t).start()
+
+    def fetch_g(t):
+        arrive(1, t)
+        if t == 2:
+            own_g.wait()
+        load_g(t).start()
+
+    own_g = pltpu.make_async_copy(gb.at[0], go.at[me], own.at[0])
+
+    def normalise(t):
         load_x(t).wait()
-        step = 32
+        step = 192
 
         def body(i):
             at = pl.ds(pl.multiple_of(i * step, step), step)
@@ -368,7 +380,7 @@
     def tables():
         for k in range(1, ways):
             labels(k).wait_recv()
-        keeps[1].wait()
+        keeps[0].wait()
         lse[...] = jnp.zeros_like(lse)
         for o in range(ways):
             at = slice(o * rows, (o + 1) * rows)
@@ -386,15 +398,17 @@
         o = blocks[t]
         at = pl.ds(pl.multiple_of(o * rows, 16), rows)
         cos, sin = cosb[at, :], sinb[at, :]
-        for pair in range(head_cols // 128):
-            lanes = pl.ds(pair * 128, 128)
-            for which, ref in enumerate((qb, kb, vb)):
-                wide_lanes = pl.ds(which * head_cols + pair * 128, 128)
-                v = dot_nn(norm[o], wqv[:, wide_lanes]) + qkv_shift[:, wide_lanes]
+        for which, ref in enumerate((qb, kb, vb)):
+            heads = pl.ds(which * head_cols, head_cols)
+            v = dot_nn(norm[o], wqv[:, heads]) + qkv_shift[:, heads]
+            for pair in range(head_cols // 128):
+                part_of = v[:, pair * 128 : (pair + 1) * 128]
                 if which < 2:
-                    v = turn(v, cos, sin)
-                v = v.astype(BF16)
-                ref[at, lanes] = v * BF16(1.0 / math.sqrt(HD)) if which == 0 else v
+                    part_of = turn(part_of, cos, sin)
+                part_of = part_of.astype(BF16)
+                if which == 0:
+                    part_of = part_of * BF16(1.0 / math.sqrt(HD))
+                ref[at, pl.ds(pair * 128, 128)] = part_of
 
     def attend(pair, i):
         lanes = pl.ds(pair * 128, 128)
@@ -431,11 +445,13 @@
         store(3, t).start()
 
     def back(t):
-        arrive(1, t)
-        load_g(t).start()
         if t >= 2:
             store(5, t - 2).wait()
         load_g(t).wait()
+        if t == 0:
+            own_g.start()
+            small[...] = jnp.zeros_like(small)
+            small[2:3, :] = jnp.sum(gb[0].astype(F32), 0, keepdims=True)
         o = blocks[t]
 
         def mul(i):
@@ -443,7 +459,7 @@
             grad = (act * slope[o, :, span(i)]).astype(BF16)
             hgb[t % 2, :, span(i)] = grad
             total = jnp.sum(grad.astype(F32), 0, keepdims=True)
-            biaso[:, span(i)] = total if t == 0 else biaso[:, span(i)] + total
+            small[3:4, span(i)] += total
 
         loop(cols // wide, mul)
         store(5, t).start()
@@ -464,7 +480,6 @@
     for k in range(1, ways):
         labels(k).start()
     keeps = [
-        pltpu.make_async_copy(g, go.at[me], own.at[0]),
         pltpu.make_async_copy(ids, ido.at[me], own.at[1]),
     ]
     for copy in keeps:
@@ -489,6 +504,8 @@
         c=corner_on,
         e=settle,
         l=tables,
+        i=fetch_x,
+        j=fetch_g,
         n=normalise,
         u=up,
         p=project,
@@ -498,18 +515,17 @@
         r=back_on,
     )
     plan = (
-        "S03", "S20", "X0", "S10", "l", "S01", "S00", "S02", "n0", "s01", "X1", "c10", "c20",
-        "s03", "x10", "S21", "S23", "s02", "c00", "c01", "c03", "S22", "x11", "s21", "x20", "n1",
-        "c02", "s23", "e0", "S11", "s22", "S13", "u0", "c21", "c23", "u1", "c22", "x21", "n2",
-        "u2", "x30", "S12", "e2", "p0", "s13", "p1", "s11", "W", "p2", "x31", "G0", "G1", "n3",
-        "p3", "a11", "s12", "a12", "a05", "a01", "c13", "a14", "a15", "u3", "c12", "c11", "g10",
-        "a04", "a02", "a00", "a03", "a13", "g11", "e1", "b0", "a10", "r0", "b1", "g20", "Z", "d0",
-        "d1", "d2", "g21", "r1", "g30", "b2", "r2", "g31", "d3", "b3", "r3",
+        "S22", "S21", "X0", "S10", "S20", "S23", "X1", "S01", "c10", "s22", "l", "S00", "c20",
+        "x10", "s23", "i0", "S03", "s21", "c22", "S02", "x11", "S11", "c23", "c21", "s01", "c01",
+        "i1", "S13", "s03", "e2", "j0", "n0", "c00", "x20", "s02", "W", "x21", "i2", "p0", "n1",
+        "x30", "c02", "c03", "p1", "S12", "n2", "p2", "s13", "e0", "G0", "u0", "s11", "x31", "i3",
+        "u1", "G1", "u2", "n3", "c13", "p3", "a12", "a05", "s12", "a14", "a00", "g10", "a04",
+        "a11", "a03", "a10", "a01", "c11", "a02", "c12", "a15", "g11", "a13", "u3", "j1", "e1",
+        "b0", "Z", "g20", "d0", "d1", "b1", "g21", "r1", "r0", "j2", "g30", "d2", "g31", "d3",
+        "j3", "b2", "r2", "b3", "r3",
     )
     for word in plan:
         steps[word[0]](*(int(digit) for digit in word[1:]))
-    keeps[0].wait()
-
     for k in range(1, ways):
         labels(k).wait_send()
     for copy in table_stores + state_stores:
@@ -546,7 +562,7 @@
             wait_send(corner(grp, k))
 
 
-def forward(x, g, w1, w2, wq, wd, ids, gain, shift, fc1_shift, qkv_shift):
+def forward(x, g, w1, w2, wq, wd, ids, lines):
     ways = lax.axis_size("ctx")
     rows, width = x.shape
     groups, cols, head_cols = 3, w1.shape[1] // ways, wd.shape[0] // ways
@@ -559,7 +575,7 @@
     line = lambda n, dtype: jax.ShapeDtypeStruct((tokens, n), dtype)
     outs = pl.pallas_call(
         functools.partial(forward_body, ways),
-        in_specs=[anywhere] * 7 + [inside] * 5,
+        in_specs=[anywhere] * 7 + [inside] * 2,
         out_specs=[anywhere] * 16 + [inside] * 2 + [anywhere],
         out_shape=[
             seq(width),
@@ -579,7 +595,7 @@
             line(128, F32),
             line(128, F32),
             jax.ShapeDtypeStruct((ways, 8, rows), jnp.int32),
-            jax.ShapeDtypeStruct((1, cols), F32),
+            jax.ShapeDtypeStruct((8, width), F32),
             seq(width),
         ],
         scratch_shapes=[
@@ -627,23 +643,21 @@
             collective_id=0, has_side_effects=True, vmem_limit_bytes=62 * MIB
         ),
     )(
-        x, g, w1, w2, wq, wd, ids,
-        gain.reshape(1, width), shift.reshape(1, width), fc1_shift.reshape(1, cols),
-        qkv_shift.reshape(1, 3 * head_cols), frequencies(),
+        x, g, w1, w2, wq, wd, ids, lines, frequencies(),
     )
     return outs
 
 
 def backward_body(
     ways,
-    p0, ngm, normed, xh, g, hg, hidden, q, k, v, mg, mix, lse, cos, sin, wa, labels, small,
-    out, g1, g2, gq, gd, tin, smallo,
+    p0, ngm, normed, xh, g_flat, hg, hidden, q, k, v, mg, mix, lse, cos, sin, wa, labels, small,
+    x, g, lines, out, gin, g1, g2, gq, gd, tin, smallo,
     lt, ra, rb, wp, qv, kv, vv, mgv, lsev, cosv, sinv, dkv, dvv, labr, labc,
     acc, zin, tst, ngi, xhi, ngs, gown, gsend, first_in, second_in, sums, sum_in, sum_out,
     tps, tpr, zs, zr, fs, fr, ss, sr, ws, wr, os, orr, loc, tloc, sms, smr, ins, lts, ngl,
 ):
     dp, me, core, dpx, dpy = place_of()
-    rows, width = out.shape[1:]
+    rows, width = out.shape
     half = rows // 2
     piece = half // PIECES
     groups = first_in.shape[0]
@@ -712,12 +726,21 @@
             ref, ref, zs.at[a, d, s], zr.at[a, came(d, side), s], (dp, me - 1 + 2 * side, core)
         )
 
+    results = (out, gin)
+
     def finish(a, s, which):
-        ref = out.at[a, part(which, s), :]
+        ref = results[a].at[part(which, s), :]
         return remote(acc.at[a, me, s], ref, os.at[0, a, s], orr.at[a, s], (dp, me, 1 - core))
 
     def finish_here(a, s):
-        return pltpu.make_async_copy(acc.at[a, me, s], out.at[a, part(core, s), :], os.at[1, a, s])
+        return pltpu.make_async_copy(
+            acc.at[a, me, s], results[a].at[part(core, s), :], os.at[1, a, s]
+        )
+
+    def load_own(i):
+        at = pl.ds(pl.multiple_of(core * half, 16), half)
+        src, dst = ((x.at[at, :], ngi.at[0]), (g.at[at, :], ngi.at[1]))[i]
+        return pltpu.make_async_copy(src, dst, ins.at[11 + i])
 
     def merge(a, d):
         for s in range(PIECES):
@@ -749,7 +772,28 @@
                 stream(a, j, s, 0).start()
 
     def last(a):
+        if a == 0:
+            for i in range(2):
+                load_own(i).start()
+            for i in range(2):
+                load_own(i).wait()
         for s in range(PIECES):
+            at = pl.ds(s * piece, piece)
+            xf = ngi[0, at, :].astype(F32)
+            total = acc[a, me, s].astype(F32)
+            if a == 0:
+                acc[a, me, s] = (xf + total + lines[4:5, :]).astype(BF16)
+            else:
+                centred = xf - jnp.mean(xf, -1, keepdims=True)
+                inv_std = lax.rsqrt(jnp.mean(centred * centred, -1, keepdims=True) + EPS)
+                x_hat = centred * inv_std
+                scaled = total * lines[0:1, :]
+                change = (
+                    scaled
+                    - jnp.mean(scaled, -1, keepdims=True)
+                    - x_hat * jnp.mean(scaled * x_hat, -1, keepdims=True)
+                )
+                acc[a, me, s] = (ngi[1, at, :].astype(F32) + inv_std * change).astype(BF16)
             finish(a, s, core).start()
             finish_here(a, s).start()
 
@@ -829,15 +873,13 @@
 
     def load_left(grp, r, which=0):
         at = pl.ds(pl.multiple_of(quarters[r] * span_rows, 128), span_rows)
-        src = (normed, g, normed)[grp] if which == 0 else g
+        src = (normed, g_flat, normed)[grp] if which == 0 else g_flat
         into = (4 * grp + r) % 2 if grp < 2 else which
         return pltpu.make_async_copy(src.at[:, at], lt.at[into], lts.at[grp, r, which])
 
     def products(grp, r):
         load_left(grp, r).wait()
-        if grp == 2:
-            load_left(grp, r, 1).wait()
-        elif 4 * grp + r < 7:
+        if 4 * grp + r < 7:
             after = 4 * grp + r + 1
             load_left(after // 4, after % 4).start()
         left = (4 * grp + r) % 2 if grp < 2 else 0
@@ -865,6 +907,9 @@
                 dst[...] = dot_tn(right[:, lanes_of(path)], lt[left]).astype(BF16)
             elif grp == 2 and path == 1:
                 dst[:, :head_cols] = dot_tn(lt[0], right[:, 2 * head_cols : 3 * head_cols]).astype(BF16)
+                if r < 3:
+                    load_left(grp, r + 1).start()
+                load_left(grp, r, 1).wait()
                 dense = dot_tn(right[:, 3 * head_cols :], lt[1]).astype(BF16)
                 dst[:head_cols, head_cols:] = dense[:, :head_cols]
                 dst[head_cols:, head_cols:] = dense[:, head_cols:]
@@ -873,7 +918,6 @@
             if i is not None:
                 first(grp, path, i).start()
         if grp == 2 and r < 3:
-            load_left(grp, r + 1).start()
             load_left(grp, r + 1, 1).start()
 
     def pass_sum(grp, path):
@@ -1046,14 +1090,14 @@
         y=small_step,
     )
     plan = (
-        "t00", "m00", "m03", "t01", "t02", "m01", "t03", "f01", "z0100", "B", "a00", "a01", "a02",
-        "z0101", "a03", "a04", "a05", "F01", "F00", "t10", "m02", "z0200", "a10", "h01", "a11",
-        "t11", "a12", "t12", "z0110", "a13", "f00", "a14", "a15", "n0", "n1", "z0111", "m10",
-        "m13", "h00", "n2", "f10", "z0300", "n3", "f11", "m12", "m11", "z0201", "t13", "F10",
-        "z1100", "L", "Y", "z1101", "y0", "z0210", "z0120", "z0121", "F11", "h10", "z0211", "y1",
-        "t20", "y2", "h11", "z1200", "z1110", "z0301", "t21", "t22", "f21", "z1120", "z1121",
-        "f20", "z1201", "z1300", "z1301", "t23", "z1111", "F20", "h20", "z1210", "z1211", "o1",
-        "o0", "F21", "h21",
+        "t00", "m00", "m03", "t01", "t02", "t03", "B", "m01", "z0100", "a00", "f00", "a01", "a02",
+        "a03", "a04", "f01", "z0101", "F00", "a05", "m02", "z0200", "t10", "a10", "h00", "F01",
+        "t11", "a11", "h01", "a12", "a13", "a14", "t12", "t13", "a15", "z0120", "n0", "z0300",
+        "n1", "m10", "z0110", "F11", "n2", "z0111", "m13", "f11", "n3", "F10", "L", "Y", "t20",
+        "m12", "z1100", "z0201", "t21", "y0", "m11", "f10", "z1101", "h11", "h10", "z1110",
+        "z1200", "t22", "t23", "z0121", "z0210", "f20", "y1", "f21", "z1111", "z1120", "z1201",
+        "z0211", "z1121", "z1210", "F20", "F21", "h20", "z1300", "y2", "z1211", "h21", "z0301",
+        "z1301", "o0", "o1",
     )
     for word in plan:
         steps[word[0]](*(int(digit) for digit in word[1:]))
@@ -1086,7 +1130,10 @@
                     wait_send(share(grp, path, i))
 
 
-def backward(p0, ngm, normed, xh, g, hg, hidden, q, k, v, mg, mix, lse, cos, sin, wa, labels, small):
+def backward(
+    p0, ngm, normed, xh, g_all, hg, hidden, q, k, v, mg, mix, lse, cos, sin, wa, labels, small,
+    x, g, lines,
+):
     ways, rows, width = p0.shape
     chips = lax.axis_size("dp")
     tokens = ways * rows
@@ -1101,12 +1148,13 @@
     inside = pl.BlockSpec(memory_space=pltpu.VMEM)
     flat = lambda t: t.reshape(tokens, t.shape[-1])
     depth = span // ways
-    out, g1, g2, gq, gd, unused, smallo = pl.pallas_call(
+    out, gin, g1, g2, gq, gd, unused, smallo = pl.pallas_call(
         functools.partial(backward_body, ways),
-        in_specs=[anywhere] * 16 + [inside] * 2,
-        out_specs=[anywhere] * 6 + [inside],
+        in_specs=[anywhere] * 16 + [inside] * 2 + [anywhere] * 2 + [inside],
+        out_specs=[anywhere] * 7 + [inside],
         out_shape=[
-            jax.ShapeDtypeStruct((2, rows, width), BF16),
+            jax.ShapeDtypeStruct((rows, width), BF16),
+            jax.ShapeDtypeStruct((rows, width), BF16),
             jax.ShapeDtypeStruct((depth, ways * cols), BF16),
             jax.ShapeDtypeStruct((ways * cols, depth), BF16),
             jax.ShapeDtypeStruct((3, depth, ways * head_cols), BF16),
@@ -1159,7 +1207,7 @@
             dma((2, ways, PIECES)),
             dma((2 + ways,)),
             dma((2 + ways,)),
-            dma((11,)),
+            dma((13,)),
             dma((groups, 4, 2)),
             dma((2, ways, 2)),
         ],
@@ -1167,11 +1215,11 @@
             collective_id=1, has_side_effects=True, vmem_limit_bytes=63 * MIB
         ),
     )(
-        p0, ngm, flat(normed), xh, flat(g), flat(hg), flat(hidden), q, k, v, flat(mg), mix,
-        lse, cos, sin, wa, labels, small,
+        p0, ngm, flat(normed), xh, flat(g_all), flat(hg), flat(hidden), q, k, v, flat(mg), mix,
+        lse, cos, sin, wa, labels, small, x, g, lines,
     )
     grads = tuple(t.astype(F32) for t in (gq, gd, g1, g2))
-    return out[0].astype(F32), out[1].astype(F32), grads, smallo
+    return out, gin, grads, smallo
 
 
 def layer_norm(x):
@@ -1183,7 +1231,7 @@
 
 
 def plain_work(
-    x, g, w_qkv, w_dense, w_fc1, w_fc2, places, segments, gain, shift, fc1_shift, qkv_shift
+    x, g, w_qkv, w_dense, w_fc1, w_fc2, places, segments, gain, shift, fc1_shift, qkv_shift, out_bias
 ):
     me, ways = lax.axis_index("ctx"), lax.axis_size("ctx")
     width = x.shape[1]
@@ -1252,38 +1300,45 @@
     grad_qkv = grad_att[:, :, :3].transpose(2, 1, 0, 3).reshape(3, depth, ways * head_cols)
     grad_dense = grad_att[:, :, 3].transpose(0, 2, 1).reshape(ways * head_cols, depth)
     weight_grads = (grad_qkv, grad_dense, grad_fc1, grad_fc2)
-    return branches, normed_grad, weight_grads, norms + small
+    gf = g.astype(F32)
+    output = (x.astype(F32) + branches + out_bias).astype(BF16)
+    own_hat, inv_std = layer_norm(x)
+    scaled = normed_grad * gain
+    grad_input = gf + inv_std * (
+        scaled
+        - jnp.mean(scaled, -1, keepdims=True)
+        - own_hat * jnp.mean(scaled * own_hat, -1, keepdims=True)
+    )
+    return output, grad_input.astype(BF16), weight_grads, norms + small
 
 
 def fast_work(
-    x, g, w_qkv, w_dense, w_fc1, w_fc2, places, segments, gain, shift, fc1_shift, qkv_shift
+    x, g, w_qkv, w_dense, w_fc1, w_fc2, places, segments, gain, shift, fc1_shift, qkv_shift, out_bias
 ):
     ways = lax.axis_size("ctx")
     rows, width = x.shape
     cols, head_cols = w_fc1.shape[1] // ways, w_dense.shape[0] // ways
-    ids = jnp.zeros((8, rows), jnp.int32).at[0].set(places).at[1].set(segments)
+    ids = jnp.concatenate([places[None], segments[None], jnp.zeros((6, rows), jnp.int32)])
+    line = lambda t: jnp.pad(t.reshape(1, -1), ((0, 0), (0, width - t.size)))
+    lines = jnp.concatenate(
+        [line(t) for t in (gain, shift, fc1_shift, qkv_shift, out_bias)]
+        + [jnp.zeros((3, width), F32)]
+    )
     (
         g_all, normed, x_hat, hidden, hidden_grad, out_part, back_mlp, mix_grad, wa,
-        q, k, v, mixture, lse, cos, sin, labels, fc1_sum, unused,
-    ) = forward(x, g, w_fc1, w_fc2, w_qkv, w_dense, ids, gain, shift, fc1_shift, qkv_shift)
-    line = lambda t: jnp.pad(t.reshape(1, -1), ((0, 0), (0, width - t.size)))
-    none = jnp.zeros((1, width), F32)
-    small = jnp.concatenate(
-        [none, none, jnp.sum(g.astype(F32), 0, keepdims=True), line(fc1_sum)] + [none] * 4
-    )
-    branches, normed_grad, weight_grads, sums = backward(
+        q, k, v, mixture, lse, cos, sin, labels, small, unused,
+    ) = forward(x, g, w_fc1, w_fc2, w_qkv, w_dense, ids, lines)
+    output, grad_input, weight_grads, sums = backward(
         out_part, back_mlp, normed, x_hat, g_all, hidden_grad, hidden,
-        q, k, v, mix_grad, mixture, lse, cos, sin, wa, labels, small,
+        q, k, v, mix_grad, mixture, lse, cos, sin, wa, labels, small, x, g, lines,
     )
     total = jnp.sum(sums[:, :3], 0)
     fc1_bias_sum = sums[:, 3, :cols].reshape(ways * cols)
     qkv_bias_sum = sums[:, 4, : 3 * head_cols].reshape(ways, 3, head_cols).transpose(1, 0, 2)
-    return (
-        branches,
-        normed_grad,
-        weight_grads,
-        (total[0], total[1], qkv_bias_sum.reshape(3, ways * head_cols), fc1_bias_sum, total[2]),
-    )
+    sums = (
+        total[0], total[1], qkv_bias_sum.reshape(3, ways * head_cols), fc1_bias_sum, total[2]
+    )
+    return output, grad_input, weight_grads, sums
 
 
 def per_device(
@@ -1311,27 +1366,18 @@
     qkv_shift = lax.dynamic_slice_in_dim(qkv_bias, me * head_cols, head_cols, 1).astype(F32)
     fc1_shift = lax.dynamic_slice_in_dim(fc1_bias, me * cols, cols, 0).astype(F32)
     fast = ways == 4 and lax.axis_size("dp") == 4 and rows % 128 == 0
-    fast = fast and head_cols == 256 and x.shape[1] == 8 * head_cols
+    fast = fast and head_cols == 256 and width == 8 * head_cols and 4 * cols == width * 2
     work = fast_work if fast else plain_work
-    branches, normed_grad, weight_grads, sums = work(
-        x, g, w_qkv, w_dense, w_fc1, w_fc2, positions[0], segment_ids[0], gain, shift, fc1_shift, qkv_shift
-    )
-
-    gf = g.astype(F32)
-    output = (x.astype(F32) + branches + out_bias.astype(F32)).astype(BF16)
-    own_hat, inv_std = layer_norm(x)
-    scaled = normed_grad * gain
-    grad_input = gf + inv_std * (
-        scaled
-        - jnp.mean(scaled, -1, keepdims=True)
-        - own_hat * jnp.mean(scaled * own_hat, -1, keepdims=True)
-    )
+    output, grad_input, weight_grads, sums = work(
+        x, g, w_qkv, w_dense, w_fc1, w_fc2, positions[0], segment_ids[0],
+        gain, shift, fc1_shift, qkv_shift, out_bias.astype(F32),
+    )
+    grad_qkv, grad_dense, grad_fc1, grad_fc2 = weight_grads
     gain_sum, shift_sum, qkv_bias_sum, fc1_bias_sum, out_bias_sum = sums
 
-    grad_qkv, grad_dense, grad_fc1, grad_fc2 = weight_grads
     return (
         output[None],
-        grad_input.astype(BF16)[None],
+        grad_input[None],
         gain_sum,
         shift_sum,
         grad_qkv,

time: 401 us -> 385 us (0.960)
  other arithmetic: 21.3 us -> 11.7 us
  Pallas kernels: 368 us -> 360 us
    reduce_sum x4 -> x0, other arithmetic: 6.91 us -> none  [the longest x1 2.41 us: per_device(): jnp.mean(scaled, -1, keepdims=True)]
    convert_element_type x3 -> x0, other arithmetic: 4.56 us -> none  [the longest x1 3.27 us: per_device(): grad_input.astype(BF16)[None]]
    pallas_call x1, Pallas kernels: 182 us -> 178 us  [forward(): pl.pallas_call(functools.partial(forward_body, ways), in_specs=[anywhere]...]
where the time goes in v6:
time: 385 us; the launch traced here: 381 us
  Pallas kernels  360 us (94%)
  other arithmetic  11.7 us (3%)
  local copies, waits for them, and re-layouts  8.16 us (2%)
    pallas_call x1, Pallas kernels, backward(): pl.pallas_call(functools.partial(backward_body, ways), in_specs=[anywhere...  182 us
    pallas_call x1, Pallas kernels, forward(): pl.pallas_call(functools.partial(forward_body, ways), in_specs=[anywhere]...  178 us

profile of v6, /device:TPU:0, one launch (start us, length us, event | category | flops | bytes accessed | tf_op | source)
XLA Modules:
  0.0 380.7 jit_solution(6572377468461501769)
XLA Ops:
  0.6 0.0 copy-start
  0.7 0.1 pad.20.clone
  0.8 0.6 copy-done
  1.4 0.7 dynamic_slice.6
  2.1 0.7 reshape.80
  2.7 0.7 reshape.82
  3.4 0.7 reshape.84
  4.1 1.4 add_add_fusion.ids
  5.5 0.7 concatenate.7.lines
  6.2 177.7 %shard_map.221 = (bf16[4,384,2048]{2,1,0:T(8,128)(2,1)}, bf16[4,384,2048]{2,1,0:T(8,128)(2,1)}, bf16[4,384,2048]{2,1,0:T(8,128)(2,1)}, bf16[4,384,1024]{2,1,0:T(...) custom-call(bf16[384,2048]{1,0:T(8,128)(2,1)} %bitcast.25, ...), custom_call_target="tpu_custom_call" | custom-call | tf_op jit(solution)/shard_map/pallas_call | solution.py:576
  184.0 182.1 %shard_map.222 = (bf16[384,2048]{1,0:T(8,128)(2,1)}, bf16[384,2048]{1,0:T(8,128)(2,1)}, bf16[128,4096]{1,0:T(8,128)(2,1)}, bf16[4096,128]{1,0:T(8,128)(2,1)}, bf...) custom-call(bf16[4,384,2048]{2,1,0:T(8,128)(2,1)} %get-tuple-element, ...), custom_call_target="tpu_custom_call" | custom-call | tf_op jit(solution)/shard_map/pallas_call | solution.py:1151
  366.1 1.0 slice.21
  367.1 0.6 copy.28
  367.7 1.5 slice.22
  369.3 1.0 slice_reduce_fusion
  370.2 0.6 fusion
  370.9 1.9 convert_element_type.22
  372.7 2.5 convert_element_type.12
  375.2 1.5 convert_element_type.23
  376.7 1.5 convert_element_type.24
  378.2 0.0 copy-done.3
  378.2 1.1 copy.31
  379.3 1.1 copy.32
  380.5 0.0 copy-done.1
  (15 shorter events, 0.1 us)
Async XLA Ops:
  0.6 0.7 copy-start
  366.1 9.1 %copy-start.5 = (bf16[128,4096]{1,0:T(8,128)(2,1)S(1)}, bf16[128,4096]{1,0:T(8,128)(2,1)}, u32[]{:S(2)}) copy-start(bf16[128,4096]{1,0:T(8,128)(2,1)} %get-tuple-element.59) | copy-start | bytes 3145732
  370.9 5.9 %copy-start.4 = (bf16[4096,128]{1,0:T(8,128)(2,1)S(1)}, bf16[4096,128]{1,0:T(8,128)(2,1)}, u32[]{:S(2)}) copy-start(bf16[4096,128]{1,0:T(8,128)(2,1)} %get-tuple-element.60) | copy-start | bytes 3145732
  375.2 3.0 copy-start.3
  376.7 2.6 copy-start.2
  376.7 3.8 copy-start.1
